TPU v7x, 32 devices: a whole 2x2x4 slice. The times are simulated.
32 devices in a mesh: ctx: 16 (over z, x, core), head: 2 (over y).
Axes of the slice: x: 2, y: 2, z: 4, core: 2. Of those that a mesh axis runs over, the one named last changes fastest.
Arguments:
- queries: bfloat16 [3072, 4096], P('ctx', 'head'), may hold values from -6 to 6
- key_rows: bfloat16 [3072, 4096], P('ctx', 'head'), may hold values from -6 to 6
- value_rows: bfloat16 [3072, 4096], P('ctx', 'head'), may hold values from -120 to 120
- gate_rows: bfloat16 [3072, 4096], P('ctx', 'head'), may hold values from -8 to 8
- cotangent: bfloat16 [3072, 4096], P('ctx', 'head'), may hold values from -6 to 6
Outputs:
- grad_queries: bfloat16 [3072, 4096], P('ctx', 'head')
- grad_keys: bfloat16 [3072, 4096], P('ctx', 'head')
- grad_values: bfloat16 [3072, 4096], P('ctx', 'head')
- grad_gates: bfloat16 [3072, 4096], P('ctx', 'head')
All inputs are finite; a program needn't handle non-finite values.
Results may differ from a plain program's by a relative error of at most 0.0065.
Values sent between devices are 32-bit elements; how exact they have to be, the bound alone decides.
No kernel may reach another device: no remote copies, remote signals or barrier semaphores. Data moves between devices by JAX's collectives and lax.ppermute only.
A program may use at most 64 MiB of HBM per device.

v0:
```python
import jax
import jax.numpy as jnp
from jax import lax
from jax.sharding import PartitionSpec as P

H = 32
DH = 128


EPSILON = 1e-06


def carried_in(part, axis, combine, identity, reverse):
    count = lax.axis_size(axis)
    place = lax.axis_index(axis)
    ahead = count - 1 - place if reverse else place
    gathered = lax.all_gather(part, axis)
    state = jnp.zeros_like(part) + jnp.asarray(identity, part.dtype)

    def one(step, state):
        source = count - 1 - step if reverse else step
        return combine(state, lax.dynamic_index_in_dim(gathered, source, 0, False))

    return lax.fori_loop(0, ahead, one, state)


def silu_slope(x):
    sig = jax.nn.sigmoid(x)
    return sig * (1.0 + x * (1.0 - sig))


def add_states(earlier, later):
    return earlier + later


def per_device(queries, key_rows, value_rows, gate_rows, cotangent):
    rows, width = queries.shape
    heads = width // DH
    full_width = H * DH
    q_float = queries.astype(jnp.float32)
    k_float = key_rows.astype(jnp.float32)
    lifted_q = jax.nn.silu(q_float).astype(jnp.bfloat16).reshape(rows, heads, DH)
    lifted_k = jax.nn.silu(k_float).astype(jnp.bfloat16).reshape(rows, heads, DH)
    values = value_rows.reshape(rows, heads, DH)
    causal = lax.broadcasted_iota(jnp.int32, (rows, rows), 0) >= lax.broadcasted_iota(
        jnp.int32, (rows, rows), 1
    )
    local_state = jnp.einsum("thd,the->hde", lifted_k, values, preferred_element_type=jnp.float32)
    prefix = carried_in(local_state, "ctx", add_states, jnp.zeros_like(local_state), False)
    scores = jnp.einsum("thd,shd->hts", lifted_q, lifted_k, preferred_element_type=jnp.float32)
    weights = jnp.where(causal[None], scores, 0.0).astype(jnp.bfloat16)
    prefix_low = prefix.astype(jnp.bfloat16)
    attended = jnp.einsum("hts,shd->thd", weights, values, preferred_element_type=jnp.float32)
    attended = attended + jnp.einsum(
        "thd,hde->the", lifted_q, prefix_low, preferred_element_type=jnp.float32
    )
    attended = attended.reshape(rows, width)
    sig = jax.nn.sigmoid(gate_rows.astype(jnp.float32))
    grad_out = cotangent.astype(jnp.float32)
    gated = grad_out * sig
    sumsq, raw_inner = lax.psum(
        (jnp.sum(attended * attended, axis=1), jnp.sum(gated * attended, axis=1)), "head"
    )
    rms = jnp.sqrt(sumsq / full_width + EPSILON)[:, None]
    normed = attended / rms
    inner = raw_inner[:, None] / rms
    grad_gates = (grad_out * normed * sig * (1.0 - sig)).astype(jnp.bfloat16)
    d_attn = (
        ((gated - normed * inner / full_width) / rms).astype(jnp.bfloat16).reshape(rows, heads, DH)
    )
    grad_local = jnp.einsum("thd,the->hde", lifted_q, d_attn, preferred_element_type=jnp.float32)
    suffix = carried_in(grad_local, "ctx", add_states, jnp.zeros_like(grad_local), True)
    suffix_low = suffix.astype(jnp.bfloat16)
    d_scores = jnp.einsum("the,she->hts", d_attn, values, preferred_element_type=jnp.float32)
    d_weights = jnp.where(causal[None], d_scores, 0.0).astype(jnp.bfloat16)
    grad_lq = jnp.einsum("hts,shd->thd", d_weights, lifted_k, preferred_element_type=jnp.float32)
    grad_lq = grad_lq + jnp.einsum(
        "the,hde->thd", d_attn, prefix_low, preferred_element_type=jnp.float32
    )
    grad_lk = jnp.einsum("hts,thd->shd", d_weights, lifted_q, preferred_element_type=jnp.float32)
    grad_lk = grad_lk + jnp.einsum(
        "she,hde->shd", values, suffix_low, preferred_element_type=jnp.float32
    )
    grad_v = jnp.einsum("hts,the->she", weights, d_attn, preferred_element_type=jnp.float32)
    grad_v = grad_v + jnp.einsum(
        "shd,hde->she", lifted_k, suffix_low, preferred_element_type=jnp.float32
    )
    grad_queries = (grad_lq.reshape(rows, width) * silu_slope(q_float)).astype(jnp.bfloat16)
    grad_keys = (grad_lk.reshape(rows, width) * silu_slope(k_float)).astype(jnp.bfloat16)
    grad_values = grad_v.reshape(rows, width).astype(jnp.bfloat16)
    return (grad_queries, grad_keys, grad_values, grad_gates)


def solution(mesh):
    in_specs = (
        P("ctx", "head"),
        P("ctx", "head"),
        P("ctx", "head"),
        P("ctx", "head"),
        P("ctx", "head"),
    )
    out_specs = (P("ctx", "head"), P("ctx", "head"), P("ctx", "head"), P("ctx", "head"))
    return jax.shard_map(
        per_device, mesh=mesh, in_specs=in_specs, out_specs=out_specs, check_vma=False
    )
```

profile of v0, /device:TPU:0, one launch (start us, length us, event | category | flops | bytes accessed | tf_op | source)
XLA Modules:
  0.0 336.7 jit_solution(15047605338116457564)
XLA Ops:
  7.2 0.0 copy-start
  7.2 0.0 all-gather.5.cloned.1.call-start
  7.2 2.3 fusion.21
  9.5 0.0 copy-start.1
  9.5 0.0 copy-start.5
  9.5 0.0 copy-done
  9.5 1.5 fusion.31
  11.0 0.0 all-gather.5.cloned.1.call-update
  11.0 0.0 all-gather.7.cloned.1.call-start
  11.1 0.0 copy-done.1
  11.1 0.0 copy-done.5
  11.1 0.6 select_convert_fusion.1
  11.7 0.0 copy-start.9
  11.7 1.2 copy-done.9
  12.9 1.7 fusion.33
  14.6 126.2 %all-gather.5.cloned.1.call-done = f32[256,128,128]{2,1,0:T(8,128)} async-done(((f32[16,128,128]{2,1,0:T(8,128)}), f32[256,128,128]{2,1,0:T(8,128)}) %all-gather.5.cloned.1.call-update) | async-done | bytes 16777232 | tf_op jit(solution)/shard_map/all_gather | solution.py:17
  140.8 0.1 broadcast.11.clone
  140.9 0.0 copy-start.13
  140.9 0.0 copy-start.14
  140.9 2.2 multiply_reduce_fusion
  143.2 0.0 copy-done.13
  143.2 0.0 copy-done.14
  143.2 0.6 fusion.19
  143.7 4.9 %all-reduce = (f32[192]{0:T(256)S(1)}, f32[192]{0:T(256)S(1)}) all-reduce(f32[192]{0:T(256)S(1)} %get-tuple-element.107, f32[192]{0:T(256)S(1)} %fusion.19), channel_id=1, replica_groups=mesh['ctx'=16,'head'=2] {'head'}, use_global_device_ids=true, to_apply=%region_3.4 | all-reduce | flops 384 | bytes 3072 | tf_op jit(solution)/shard_map/psum | solution.py:61
  148.7 3.4 fusion.2
  152.1 0.9 copy-done.3
  152.9 0.0 copy-done.6
  152.9 1.5 fusion.25
  154.4 0.0 all-gather.7.cloned.1.call-update
  154.4 0.0 copy-start.2
  154.5 1.8 select_convert_fusion
  156.3 0.0 copy-done.2
  156.3 0.0 copy-start.4
  156.3 0.6 fusion.35
  156.9 0.6 copy-done.4
  157.4 0.5 add_bitcast_fusion.1
  157.9 0.9 copy-done.10
  158.8 1.9 fusion.23
  160.7 1.9 fusion.41
  162.7 1.5 fusion.18
  164.1 136.8 %all-gather.7.cloned.1.call-done = f32[256,128,128]{2,1,0:T(8,128)} async-done(((f32[16,128,128]{2,1,0:T(8,128)}), f32[256,128,128]{2,1,0:T(8,128)}) %all-gather.7.cloned.1.call-update) | async-done | bytes 16777232 | tf_op jit(solution)/shard_map/all_gather | solution.py:17
  301.0 0.1 broadcast.11
  301.1 22.7 %while.23 = (s32[]{:T(128)}, f32[16,128,128]{2,1,0:T(8,128)S(1)}, s32[]{:T(128)}, f32[16,16,128,128]{3,2,1,0:T(8,128)}, s32[]{:T(128)}, /*index=5*/s32[]{:T(128)}, s32[]{:T(128)}, s32[]{:T(128)}) while((s32[]{:T(128)}, f32[16,128,128]{2,1,0:T(8,128)S(1)}, s32[]{:T(128)}, f32[16,16,128,128]{3,2,1,0:T(8,128)}, s32[]{:T(128)}, ...), condition=%wide.region_7.8_spmd, body=%wide.region_6.7_spmd.sunk | while | flops 262150 | bytes 3145871 | solution.py:24
  301.1 1.5 bitcast_add_fusion.6
  302.6 1.5 bitcast_add_fusion.6
  304.1 1.5 bitcast_add_fusion.6
  305.6 1.5 bitcast_add_fusion.6
  307.1 1.5 bitcast_add_fusion.6
  308.6 1.5 bitcast_add_fusion.6
  310.2 1.5 bitcast_add_fusion.6
  311.7 1.5 bitcast_add_fusion.6
  313.2 1.5 bitcast_add_fusion.6
  314.7 1.5 bitcast_add_fusion.6
  316.2 1.5 bitcast_add_fusion.6
  317.7 1.5 bitcast_add_fusion.6
  319.2 1.5 bitcast_add_fusion.6
  320.7 1.5 bitcast_add_fusion.6
  322.2 1.5 bitcast_add_fusion.6
  323.8 1.8 fusion.20
  325.5 1.1 copy.156
  326.6 0.6 copy-done.8
  327.2 0.5 add_bitcast_fusion
  327.7 0.6 copy-done.12
  328.4 1.5 fusion.10
  (12 shorter events, 0.1 us)
Async XLA Ops:
  7.2 2.3 copy-start
  7.2 133.6 %all-gather.5.cloned.1.call-start = ((), (), s32[]{:S(2)}) async-start(), calls=%async_computation | async-start | bytes 17825792 | tf_op jit(solution)/shard_map/all_gather | solution.py:17
  9.5 1.6 copy-start.1
  9.5 1.6 copy-start.5
  11.0 289.9 %all-gather.7.cloned.1.call-start = ((), (), s32[]{:S(2)}) async-start(), calls=%async_computation.1 | async-start | bytes 17825792 | tf_op jit(solution)/shard_map/all_gather | solution.py:17
  11.7 1.2 copy-start.9
  140.9 2.3 copy-start.13
  140.9 2.3 copy-start.14
  148.7 4.2 %copy-start.6 = (bf16[24,16,8,128]{3,2,1,0:T(8,128)(2,1)S(1)}, bf16[24,16,8,128]{3,2,1,0:T(8,128)(2,1)}, u32[]{:S(2)}) copy-start(bf16[24,16,8,128]{3,2,1,0:T(8,128)(2,1)} %copy-done.5) | copy-start | bytes 2359300
  152.1 0.9 copy-start.3
  154.4 1.8 copy-start.2
  156.3 1.1 copy-start.4
  157.4 1.4 copy-start.10
  158.8 1.9 copy-start.7
  160.7 1.9 copy-start.11
  325.5 1.7 copy-start.8
  327.2 1.1 copy-start.12
Sparse Core Ops, SparseCore 0:
  11.2 129.5 all-gather.4
  154.6 146.3 all-gather.6
where the time goes:
time: 338 us; the launch traced here: 337 us
  waiting for transfers between devices  263 us (78%)
  other arithmetic  31.5 us (9%)
  matrix products  16.5 us (5%)
  between operations  14.2 us (4%)
  local copies, waits for them, and re-layouts  6.08 us (2%)
  blocking collectives  4.93 us (1%)
    all_gather x2, waiting for transfers between devices, carried_in(): gathered = lax.all_gather(part, axis)  263 us
    add x15, other arithmetic, add_states(): return earlier + later  22.3 us
  transfers between devices with their start and end apart: 2, of which 2 were waited for; matrix products, arithmetic and copies ran while one was open for 3% of the time, Pallas kernels for 0%

commit v1 on v0

v1 whole, which is shorter than its diff:
```python
import functools

import jax
import jax.numpy as jnp
from jax import lax
from jax.experimental import pallas as pl
from jax.experimental.pallas import tpu as pltpu
from jax.sharding import PartitionSpec as P

H = 32
DH = 128
EPSILON = 1e-06
QUAD = 4
F32 = jnp.float32
BF16 = jnp.bfloat16
EXACT = lax.Precision.HIGHEST


def dot(a, b, ca, cb, precision=None):
    return lax.dot_general(
        a, b, (((ca,), (cb,)), ((), ())), precision=precision, preferred_element_type=F32
    )


def sigmoid(x):
    return 0.5 + 0.5 * jnp.tanh(0.5 * x)


def core_of():
    return lax.rem(lax.axis_index("ctx"), 2)


def chip_of():
    return lax.rem(lax.axis_index("ctx") // 2, QUAD)


def params():
    return pltpu.CompilerParams(vmem_limit_bytes=48 * 1024 * 1024)


class Plan:
    def __init__(self, rows, width):
        self.rows, self.width = rows, width
        self.heads = width // DH
        self.half = self.heads // 2
        self.group = 4 if self.half % 4 == 0 else self.half
        self.per_half = self.half // self.group
        self.steps = 2 * self.per_half
        self.state = self.half * DH
        self.part = self.state // QUAD

    def place(self, step):
        side = lax.rem(step // self.per_half + 1 + core_of(), 2)
        return side * self.per_half + lax.rem(step, self.per_half)

    def given(self):
        return pl.BlockSpec((self.rows, self.group * DH), lambda i: (0, self.place(i)))

    def kept(self):
        return pl.BlockSpec((self.rows, self.group * DH), lambda i: (0, i))

    def square(self):
        return pl.BlockSpec((self.group, self.rows, self.rows), lambda i: (i, 0, 0))

    def whole(self, *shape):
        return pl.BlockSpec(shape, lambda i: (0,) * len(shape))

    def low(self):
        return jax.ShapeDtypeStruct((self.rows, self.width), BF16)

    def full(self):
        return jax.ShapeDtypeStruct((self.rows, self.width), F32)

    def halves_spec(self):
        block = (self.group * DH, DH)
        last = self.per_half - 1
        return [
            pl.BlockSpec(block, lambda i: (jnp.minimum(i, last), 0)),
            pl.BlockSpec(block, lambda i: (jnp.maximum(i - last - 1, 0), 0)),
        ]

    def halves(self):
        return [jax.ShapeDtypeStruct((self.state, DH), F32)] * 2


def store_half(plan, send_ref, keep_ref, g, value):
    step = pl.program_id(0)

    @pl.when(step < plan.per_half)
    def _():
        send_ref[g * DH : (g + 1) * DH, :] = value

    @pl.when(step >= plan.per_half)
    def _():
        keep_ref[g * DH : (g + 1) * DH, :] = value


def head(g):
    return slice(g * DH, (g + 1) * DH)


def key_state_kernel(plan, k_ref, v_ref, send_ref, keep_ref):
    for g in range(plan.group):
        x = k_ref[:, head(g)].astype(F32)
        lifted = (x * sigmoid(x)).astype(BF16)
        store_half(plan, send_ref, keep_ref, g, dot(lifted, v_ref[:, head(g)], 0, 0))


def causal_mask(rows):
    return lax.broadcasted_iota(jnp.int32, (rows, rows), 0) >= lax.broadcasted_iota(
        jnp.int32, (rows, rows), 1
    )


def local_kernel(plan, q_ref, k_ref, v_ref, gate_ref, cot_ref, lq_ref, w_ref, att_ref, gated_ref):
    causal = causal_mask(plan.rows)
    for g in range(plan.group):
        q = q_ref[:, head(g)].astype(F32)
        k = k_ref[:, head(g)].astype(F32)
        lq = (q * sigmoid(q)).astype(BF16)
        lk = (k * sigmoid(k)).astype(BF16)
        lq_ref[:, head(g)] = lq
        weights = jnp.where(causal, dot(lq, lk, 1, 1), 0.0).astype(BF16)
        w_ref[g] = weights
        att_ref[:, head(g)] = dot(weights, v_ref[:, head(g)], 1, 0)
        gated_ref[:, head(g)] = cot_ref[:, head(g)].astype(F32) * sigmoid(
            gate_ref[:, head(g)].astype(F32)
        )


def place_state(plan, reverse, own, far, near_add, far_add, state_ref):
    add = core_of() == (0 if reverse else 1)
    chip = chip_of()
    for k in range(QUAD):
        at = pl.multiple_of((chip ^ k) * plan.part, plan.part)
        here = pl.ds(at, plan.part)
        state_ref[pl.ds(pl.multiple_of(plan.state + at, plan.part), plan.part), :] = (
            own[k][...] + jnp.where(add, near_add[here, :], 0.0)
        ).astype(BF16)
        state_ref[here, :] = (far[k][...] + jnp.where(add, far_add[here, :], 0.0)).astype(BF16)


def attend_kernel(plan, *refs):
    own, far, (near_add, far_add) = refs[:4], refs[4:8], refs[8:10]
    lq_ref, local_ref, gated_ref, state_ref, att_ref, sums_ref, square, inner = refs[10:]
    step = pl.program_id(0)

    @pl.when(step == 0)
    def _():
        place_state(plan, False, own, far, near_add, far_add, state_ref)
        square[...] = jnp.zeros_like(square)
        inner[...] = jnp.zeros_like(inner)

    for g in range(plan.group):
        at = pl.multiple_of((step * plan.group + g) * DH, DH)
        att = local_ref[:, head(g)] + dot(lq_ref[:, head(g)], state_ref[pl.ds(at, DH), :], 1, 0)
        att_ref[:, head(g)] = att
        square[...] += att * att
        inner[...] += gated_ref[:, head(g)] * att

    @pl.when(step == plan.steps - 1)
    def _():
        line = lax.broadcasted_iota(jnp.int32, (8, DH), 0)
        sums_ref[...] = dot(
            jnp.where(line == 0, 1.0, 0.0), square[...], 1, 1, EXACT
        ) + dot(jnp.where(line == 1, 1.0, 0.0), inner[...], 1, 1, EXACT)


def grad_kernel(plan, mine_ref, theirs_ref, att_ref, gated_ref, lq_ref, d_ref, send_ref, keep_ref, inv_ref, coef):
    step = pl.program_id(0)

    @pl.when(step == 0)
    def _():
        total = mine_ref[...] + theirs_ref[...]
        line = lax.broadcasted_iota(jnp.int32, (8, DH), 0)
        sumsq = dot(total, jnp.where(line == 0, 1.0, 0.0), 0, 0, EXACT)
        raw = dot(total, jnp.where(line == 1, 1.0, 0.0), 0, 0, EXACT)
        inv = 1.0 / jnp.sqrt(sumsq * (1.0 / (H * DH)) + EPSILON)
        inv_ref[...] = inv
        coef[...] = raw * inv * (1.0 / (H * DH)) * inv * inv

    for g in range(plan.group):
        d = (gated_ref[:, head(g)] * inv_ref[...] - att_ref[:, head(g)] * coef[...]).astype(BF16)
        d_ref[:, head(g)] = d
        store_half(plan, send_ref, keep_ref, g, dot(lq_ref[:, head(g)], d, 0, 0))


def inside_kernel(plan, state_ref, inv_ref, w_ref, d_ref, lq_ref, att_ref, gated_ref, q_ref, k_ref, v_ref, gate_ref, gq_ref, gg_ref, pk_ref, pv_ref):
    step = pl.program_id(0)
    causal = causal_mask(plan.rows)
    for g in range(plan.group):
        at = pl.multiple_of((step * plan.group + g) * DH, DH)
        d = d_ref[:, head(g)]
        k = k_ref[:, head(g)].astype(F32)
        lk = (k * sigmoid(k)).astype(BF16)
        dw = jnp.where(causal, dot(d, v_ref[:, head(g)], 1, 1), 0.0).astype(BF16)
        glq = dot(dw, lk, 1, 0) + dot(d, state_ref[pl.ds(at, DH), :], 1, 1)
        q = q_ref[:, head(g)].astype(F32)
        sig = sigmoid(q)
        gq_ref[:, head(g)] = (glq * (sig * (1.0 + q * (1.0 - sig)))).astype(BF16)
        pk_ref[:, head(g)] = dot(dw, lq_ref[:, head(g)], 0, 0)
        pv_ref[:, head(g)] = dot(w_ref[g], d, 0, 0)
        gate = sigmoid(gate_ref[:, head(g)].astype(F32))
        gg_ref[:, head(g)] = (
            gated_ref[:, head(g)] * (att_ref[:, head(g)] * inv_ref[...]) * (1.0 - gate)
        ).astype(BF16)


def finish_kernel(plan, *refs):
    own, far, (near_add, far_add) = refs[:4], refs[4:8], refs[8:10]
    k_ref, v_ref, pk_ref, pv_ref, gk_ref, gv_ref, state_ref = refs[10:]
    step = pl.program_id(0)

    @pl.when(step == 0)
    def _():
        place_state(plan, True, own, far, near_add, far_add, state_ref)

    for g in range(plan.group):
        at = pl.multiple_of((step * plan.group + g) * DH, DH)
        state = state_ref[pl.ds(at, DH), :]
        k = k_ref[:, head(g)].astype(F32)
        sig = sigmoid(k)
        lk = (k * sig).astype(BF16)
        gv_ref[:, head(g)] = (pv_ref[:, head(g)] + dot(lk, state, 1, 0)).astype(BF16)
        glk = pk_ref[:, head(g)] + dot(v_ref[:, head(g)], state, 1, 1)
        gk_ref[:, head(g)] = (glk * (sig * (1.0 + k * (1.0 - sig)))).astype(BF16)


def split_kernel(plan, keep_ref, got_ref, *outs):
    chip = chip_of()
    for k in range(QUAD):
        here = pl.ds(pl.multiple_of((chip ^ k) * plan.part, plan.part), plan.part)
        outs[k][...] = keep_ref[here, :] + got_ref[here, :]


def before_kernel(reverse, span, *refs):
    parts, got_ref, base, outs = refs[:4], refs[4], refs[5:-4], refs[-4:]
    chip = chip_of()
    far = lax.rem(lax.axis_index("ctx") // span, 2) == (0 if reverse else 1)
    start = jnp.where(far, got_ref[...], 0.0)
    for more in base:
        start = start + more[...]
    for k in range(QUAD):
        total = start
        for m in range(QUAD):
            first = (chip ^ m) > (chip ^ k) if reverse else (chip ^ m) < (chip ^ k)
            total = total + jnp.where(first, parts[m][...], 0.0)
        outs[k][...] = total


def swap(x, distance):
    count = lax.axis_size("ctx")
    return lax.ppermute(x, "ctx", [(i, i ^ distance) for i in range(count)])


def carried_in(plan, send, keep, reverse):
    count = lax.axis_size("ctx")
    near_add = swap(send, 1)
    far_add = swap(keep, 1)
    piece = jax.ShapeDtypeStruct((plan.part, DH), F32)
    mine = pl.pallas_call(
        functools.partial(split_kernel, plan), out_shape=[piece] * QUAD, compiler_params=params()
    )(keep, near_add)
    parts = [mine[0]] + [swap(mine[k], 2 * k) for k in range(1, QUAD)]
    total = (parts[0] + parts[1]) + (parts[2] + parts[3])
    base = []
    span = 2 * QUAD
    while True:
        got = swap(total, span)
        if 2 * span >= count:
            break
        far = lax.rem(lax.axis_index("ctx") // span, 2) == (0 if reverse else 1)
        term = jnp.where(far, got, 0.0)
        base = [base[0] + term] if base else [term]
        total = total + got
        span *= 2
    outs = pl.pallas_call(
        functools.partial(before_kernel, reverse, span),
        out_shape=[piece] * QUAD,
        compiler_params=params(),
    )(*parts, got, *base)
    own = [outs[0]] + [swap(outs[k], 2 * k) for k in range(1, QUAD)]
    far = [swap(x, 1) for x in own]
    return own + far + [near_add, far_add]


def head_total(sums):
    count = lax.axis_size("head")
    if count == 2:
        return sums, lax.ppermute(sums, "head", [(0, 1), (1, 0)])
    return lax.psum(sums, "head"), jnp.zeros_like(sums)


def per_device(queries, key_rows, value_rows, gate_rows, cotangent):
    rows, width = queries.shape
    plan = Plan(rows, width)
    given, kept = plan.given(), plan.kept()
    pieces = [plan.whole(plan.part, DH)] * 8 + [plan.whole(plan.state, DH)] * 2
    state_spec = plan.whole(2 * plan.state, DH)
    state_shape = jax.ShapeDtypeStruct((2 * plan.state, DH), BF16)
    sums_spec = plan.whole(8, rows)
    wide_spec = plan.whole(rows, DH)

    def call(kernel, in_specs, out_specs, out_shape, scratch=()):
        return pl.pallas_call(
            functools.partial(kernel, plan),
            grid=(plan.steps,),
            in_specs=in_specs,
            out_specs=out_specs,
            out_shape=out_shape,
            scratch_shapes=list(scratch),
            compiler_params=params(),
        )

    send, keep = call(key_state_kernel, [given] * 2, plan.halves_spec(), plan.halves())(
        key_rows, value_rows
    )
    lq, weights, local, gated = call(
        local_kernel,
        [given] * 5,
        [kept, plan.square(), kept, kept],
        [
            plan.low(),
            jax.ShapeDtypeStruct((plan.heads, rows, rows), BF16),
            plan.full(),
            plan.full(),
        ],
    )(queries, key_rows, value_rows, gate_rows, cotangent)
    arrived = carried_in(plan, send, keep, False)
    state, attended, sums = call(
        attend_kernel,
        pieces + [kept] * 3,
        [state_spec, kept, sums_spec],
        [state_shape, plan.full(), jax.ShapeDtypeStruct((8, rows), F32)],
        [pltpu.VMEM((rows, DH), F32)] * 2,
    )(*arrived, lq, local, gated)
    mine, theirs = head_total(sums)
    d_attn, send, keep, inverse = call(
        grad_kernel,
        [sums_spec] * 2 + [kept] * 3,
        [kept] + plan.halves_spec() + [wide_spec],
        [plan.low()] + plan.halves() + [jax.ShapeDtypeStruct((rows, DH), F32)],
        [pltpu.VMEM((rows, DH), F32)],
    )(mine, theirs, attended, gated, lq)
    grad_queries, grad_gates, part_k, part_v = call(
        inside_kernel,
        [state_spec, wide_spec, plan.square()] + [kept] * 4 + [given] * 4,
        [given] * 2 + [kept] * 2,
        [plan.low()] * 2 + [plan.full()] * 2,
    )(
        state, inverse, weights, d_attn, lq, attended, gated,
        queries, key_rows, value_rows, gate_rows,
    )
    arrived = carried_in(plan, send, keep, True)
    grad_keys, grad_values = call(
        finish_kernel,
        pieces + [given] * 2 + [kept] * 2,
        [given] * 2,
        [plan.low()] * 2,
        [pltpu.VMEM((2 * plan.state, DH), BF16)],
    )(*arrived, key_rows, value_rows, part_k, part_v)
    return (grad_queries, grad_keys, grad_values, grad_gates)


def solution(mesh):
    spec = P("ctx", "head")
    return jax.shard_map(
        per_device, mesh=mesh, in_specs=(spec,) * 5, out_specs=(spec,) * 4, check_vma=False
    )
```

time: 338 us -> 97 us (0.29)
  waiting for transfers between devices: 263 us -> 38.9 us
  other arithmetic: 31.5 us -> 0.06 us
  Pallas kernels: 0 us -> 29.6 us
  starting transfers between devices: 0.08 us -> 23.5 us
  matrix products: 16.5 us -> 0 us
  between operations: 14.2 us -> 0.85 us
  blocking collectives: 4.93 us -> 0 us
    all_gather x2 -> x0, waiting for transfers between devices: 263 us -> none  [carried_in(): gathered = lax.all_gather(part, axis)]
    ppermute x0 -> x27, waiting for transfers between devices: none -> 38.9 us  [the longest x26 36.9 us: swap(): return lax.ppermute(x, 'ctx', [(i, i ^ distance) for i in range(count)])]
    pallas_call x0 -> x10, Pallas kernels: none -> 29.6 us  [the longest x1 8.39 us: per_device(): call(inside_kernel, [state_spec, wide_spec, plan.square()] + [kept] * 4 +...]
    ppermute x0 -> x27, starting transfers between devices: none -> 23.5 us  [the longest x26 21.8 us: swap(): return lax.ppermute(x, 'ctx', [(i, i ^ distance) for i in range(count)])]
    add x15 -> x2, other arithmetic: 22.3 us -> 0.06 us  [carried_in(): total = parts[0] + parts[1] + (parts[2] + parts[3])]
    dot_general x12 -> x0, matrix products: 16.5 us -> none  [the longest x1 2.23 us: per_device(): jnp.einsum('thd,hde->the', lifted_q, prefix_low, preferred_element_type=j...]
    convert_element_type x3 -> x0, other arithmetic: 6.32 us -> none  [the longest x1 3.36 us: per_device(): grad_gates = (grad_out * normed * sig * (1.0 - sig)).astype(jnp.bfloat16)]
    psum x1 -> x0, blocking collectives: 4.93 us -> none  [per_device(): lax.psum((jnp.sum(attended * attended, axis=1), jnp.sum(gated * attended,...]
  transfers between devices with their start and end apart: 2 -> 27, of which waited for: 2 -> 17; matrix products, arithmetic and copies ran while one was open for 3% -> 0% of each run, Pallas kernels for 0% -> 14%
where the time goes in v1:
time: 97 us; the launch traced here: 96.6 us
  waiting for transfers between devices  38.9 us (40%)
  Pallas kernels  29.6 us (31%)
  starting transfers between devices  23.5 us (24%)
  local copies, waits for them, and re-layouts  3.7 us (4%)
    ppermute x26, waiting for transfers between devices, swap(): return lax.ppermute(x, 'ctx', [(i, i ^ distance) for i in range(count)])  36.9 us
    ppermute x26, starting transfers between devices, swap(): return lax.ppermute(x, 'ctx', [(i, i ^ distance) for i in range(count)])  21.8 us
    pallas_call x1, Pallas kernels, per_device(): call(inside_kernel, [state_spec, wide_spec, plan.square()] + [kept] * 4 +...  8.39 us
    pallas_call x1, Pallas kernels, per_device(): call(local_kernel, [given] * 5, [kept, plan.square(), kept, kept], [plan....  4.71 us
    pallas_call x1, Pallas kernels, per_device(): call(finish_kernel, pieces + [given] * 2 + [kept] * 2, [given] * 2, [plan...  4.3 us
    pallas_call x1, Pallas kernels, per_device(): call(grad_kernel, [sums_spec] * 2 + [kept] * 3, [kept] + plan.halves_spec...  4.11 us
    pallas_call x1, Pallas kernels, per_device(): call(key_state_kernel, [given] * 2, plan.halves_spec(), plan.halves())  3.86 us
    pallas_call x1, Pallas kernels, per_device(): call(attend_kernel, pieces + [kept] * 3, [state_spec, kept, sums_spec], [...  3.85 us
  transfers between devices with their start and end apart: 27, of which 17 were waited for; matrix products, arithmetic and copies ran while one was open for 0% of the time, Pallas kernels for 14%

profile of v1, /device:TPU:0, one launch (start us, length us, event | category | flops | bytes accessed | tf_op | source)
XLA Modules:
  0.0 96.6 jit_solution(11931676725481590191)
XLA Ops:
  0.6 0.0 copy-start.1
  0.6 1.1 %copy-done.1 = bf16[192,2048]{1,0:T(8,128)(2,1)S(1)} copy-done((bf16[192,2048]{1,0:T(8,128)(2,1)S(1)}, bf16[192,2048]{1,0:T(8,128)(2,1)}, u32[]{:S(2)}) %copy-start.1) | copy-done | bytes 786456
  1.8 1.1 %copy-done.3 = bf16[192,2048]{1,0:T(8,128)(2,1)S(1)} copy-done((bf16[192,2048]{1,0:T(8,128)(2,1)S(1)}, bf16[192,2048]{1,0:T(8,128)(2,1)}, u32[]{:S(2)}) %copy-start.3) | copy-done | bytes 786456
  2.9 3.9 %shard_map.84 = (f32[1024,128]{1,0:T(8,128)S(1)}, f32[1024,128]{1,0:T(8,128)S(1)}) custom-call(bf16[192,2048]{1,0:T(8,128)(2,1)S(1)} %copy-done.1, bf16[192,2048]{1,0:T(8,128)(2,1)S(1)} %copy-done.3), custom_call_target="tpu_custom_call" | custom-call | tf_op jit(solution)/shard_map/pallas_call | solution.py:315
  6.8 0.0 copy-start.2
  6.8 0.0 copy-start.4
  6.8 0.0 copy-start.6
  6.8 0.5 collective-permute-start
  7.3 1.5 %collective-permute-done.got_ref.refs_8_ = f32[1024,128]{1,0:T(8,128)S(1)} collective-permute-done((f32[1024,128]{1,0:T(8,128)S(1)}, f32[1024,128]{1,0:T(8,128)S(1)}, u32[]{:S(2)}, u32[]{:S(2)}) %collective-permute-start) | collective-permute-done | bytes 524320 | tf_op jit(solution)/shard_map/ppermute | solution.py:253
  8.9 0.1 shard_map.85
  8.9 2.9 %collective-permute-start.1 = (f32[256,128]{1,0:T(8,128)S(1)}, f32[256,128]{1,0:T(8,128)S(1)}, u32[]{:S(2)}, u32[]{:S(2)}) collective-permute-start(f32[256,128]{1,0:T(8,128)S(1)} %get-tuple-element.42), channel_id=1, source_target_pairs={{0,4},{2,6},{4,0},{6,2},{8,12},{10,14},{12,8},{14,10},{16,20},{18,... | collective-permute-start | bytes 393224 | tf_op jit(solution)/shard_map/ppermute | solution.py:253
  11.9 1.6 %collective-permute-start.2 = (f32[256,128]{1,0:T(8,128)S(1)}, f32[256,128]{1,0:T(8,128)S(1)}, u32[]{:S(2)}, u32[]{:S(2)}) collective-permute-start(f32[256,128]{1,0:T(8,128)S(1)} %get-tuple-element.43), channel_id=1, source_target_pairs={{0,8},{2,10},{4,12},{6,14},{8,0},{10,2},{12,4},{14,6},{16,24},{18,... | collective-permute-start | bytes 393224 | tf_op jit(solution)/shard_map/ppermute | solution.py:253
  13.4 0.0 collective-permute-start.3
  13.4 0.0 collective-permute-start.12
  13.4 2.2 %collective-permute-done.1.refs_1_ = f32[256,128]{1,0:T(8,128)S(1)} collective-permute-done((f32[256,128]{1,0:T(8,128)S(1)}, f32[256,128]{1,0:T(8,128)S(1)}, u32[]{:S(2)}, u32[]{:S(2)}) %collective-permute-start.1) | collective-permute-done | bytes 131104 | tf_op jit(solution)/shard_map/ppermute | solution.py:253
  15.7 2.6 %collective-permute-done.2.refs_2_ = f32[256,128]{1,0:T(8,128)S(1)} collective-permute-done((f32[256,128]{1,0:T(8,128)S(1)}, f32[256,128]{1,0:T(8,128)S(1)}, u32[]{:S(2)}, u32[]{:S(2)}) %collective-permute-start.2) | collective-permute-done | bytes 131104 | tf_op jit(solution)/shard_map/ppermute | solution.py:253
  18.2 1.5 %collective-permute-done.3.refs_3_ = f32[256,128]{1,0:T(8,128)S(1)} collective-permute-done((f32[256,128]{1,0:T(8,128)S(1)}, f32[256,128]{1,0:T(8,128)S(1)}, u32[]{:S(2)}, u32[]{:S(2)}) %collective-permute-start.3) | collective-permute-done | bytes 131104 | tf_op jit(solution)/shard_map/ppermute | solution.py:253
  19.8 2.8 %collective-permute-start.4 = (f32[256,128]{1,0:T(8,128)S(1)}, f32[256,128]{1,0:T(8,128)S(1)}, u32[]{:S(2)}, u32[]{:S(2)}) collective-permute-start(f32[256,128]{1,0:T(8,128)S(1)} %add_add_fusion.1), channel_id=1, source_target_pairs={{0,16},{2,18},{4,20},{6,22},{8,24},{10,26},{12,28},{14,30},{16,0},... | collective-permute-start | bytes 393224 | tf_op jit(solution)/shard_map/ppermute | solution.py:253
  22.6 5.7 %collective-permute-done.4.refs_4_ = f32[256,128]{1,0:T(8,128)S(1)} collective-permute-done((f32[256,128]{1,0:T(8,128)S(1)}, f32[256,128]{1,0:T(8,128)S(1)}, u32[]{:S(2)}, u32[]{:S(2)}) %collective-permute-start.4) | collective-permute-done | bytes 131104 | tf_op jit(solution)/shard_map/ppermute | solution.py:253
  28.3 0.1 shard_map.86
  28.4 1.3 %collective-permute-start.5 = (f32[256,128]{1,0:T(8,128)S(1)}, f32[256,128]{1,0:T(8,128)S(1)}, u32[]{:S(2)}, u32[]{:S(2)}) collective-permute-start(f32[256,128]{1,0:T(8,128)S(1)} %get-tuple-element.46), channel_id=1, source_target_pairs={{0,4},{2,6},{4,0},{6,2},{8,12},{10,14},{12,8},{14,10},{16,20},{18,... | collective-permute-start | bytes 393224 | tf_op jit(solution)/shard_map/ppermute | solution.py:253
  29.8 0.7 collective-permute-start.6
  30.4 1.5 %collective-permute-start.7 = (f32[256,128]{1,0:T(8,128)S(1)}, f32[256,128]{1,0:T(8,128)S(1)}, u32[]{:S(2)}, u32[]{:S(2)}) collective-permute-start(f32[256,128]{1,0:T(8,128)S(1)} %get-tuple-element.48), channel_id=1, source_target_pairs={{0,12},{2,14},{4,8},{6,10},{8,4},{10,6},{12,0},{14,2},{16,28},{18,... | collective-permute-start | bytes 393224 | tf_op jit(solution)/shard_map/ppermute | solution.py:253
  32.0 0.0 collective-permute-start.8
  32.0 2.9 %collective-permute-done.5.refs_1_ = f32[256,128]{1,0:T(8,128)S(1)} collective-permute-done((f32[256,128]{1,0:T(8,128)S(1)}, f32[256,128]{1,0:T(8,128)S(1)}, u32[]{:S(2)}, u32[]{:S(2)}) %collective-permute-start.5) | collective-permute-done | bytes 131104 | tf_op jit(solution)/shard_map/ppermute | solution.py:253
  34.9 0.1 collective-permute-done.6.refs_2_
  35.0 0.4 collective-permute-start.10
  35.4 1.7 %collective-permute-done.7.refs_3_ = f32[256,128]{1,0:T(8,128)S(1)} collective-permute-done((f32[256,128]{1,0:T(8,128)S(1)}, f32[256,128]{1,0:T(8,128)S(1)}, u32[]{:S(2)}, u32[]{:S(2)}) %collective-permute-start.7) | collective-permute-done | bytes 131104 | tf_op jit(solution)/shard_map/ppermute | solution.py:253
  37.0 0.0 collective-permute-start.11
  37.1 4.7 %shard_map.87 = (bf16[192,2048]{1,0:T(8,128)(2,1)S(1)}, bf16[16,192,192]{2,1,0:T(8,128)(2,1)}, f32[192,2048]{1,0:T(8,128)}, f32[192,2048]{1,0:T(8,128)}) custom-call(bf16[192,2048]{1,0:T(8,128)(2,1)S(1)} %copy-done.6, bf16[192,2048]{1,0:T(8,128)(2,1)S(1)} %copy-done.2, bf16[192,2048]{1,0:T(8,128)(2,1)S(1)} %copy-done.4, bf16[192,2048]{1,0:T(8,128)(2,1)S(1)} %copy-done.7, ...), custom_call_target="tpu_custom_call" | custom-call | tf_op jit(solution)/shard_map/pallas_call | solution.py:318
  41.8 0.0 collective-permute-done.10.refs_6_
  41.8 0.0 collective-permute-done.11.refs_7_
  41.8 3.8 %shard_map.88 = (bf16[2048,128]{1,0:T(8,128)(2,1)S(1)}, f32[192,2048]{1,0:T(8,128)S(1)}, f32[8,192]{1,0:T(8,128)S(1)}) custom-call(f32[256,128]{1,0:T(8,128)S(1)} %get-tuple-element.45.refs_0_, f32[256,128]{1,0:T(8,128)S(1)} %collective-permute-done.5.refs_1_, f32[256,128]{1,0:T(8,128)S(1)} %collective-permute-done.6.refs_2_, ...), custom_call_target="tpu_custom_call" | custom-call | tf_op jit(solution)/shard_map/pallas_call | solution.py:330
  45.7 1.7 %collective-permute-start.13 = (f32[8,192]{1,0:T(8,128)S(1)}, f32[8,192]{1,0:T(8,128)S(1)}, u32[]{:S(2)}, u32[]{:S(2)}) collective-permute-start(f32[8,192]{1,0:T(8,128)S(1)} %get-tuple-element.53.mine_ref), channel_id=1, source_target_pairs={{0,1},{1,0},{2,3},{3,2},{4,5},{5,4},{6,7},{7,6},{8,9},{9,8},{10,11... | collective-permute-start | bytes 18440 | tf_op jit(solution)/shard_map/ppermute | solution.py:290
  47.4 2.0 %collective-permute-done.13.theirs_ref = f32[8,192]{1,0:T(8,128)S(1)} collective-permute-done((f32[8,192]{1,0:T(8,128)S(1)}, f32[8,192]{1,0:T(8,128)S(1)}, u32[]{:S(2)}, u32[]{:S(2)}) %collective-permute-start.13) | collective-permute-done | bytes 6176 | tf_op jit(solution)/shard_map/ppermute | solution.py:290
  49.4 4.1 %shard_map.89 = (bf16[192,2048]{1,0:T(8,128)(2,1)S(1)}, f32[1024,128]{1,0:T(8,128)S(1)}, f32[1024,128]{1,0:T(8,128)S(1)}, f32[192,128]{1,0:T(8,128)S(1)}) custom-call(f32[8,192]{1,0:T(8,128)S(1)} %get-tuple-element.53.mine_ref, f32[8,192]{1,0:T(8,128)S(1)} %collective-permute-done.13.theirs_ref, f32[192,2048]{1,0:T(8,128)S(1)} %get-tuple-element.54.att_ref, ...), custom_call_target="tpu_custom_call" | custom-call | tf_op jit(solution)/shard_map/pallas_call | solution.py:338
  53.5 0.1 collective-permute-start.14
  53.6 1.9 %collective-permute-done.14.got_ref.refs_8_ = f32[1024,128]{1,0:T(8,128)S(1)} collective-permute-done((f32[1024,128]{1,0:T(8,128)S(1)}, f32[1024,128]{1,0:T(8,128)S(1)}, u32[]{:S(2)}, u32[]{:S(2)}) %collective-permute-start.14) | collective-permute-done | bytes 524320 | tf_op jit(solution)/shard_map/ppermute | solution.py:253
  55.5 0.1 shard_map.91
  55.6 0.9 collective-permute-start.15
  56.5 1.3 %collective-permute-start.16 = (f32[256,128]{1,0:T(8,128)S(1)}, f32[256,128]{1,0:T(8,128)S(1)}, u32[]{:S(2)}, u32[]{:S(2)}) collective-permute-start(f32[256,128]{1,0:T(8,128)S(1)} %get-tuple-element.63), channel_id=1, source_target_pairs={{0,8},{2,10},{4,12},{6,14},{8,0},{10,2},{12,4},{14,6},{16,24},{18,... | collective-permute-start | bytes 393224 | tf_op jit(solution)/shard_map/ppermute | solution.py:253
  57.8 1.3 %collective-permute-start.17 = (f32[256,128]{1,0:T(8,128)S(1)}, f32[256,128]{1,0:T(8,128)S(1)}, u32[]{:S(2)}, u32[]{:S(2)}) collective-permute-start(f32[256,128]{1,0:T(8,128)S(1)} %get-tuple-element.64), channel_id=1, source_target_pairs={{0,12},{2,14},{4,8},{6,10},{8,4},{10,6},{12,0},{14,2},{16,28},{18,... | collective-permute-start | bytes 393224 | tf_op jit(solution)/shard_map/ppermute | solution.py:253
  59.1 0.0 collective-permute-start.26
  59.1 2.0 %collective-permute-done.15.refs_1_ = f32[256,128]{1,0:T(8,128)S(1)} collective-permute-done((f32[256,128]{1,0:T(8,128)S(1)}, f32[256,128]{1,0:T(8,128)S(1)}, u32[]{:S(2)}, u32[]{:S(2)}) %collective-permute-start.15) | collective-permute-done | bytes 131104 | tf_op jit(solution)/shard_map/ppermute | solution.py:253
  61.2 1.7 %collective-permute-done.16.refs_2_ = f32[256,128]{1,0:T(8,128)S(1)} collective-permute-done((f32[256,128]{1,0:T(8,128)S(1)}, f32[256,128]{1,0:T(8,128)S(1)}, u32[]{:S(2)}, u32[]{:S(2)}) %collective-permute-start.16) | collective-permute-done | bytes 131104 | tf_op jit(solution)/shard_map/ppermute | solution.py:253
  62.9 2.3 %collective-permute-done.17.refs_3_ = f32[256,128]{1,0:T(8,128)S(1)} collective-permute-done((f32[256,128]{1,0:T(8,128)S(1)}, f32[256,128]{1,0:T(8,128)S(1)}, u32[]{:S(2)}, u32[]{:S(2)}) %collective-permute-start.17) | collective-permute-done | bytes 131104 | tf_op jit(solution)/shard_map/ppermute | solution.py:253
  65.2 2.7 %collective-permute-start.18 = (f32[256,128]{1,0:T(8,128)S(1)}, f32[256,128]{1,0:T(8,128)S(1)}, u32[]{:S(2)}, u32[]{:S(2)}) collective-permute-start(f32[256,128]{1,0:T(8,128)S(1)} %add_add_fusion), channel_id=1, source_target_pairs={{0,16},{2,18},{4,20},{6,22},{8,24},{10,26},{12,28},{14,30},{16,0},... | collective-permute-start | bytes 393224 | tf_op jit(solution)/shard_map/ppermute | solution.py:253
  67.9 5.8 %collective-permute-done.18.refs_4_ = f32[256,128]{1,0:T(8,128)S(1)} collective-permute-done((f32[256,128]{1,0:T(8,128)S(1)}, f32[256,128]{1,0:T(8,128)S(1)}, u32[]{:S(2)}, u32[]{:S(2)}) %collective-permute-start.18) | collective-permute-done | bytes 131104 | tf_op jit(solution)/shard_map/ppermute | solution.py:253
  73.7 0.1 shard_map.92
  73.9 1.1 %collective-permute-start.19 = (f32[256,128]{1,0:T(8,128)S(1)}, f32[256,128]{1,0:T(8,128)S(1)}, u32[]{:S(2)}, u32[]{:S(2)}) collective-permute-start(f32[256,128]{1,0:T(8,128)S(1)} %get-tuple-element.66), channel_id=1, source_target_pairs={{0,4},{2,6},{4,0},{6,2},{8,12},{10,14},{12,8},{14,10},{16,20},{18,... | collective-permute-start | bytes 393224 | tf_op jit(solution)/shard_map/ppermute | solution.py:253
  74.9 0.7 collective-permute-start.20
  75.6 1.8 %collective-permute-start.21 = (f32[256,128]{1,0:T(8,128)S(1)}, f32[256,128]{1,0:T(8,128)S(1)}, u32[]{:S(2)}, u32[]{:S(2)}) collective-permute-start(f32[256,128]{1,0:T(8,128)S(1)} %get-tuple-element.68), channel_id=1, source_target_pairs={{0,12},{2,14},{4,8},{6,10},{8,4},{10,6},{12,0},{14,2},{16,28},{18,... | collective-permute-start | bytes 393224 | tf_op jit(solution)/shard_map/ppermute | solution.py:253
  77.4 0.0 collective-permute-start.22
  77.4 2.9 %collective-permute-done.19.refs_1_ = f32[256,128]{1,0:T(8,128)S(1)} collective-permute-done((f32[256,128]{1,0:T(8,128)S(1)}, f32[256,128]{1,0:T(8,128)S(1)}, u32[]{:S(2)}, u32[]{:S(2)}) %collective-permute-start.19) | collective-permute-done | bytes 131104 | tf_op jit(solution)/shard_map/ppermute | solution.py:253
  80.3 0.0 collective-permute-start.23
  80.3 0.4 collective-permute-done.20.refs_2_
  80.7 0.2 collective-permute-start.24
  80.8 1.6 %collective-permute-done.21.refs_3_ = f32[256,128]{1,0:T(8,128)S(1)} collective-permute-done((f32[256,128]{1,0:T(8,128)S(1)}, f32[256,128]{1,0:T(8,128)S(1)}, u32[]{:S(2)}, u32[]{:S(2)}) %collective-permute-start.21) | collective-permute-done | bytes 131104 | tf_op jit(solution)/shard_map/ppermute | solution.py:253
  82.5 0.0 collective-permute-start.25
  82.5 8.4 %shard_map.90 = (bf16[192,2048]{1,0:T(8,128)(2,1)}, bf16[192,2048]{1,0:T(8,128)(2,1)}, f32[192,2048]{1,0:T(8,128)}, f32[192,2048]{1,0:T(8,128)}) custom-call(bf16[2048,128]{1,0:T(8,128)(2,1)S(1)} %get-tuple-element.52.state_ref, f32[192,128]{1,0:T(8,128)S(1)} %get-tuple-element.55.inv_ref, bf16[16,192,192]{2,1,0:T(8,128)(2,1)} %get-tuple-element.56.w_ref, ...), custom_call_target="tpu_custom_call" | custom-call | tf_op jit(solution)/shard_map/pallas_call | solution.py:345
  90.9 0.0 collective-permute-done.26.refs_9_
  90.9 0.0 collective-permute-done.23.refs_5_
  90.9 1.4 %copy-done.8 = f32[192,2048]{1,0:T(8,128)S(1)} copy-done((f32[192,2048]{1,0:T(8,128)S(1)}, f32[192,2048]{1,0:T(8,128)}, u32[]{:S(2)}) %copy-start.8) | copy-done | bytes 1572888
  92.3 4.3 %shard_map.93 = (bf16[192,2048]{1,0:T(8,128)(2,1)}, bf16[192,2048]{1,0:T(8,128)(2,1)}) custom-call(f32[256,128]{1,0:T(8,128)S(1)} %get-tuple-element.65.refs_0_, f32[256,128]{1,0:T(8,128)S(1)} %collective-permute-done.19.refs_1_, f32[256,128]{1,0:T(8,128)S(1)} %collective-permute-done.20.refs_2_, f32[256,128]{1,0:T(8,128)S(1)} %collective-permute-done.21.refs_3_, ...), custom_call_target="tpu_custom_call" | custom-call | tf_op jit(solution)/shard_map/pallas_call | solution.py:355
  (22 shorter events, 0.1 us)
Async XLA Ops:
  0.6 1.1 %copy-start.1 = (bf16[192,2048]{1,0:T(8,128)(2,1)S(1)}, bf16[192,2048]{1,0:T(8,128)(2,1)}, u32[]{:S(2)}) copy-start(bf16[192,2048]{1,0:T(8,128)(2,1)} %refs_10_.1) | copy-start | bytes 2359300
  1.8 1.1 %copy-start.3 = (bf16[192,2048]{1,0:T(8,128)(2,1)S(1)}, bf16[192,2048]{1,0:T(8,128)(2,1)}, u32[]{:S(2)}) copy-start(bf16[192,2048]{1,0:T(8,128)(2,1)} %refs_11_.1) | copy-start | bytes 2359300
  2.9 34.1 %copy-start.7 = (bf16[192,2048]{1,0:T(8,128)(2,1)S(1)}, bf16[192,2048]{1,0:T(8,128)(2,1)}, u32[]{:S(2)}) copy-start(bf16[192,2048]{1,0:T(8,128)(2,1)} %gate_ref.3) | copy-start | bytes 2359300
  2.9 34.1 %copy-start.9 = (bf16[192,2048]{1,0:T(8,128)(2,1)S(1)}, bf16[192,2048]{1,0:T(8,128)(2,1)}, u32[]{:S(2)}) copy-start(bf16[192,2048]{1,0:T(8,128)(2,1)} %cot_ref.1) | copy-start | bytes 2359300
  6.8 30.3 %copy-start.2 = (bf16[192,2048]{1,0:T(8,128)(2,1)S(1)}, bf16[192,2048]{1,0:T(8,128)(2,1)}, u32[]{:S(2)}) copy-start(bf16[192,2048]{1,0:T(8,128)(2,1)} %refs_10_.1) | copy-start | bytes 2359300
  6.8 30.3 %copy-start.4 = (bf16[192,2048]{1,0:T(8,128)(2,1)S(1)}, bf16[192,2048]{1,0:T(8,128)(2,1)}, u32[]{:S(2)}) copy-start(bf16[192,2048]{1,0:T(8,128)(2,1)} %refs_11_.1) | copy-start | bytes 2359300
  6.8 30.3 %copy-start.6 = (bf16[192,2048]{1,0:T(8,128)(2,1)S(1)}, bf16[192,2048]{1,0:T(8,128)(2,1)}, u32[]{:S(2)}) copy-start(bf16[192,2048]{1,0:T(8,128)(2,1)} %q_ref.3) | copy-start | bytes 2359300
  6.8 2.1 %collective-permute-start = (f32[1024,128]{1,0:T(8,128)S(1)}, f32[1024,128]{1,0:T(8,128)S(1)}, u32[]{:S(2)}, u32[]{:S(2)}) collective-permute-start(f32[1024,128]{1,0:T(8,128)S(1)} %get-tuple-element.40), channel_id=1, source_target_pairs={{0,2},{2,0},{4,6},{6,4},{8,10},{10,8},{12,14},{14,12},{16,18},{18,... | collective-permute-start | bytes 1572872 | tf_op jit(solution)/shard_map/ppermute | solution.py:253
  8.9 6.7 %collective-permute-start.1 = (f32[256,128]{1,0:T(8,128)S(1)}, f32[256,128]{1,0:T(8,128)S(1)}, u32[]{:S(2)}, u32[]{:S(2)}) collective-permute-start(f32[256,128]{1,0:T(8,128)S(1)} %get-tuple-element.42), channel_id=1, source_target_pairs={{0,4},{2,6},{4,0},{6,2},{8,12},{10,14},{12,8},{14,10},{16,20},{18,... | collective-permute-start | bytes 393224 | tf_op jit(solution)/shard_map/ppermute | solution.py:253
  11.9 6.4 %collective-permute-start.2 = (f32[256,128]{1,0:T(8,128)S(1)}, f32[256,128]{1,0:T(8,128)S(1)}, u32[]{:S(2)}, u32[]{:S(2)}) collective-permute-start(f32[256,128]{1,0:T(8,128)S(1)} %get-tuple-element.43), channel_id=1, source_target_pairs={{0,8},{2,10},{4,12},{6,14},{8,0},{10,2},{12,4},{14,6},{16,24},{18,... | collective-permute-start | bytes 393224 | tf_op jit(solution)/shard_map/ppermute | solution.py:253
  13.4 6.3 %collective-permute-start.3 = (f32[256,128]{1,0:T(8,128)S(1)}, f32[256,128]{1,0:T(8,128)S(1)}, u32[]{:S(2)}, u32[]{:S(2)}) collective-permute-start(f32[256,128]{1,0:T(8,128)S(1)} %get-tuple-element.44), channel_id=1, source_target_pairs={{0,12},{2,14},{4,8},{6,10},{8,4},{10,6},{12,0},{14,2},{16,28},{18,... | collective-permute-start | bytes 393224 | tf_op jit(solution)/shard_map/ppermute | solution.py:253
  13.4 28.4 %collective-permute-start.12 = (f32[1024,128]{1,0:T(8,128)S(1)}, f32[1024,128]{1,0:T(8,128)S(1)}, u32[]{:S(2)}, u32[]{:S(2)}) collective-permute-start(f32[1024,128]{1,0:T(8,128)S(1)} %get-tuple-element.39.keep_ref), channel_id=1, source_target_pairs={{0,2},{2,0},{4,6},{6,4},{8,10},{10,8},{12,14},{14,12},{16,18},{18,... | collective-permute-start | bytes 1572872 | tf_op jit(solution)/shard_map/ppermute | solution.py:253
  19.8 8.5 %collective-permute-start.4 = (f32[256,128]{1,0:T(8,128)S(1)}, f32[256,128]{1,0:T(8,128)S(1)}, u32[]{:S(2)}, u32[]{:S(2)}) collective-permute-start(f32[256,128]{1,0:T(8,128)S(1)} %add_add_fusion.1), channel_id=1, source_target_pairs={{0,16},{2,18},{4,20},{6,22},{8,24},{10,26},{12,28},{14,30},{16,0},... | collective-permute-start | bytes 393224 | tf_op jit(solution)/shard_map/ppermute | solution.py:253
  28.4 6.4 %collective-permute-start.5 = (f32[256,128]{1,0:T(8,128)S(1)}, f32[256,128]{1,0:T(8,128)S(1)}, u32[]{:S(2)}, u32[]{:S(2)}) collective-permute-start(f32[256,128]{1,0:T(8,128)S(1)} %get-tuple-element.46), channel_id=1, source_target_pairs={{0,4},{2,6},{4,0},{6,2},{8,12},{10,14},{12,8},{14,10},{16,20},{18,... | collective-permute-start | bytes 393224 | tf_op jit(solution)/shard_map/ppermute | solution.py:253
  29.8 5.2 %collective-permute-start.6 = (f32[256,128]{1,0:T(8,128)S(1)}, f32[256,128]{1,0:T(8,128)S(1)}, u32[]{:S(2)}, u32[]{:S(2)}) collective-permute-start(f32[256,128]{1,0:T(8,128)S(1)} %get-tuple-element.47), channel_id=1, source_target_pairs={{0,8},{2,10},{4,12},{6,14},{8,0},{10,2},{12,4},{14,6},{16,24},{18,... | collective-permute-start | bytes 393224 | tf_op jit(solution)/shard_map/ppermute | solution.py:253
  30.4 6.6 %collective-permute-start.7 = (f32[256,128]{1,0:T(8,128)S(1)}, f32[256,128]{1,0:T(8,128)S(1)}, u32[]{:S(2)}, u32[]{:S(2)}) collective-permute-start(f32[256,128]{1,0:T(8,128)S(1)} %get-tuple-element.48), channel_id=1, source_target_pairs={{0,12},{2,14},{4,8},{6,10},{8,4},{10,6},{12,0},{14,2},{16,28},{18,... | collective-permute-start | bytes 393224 | tf_op jit(solution)/shard_map/ppermute | solution.py:253
  32.0 9.8 %collective-permute-start.8 = (f32[256,128]{1,0:T(8,128)S(1)}, f32[256,128]{1,0:T(8,128)S(1)}, u32[]{:S(2)}, u32[]{:S(2)}) collective-permute-start(f32[256,128]{1,0:T(8,128)S(1)} %get-tuple-element.45.refs_0_), channel_id=1, source_target_pairs={{0,2},{2,0},{4,6},{6,4},{8,10},{10,8},{12,14},{14,12},{16,18},{18,... | collective-permute-start | bytes 393224 | tf_op jit(solution)/shard_map/ppermute | solution.py:253
  34.9 6.9 %collective-permute-start.9 = (f32[256,128]{1,0:T(8,128)S(1)}, f32[256,128]{1,0:T(8,128)S(1)}, u32[]{:S(2)}, u32[]{:S(2)}) collective-permute-start(f32[256,128]{1,0:T(8,128)S(1)} %collective-permute-done.5.refs_1_), channel_id=1, source_target_pairs={{0,2},{2,0},{4,6},{6,4},{8,10},{10,8},{12,14},{14,12},{16,18},{18,... | collective-permute-start | bytes 393224 | tf_op jit(solution)/shard_map/ppermute | solution.py:253
  35.0 6.8 %collective-permute-start.10 = (f32[256,128]{1,0:T(8,128)S(1)}, f32[256,128]{1,0:T(8,128)S(1)}, u32[]{:S(2)}, u32[]{:S(2)}) collective-permute-start(f32[256,128]{1,0:T(8,128)S(1)} %collective-permute-done.6.refs_2_), channel_id=1, source_target_pairs={{0,2},{2,0},{4,6},{6,4},{8,10},{10,8},{12,14},{14,12},{16,18},{18,... | collective-permute-start | bytes 393224 | tf_op jit(solution)/shard_map/ppermute | solution.py:253
  37.0 4.8 %collective-permute-start.11 = (f32[256,128]{1,0:T(8,128)S(1)}, f32[256,128]{1,0:T(8,128)S(1)}, u32[]{:S(2)}, u32[]{:S(2)}) collective-permute-start(f32[256,128]{1,0:T(8,128)S(1)} %collective-permute-done.7.refs_3_), channel_id=1, source_target_pairs={{0,2},{2,0},{4,6},{6,4},{8,10},{10,8},{12,14},{14,12},{16,18},{18,... | collective-permute-start | bytes 393224 | tf_op jit(solution)/shard_map/ppermute | solution.py:253
  41.8 7.6 %copy-start = (f32[192,2048]{1,0:T(8,128)S(1)}, f32[192,2048]{1,0:T(8,128)}, u32[]{:S(2)}) copy-start(f32[192,2048]{1,0:T(8,128)} %get-tuple-element.51.refs_12_.gated_ref) | copy-start | bytes 4718596
  45.7 7.8 %copy-start.5 = (f32[192,2048]{1,0:T(8,128)}, f32[192,2048]{1,0:T(8,128)S(1)}, u32[]{:S(2)}) copy-start(f32[192,2048]{1,0:T(8,128)S(1)} %get-tuple-element.54.att_ref) | copy-start | bytes 4718596
  45.7 3.7 %collective-permute-start.13 = (f32[8,192]{1,0:T(8,128)S(1)}, f32[8,192]{1,0:T(8,128)S(1)}, u32[]{:S(2)}, u32[]{:S(2)}) collective-permute-start(f32[8,192]{1,0:T(8,128)S(1)} %get-tuple-element.53.mine_ref), channel_id=1, source_target_pairs={{0,1},{1,0},{2,3},{3,2},{4,5},{5,4},{6,7},{7,6},{8,9},{9,8},{10,11... | collective-permute-start | bytes 18440 | tf_op jit(solution)/shard_map/ppermute | solution.py:290
  53.5 2.0 %collective-permute-start.14 = (f32[1024,128]{1,0:T(8,128)S(1)}, f32[1024,128]{1,0:T(8,128)S(1)}, u32[]{:S(2)}, u32[]{:S(2)}) collective-permute-start(f32[1024,128]{1,0:T(8,128)S(1)} %get-tuple-element.60), channel_id=1, source_target_pairs={{0,2},{2,0},{4,6},{6,4},{8,10},{10,8},{12,14},{14,12},{16,18},{18,... | collective-permute-start | bytes 1572872 | tf_op jit(solution)/shard_map/ppermute | solution.py:253
  55.6 5.6 %collective-permute-start.15 = (f32[256,128]{1,0:T(8,128)S(1)}, f32[256,128]{1,0:T(8,128)S(1)}, u32[]{:S(2)}, u32[]{:S(2)}) collective-permute-start(f32[256,128]{1,0:T(8,128)S(1)} %get-tuple-element.62), channel_id=1, source_target_pairs={{0,4},{2,6},{4,0},{6,2},{8,12},{10,14},{12,8},{14,10},{16,20},{18,... | collective-permute-start | bytes 393224 | tf_op jit(solution)/shard_map/ppermute | solution.py:253
  56.5 6.4 %collective-permute-start.16 = (f32[256,128]{1,0:T(8,128)S(1)}, f32[256,128]{1,0:T(8,128)S(1)}, u32[]{:S(2)}, u32[]{:S(2)}) collective-permute-start(f32[256,128]{1,0:T(8,128)S(1)} %get-tuple-element.63), channel_id=1, source_target_pairs={{0,8},{2,10},{4,12},{6,14},{8,0},{10,2},{12,4},{14,6},{16,24},{18,... | collective-permute-start | bytes 393224 | tf_op jit(solution)/shard_map/ppermute | solution.py:253
  57.8 7.4 %collective-permute-start.17 = (f32[256,128]{1,0:T(8,128)S(1)}, f32[256,128]{1,0:T(8,128)S(1)}, u32[]{:S(2)}, u32[]{:S(2)}) collective-permute-start(f32[256,128]{1,0:T(8,128)S(1)} %get-tuple-element.64), channel_id=1, source_target_pairs={{0,12},{2,14},{4,8},{6,10},{8,4},{10,6},{12,0},{14,2},{16,28},{18,... | collective-permute-start | bytes 393224 | tf_op jit(solution)/shard_map/ppermute | solution.py:253
  59.1 31.7 %collective-permute-start.26 = (f32[1024,128]{1,0:T(8,128)S(1)}, f32[1024,128]{1,0:T(8,128)S(1)}, u32[]{:S(2)}, u32[]{:S(2)}) collective-permute-start(f32[1024,128]{1,0:T(8,128)S(1)} %get-tuple-element.59.keep_ref), channel_id=1, source_target_pairs={{0,2},{2,0},{4,6},{6,4},{8,10},{10,8},{12,14},{14,12},{16,18},{18,... | collective-permute-start | bytes 1572872 | tf_op jit(solution)/shard_map/ppermute | solution.py:253
  65.2 8.5 %collective-permute-start.18 = (f32[256,128]{1,0:T(8,128)S(1)}, f32[256,128]{1,0:T(8,128)S(1)}, u32[]{:S(2)}, u32[]{:S(2)}) collective-permute-start(f32[256,128]{1,0:T(8,128)S(1)} %add_add_fusion), channel_id=1, source_target_pairs={{0,16},{2,18},{4,20},{6,22},{8,24},{10,26},{12,28},{14,30},{16,0},... | collective-permute-start | bytes 393224 | tf_op jit(solution)/shard_map/ppermute | solution.py:253
  73.9 6.4 %collective-permute-start.19 = (f32[256,128]{1,0:T(8,128)S(1)}, f32[256,128]{1,0:T(8,128)S(1)}, u32[]{:S(2)}, u32[]{:S(2)}) collective-permute-start(f32[256,128]{1,0:T(8,128)S(1)} %get-tuple-element.66), channel_id=1, source_target_pairs={{0,4},{2,6},{4,0},{6,2},{8,12},{10,14},{12,8},{14,10},{16,20},{18,... | collective-permute-start | bytes 393224 | tf_op jit(solution)/shard_map/ppermute | solution.py:253
  74.9 5.7 %collective-permute-start.20 = (f32[256,128]{1,0:T(8,128)S(1)}, f32[256,128]{1,0:T(8,128)S(1)}, u32[]{:S(2)}, u32[]{:S(2)}) collective-permute-start(f32[256,128]{1,0:T(8,128)S(1)} %get-tuple-element.67), channel_id=1, source_target_pairs={{0,8},{2,10},{4,12},{6,14},{8,0},{10,2},{12,4},{14,6},{16,24},{18,... | collective-permute-start | bytes 393224 | tf_op jit(solution)/shard_map/ppermute | solution.py:253
  75.6 6.8 %collective-permute-start.21 = (f32[256,128]{1,0:T(8,128)S(1)}, f32[256,128]{1,0:T(8,128)S(1)}, u32[]{:S(2)}, u32[]{:S(2)}) collective-permute-start(f32[256,128]{1,0:T(8,128)S(1)} %get-tuple-element.68), channel_id=1, source_target_pairs={{0,12},{2,14},{4,8},{6,10},{8,4},{10,6},{12,0},{14,2},{16,28},{18,... | collective-permute-start | bytes 393224 | tf_op jit(solution)/shard_map/ppermute | solution.py:253
  77.4 13.4 %collective-permute-start.22 = (f32[256,128]{1,0:T(8,128)S(1)}, f32[256,128]{1,0:T(8,128)S(1)}, u32[]{:S(2)}, u32[]{:S(2)}) collective-permute-start(f32[256,128]{1,0:T(8,128)S(1)} %get-tuple-element.65.refs_0_), channel_id=1, source_target_pairs={{0,2},{2,0},{4,6},{6,4},{8,10},{10,8},{12,14},{14,12},{16,18},{18,... | collective-permute-start | bytes 393224 | tf_op jit(solution)/shard_map/ppermute | solution.py:253
  80.3 10.6 %collective-permute-start.23 = (f32[256,128]{1,0:T(8,128)S(1)}, f32[256,128]{1,0:T(8,128)S(1)}, u32[]{:S(2)}, u32[]{:S(2)}) collective-permute-start(f32[256,128]{1,0:T(8,128)S(1)} %collective-permute-done.19.refs_1_), channel_id=1, source_target_pairs={{0,2},{2,0},{4,6},{6,4},{8,10},{10,8},{12,14},{14,12},{16,18},{18,... | collective-permute-start | bytes 393224 | tf_op jit(solution)/shard_map/ppermute | solution.py:253
  80.7 10.2 %collective-permute-start.24 = (f32[256,128]{1,0:T(8,128)S(1)}, f32[256,128]{1,0:T(8,128)S(1)}, u32[]{:S(2)}, u32[]{:S(2)}) collective-permute-start(f32[256,128]{1,0:T(8,128)S(1)} %collective-permute-done.20.refs_2_), channel_id=1, source_target_pairs={{0,2},{2,0},{4,6},{6,4},{8,10},{10,8},{12,14},{14,12},{16,18},{18,... | collective-permute-start | bytes 393224 | tf_op jit(solution)/shard_map/ppermute | solution.py:253
  82.5 8.4 %collective-permute-start.25 = (f32[256,128]{1,0:T(8,128)S(1)}, f32[256,128]{1,0:T(8,128)S(1)}, u32[]{:S(2)}, u32[]{:S(2)}) collective-permute-start(f32[256,128]{1,0:T(8,128)S(1)} %collective-permute-done.21.refs_3_), channel_id=1, source_target_pairs={{0,2},{2,0},{4,6},{6,4},{8,10},{10,8},{12,14},{14,12},{16,18},{18,... | collective-permute-start | bytes 393224 | tf_op jit(solution)/shard_map/ppermute | solution.py:253
  90.9 1.4 %copy-start.8 = (f32[192,2048]{1,0:T(8,128)S(1)}, f32[192,2048]{1,0:T(8,128)}, u32[]{:S(2)}) copy-start(f32[192,2048]{1,0:T(8,128)} %get-tuple-element.69.refs_12_) | copy-start | bytes 4718596

commit v2 on v0

v2 whole, which is shorter than its diff:
```python
import functools

import jax
import jax.numpy as jnp
from jax import lax
from jax.experimental import pallas as pl
from jax.experimental.pallas import tpu as pltpu
from jax.sharding import PartitionSpec as P

H = 32
DH = 128
EPSILON = 1e-06
QUAD = 4
CHUNKS = 1
F32 = jnp.float32
BF16 = jnp.bfloat16
EXACT = lax.Precision.HIGHEST
SMALL = 16 * 1024 * 1024
LARGE = 60 * 1024 * 1024
ANY = pl.BlockSpec(memory_space=pl.ANY)
VMEM = pl.BlockSpec(memory_space=pltpu.VMEM)


def dot(a, b, ca, cb, precision=None):
    return lax.dot_general(
        a, b, (((ca,), (cb,)), ((), ())), precision=precision, preferred_element_type=F32
    )


def sigmoid(x):
    return 0.5 + 0.5 * jnp.tanh(0.5 * x)


def core_of():
    return lax.rem(lax.axis_index("ctx"), 2)


def chip_of():
    return lax.rem(lax.axis_index("ctx") // 2, QUAD)


def head(g):
    return slice(g * DH, (g + 1) * DH)


def after(values, done):
    flat, tree = jax.tree.flatten(values)
    out = lax.optimization_barrier(tuple(flat) + tuple(jax.tree.leaves(done)))
    return jax.tree.unflatten(tree, out[: len(flat)])


class Plan:
    def __init__(self, rows, width):
        self.rows, self.width = rows, width
        self.heads = width // DH
        self.group = self.heads // (2 * CHUNKS)
        self.span = self.group * DH
        self.part = self.span // QUAD
        self.tall = jax.ShapeDtypeStruct((self.span, DH), F32)
        self.piece = jax.ShapeDtypeStruct((self.part, DH), F32)
        self.low = jax.ShapeDtypeStruct((rows, self.span), BF16)
        self.full = jax.ShapeDtypeStruct((rows, self.span), F32)
        self.wide = jax.ShapeDtypeStruct((rows, DH), F32)
        self.square = jax.ShapeDtypeStruct((self.group, rows, rows), BF16)
        self.state = jax.ShapeDtypeStruct((self.span, DH), BF16)
        self.given = jax.ShapeDtypeStruct((rows, width), BF16)
        self.sums = jax.ShapeDtypeStruct((8, rows), F32)

    def start(self, chunk, side):
        half = lax.rem(core_of() + 1 + side, 2)
        return pl.multiple_of((half * CHUNKS + chunk) * self.span, self.span)

    def columns(self, chunk, side, g=None):
        start = self.start(chunk, side)
        if g is None:
            return pl.ds(start, self.span)
        return pl.ds(pl.multiple_of(start + g * DH, DH), DH)


def run(kernel, out_shape, *args, scratch=(), in_specs=None, out_specs=None, limit=SMALL, aliases=None):
    extra = {}
    if in_specs is not None:
        extra["in_specs"] = in_specs
    if out_specs is not None:
        extra["out_specs"] = out_specs
    if aliases:
        extra["input_output_aliases"] = aliases
    return pl.pallas_call(
        kernel,
        out_shape=out_shape,
        scratch_shapes=list(scratch),
        compiler_params=pltpu.CompilerParams(vmem_limit_bytes=limit),
        **extra,
    )(*args)


def key_state(k, v):
    return dot((k * sigmoid(k)).astype(BF16), v, 0, 0)


def first_kernel(plan, order, k_hbm, v_hbm, k_ref, v_ref, out_ref, sems):
    copies = []
    for n, where in enumerate(order):
        at = (slice(None), plan.columns(*where))
        for m, (source, target) in enumerate(((k_hbm, k_ref), (v_hbm, v_ref))):
            copy = pltpu.make_async_copy(source.at[at], target.at[at], sems.at[2 * n + m])
            copy.start()
            copies.append(copy)
    copies[0].wait()
    copies[1].wait()
    for g in range(plan.group):
        at = plan.columns(*order[0], g)
        out_ref[head(g), :] = key_state(k_ref[:, at].astype(F32), v_ref[:, at])
    for copy in copies[2:]:
        copy.wait()


def next_kernel(plan, where, k_ref, v_ref, out_ref):
    for g in range(plan.group):
        at = plan.columns(*where, g)
        out_ref[head(g), :] = key_state(k_ref[:, at].astype(F32), v_ref[:, at])


def causal_mask(rows):
    return lax.broadcasted_iota(jnp.int32, (rows, rows), 0) >= lax.broadcasted_iota(
        jnp.int32, (rows, rows), 1
    )


def local_kernel(plan, where, q_ref, k_ref, v_ref, gate_ref, cot_ref, lq_ref, lk_ref, w_ref, att_ref, gated_ref):
    causal = causal_mask(plan.rows)
    for g in range(plan.group):
        at = plan.columns(*where, g)
        q = q_ref[:, at].astype(F32)
        k = k_ref[:, at].astype(F32)
        lq = (q * sigmoid(q)).astype(BF16)
        lk = (k * sigmoid(k)).astype(BF16)
        lq_ref[:, head(g)] = lq
        lk_ref[:, head(g)] = lk
        weights = jnp.where(causal, dot(lq, lk, 1, 1), 0.0).astype(BF16)
        w_ref[g] = weights
        att_ref[:, head(g)] = dot(weights, v_ref[:, at], 1, 0)
        gated_ref[:, head(g)] = cot_ref[:, at].astype(F32) * sigmoid(gate_ref[:, at].astype(F32))


def place_state(plan, reverse, pieces, add_ref, state_ref):
    add = core_of() == (0 if reverse else 1)
    chip = chip_of()
    for k in range(QUAD):
        here = pl.ds(pl.multiple_of((chip ^ k) * plan.part, plan.part), plan.part)
        state_ref[here, :] = (pieces[k][...] + jnp.where(add, add_ref[here, :], 0.0)).astype(BF16)


def attend_kernel(plan, first, last, *refs):
    pieces, add_ref = refs[:4], refs[4]
    lq_ref, local_ref, gated_ref = refs[5:8]
    refs = refs[8:]
    if not first:
        square, inner = refs[0][...], refs[1][...]
        refs = refs[2:]
    state_ref, att_ref = refs[:2]
    place_state(plan, False, pieces, add_ref, state_ref)
    for g in range(plan.group):
        att = local_ref[:, head(g)] + dot(lq_ref[:, head(g)], state_ref[head(g), :], 1, 0)
        att_ref[:, head(g)] = att
        if first and g == 0:
            square, inner = att * att, gated_ref[:, head(g)] * att
        else:
            square, inner = square + att * att, inner + gated_ref[:, head(g)] * att
    if last:
        line = lax.broadcasted_iota(jnp.int32, (8, DH), 0)
        refs[2][...] = dot(jnp.where(line == 0, 1.0, 0.0), square, 1, 1, EXACT) + dot(
            jnp.where(line == 1, 1.0, 0.0), inner, 1, 1, EXACT
        )
    else:
        refs[2][...] = square
        refs[3][...] = inner


def grad_kernel(plan, first, a_ref, b_ref, att_ref, gated_ref, lq_ref, d_ref, sum_ref, *more):
    if first:
        total = a_ref[...] + b_ref[...]
        line = lax.broadcasted_iota(jnp.int32, (8, DH), 0)
        sumsq = dot(total, jnp.where(line == 0, 1.0, 0.0), 0, 0, EXACT)
        raw = dot(total, jnp.where(line == 1, 1.0, 0.0), 0, 0, EXACT)
        inv = 1.0 / jnp.sqrt(sumsq * (1.0 / (H * DH)) + EPSILON)
        coef = raw * inv * (1.0 / (H * DH)) * inv * inv
        more[0][...] = inv
        more[1][...] = coef
    else:
        inv, coef = a_ref[...], b_ref[...]
    for g in range(plan.group):
        d = (gated_ref[:, head(g)] * inv - att_ref[:, head(g)] * coef).astype(BF16)
        d_ref[:, head(g)] = d
        sum_ref[head(g), :] = dot(lq_ref[:, head(g)], d, 0, 0)


def inside_kernel(plan, where, first, *refs):
    (state_ref, inv_ref, w_ref, d_ref, lq_ref, lk_ref, att_ref, gated_ref) = refs[:8]
    q_ref, v_ref, gate_ref = refs[8:11]
    gq_hbm, gg_hbm, pk_ref, pv_ref, gq, gg, sems = refs[11 if first else 13 :]
    causal = causal_mask(plan.rows)
    for g in range(plan.group):
        at = plan.columns(*where, g)
        d = d_ref[:, head(g)]
        dw = jnp.where(causal, dot(d, v_ref[:, at], 1, 1), 0.0).astype(BF16)
        glq = dot(dw, lk_ref[:, head(g)], 1, 0) + dot(d, state_ref[head(g), :], 1, 1)
        q = q_ref[:, at].astype(F32)
        sig = sigmoid(q)
        gq[:, head(g)] = (glq * (sig * (1.0 + q * (1.0 - sig)))).astype(BF16)
        pk_ref[:, head(g)] = dot(dw, lq_ref[:, head(g)], 0, 0)
        pv_ref[:, head(g)] = dot(w_ref[g], d, 0, 0)
        gate = sigmoid(gate_ref[:, at].astype(F32))
        gg[:, head(g)] = (
            gated_ref[:, head(g)] * (att_ref[:, head(g)] * inv_ref[...]) * (1.0 - gate)
        ).astype(BF16)
    send_out(plan, where, ((gq, gq_hbm), (gg, gg_hbm)), sems)


def send_out(plan, where, pairs, sems):
    at = (slice(None), plan.columns(*where))
    copies = [
        pltpu.make_async_copy(source, target.at[at], sems.at[n])
        for n, (source, target) in enumerate(pairs)
    ]
    for copy in copies:
        copy.start()
    for copy in copies:
        copy.wait()


def finish_kernel(plan, where, first, *refs):
    pieces, add_ref = refs[:4], refs[4]
    k_ref, v_ref, lk_ref, pk_ref, pv_ref = refs[5:10]
    gk_hbm, gv_hbm, state_ref, gk, gv, sems = refs[10 if first else 12 :]
    place_state(plan, True, pieces, add_ref, state_ref)
    for g in range(plan.group):
        at = plan.columns(*where, g)
        state = state_ref[head(g), :]
        k = k_ref[:, at].astype(F32)
        sig = sigmoid(k)
        gv[:, head(g)] = (pv_ref[:, head(g)] + dot(lk_ref[:, head(g)], state, 1, 0)).astype(BF16)
        glk = pk_ref[:, head(g)] + dot(v_ref[:, at], state, 1, 1)
        gk[:, head(g)] = (glk * (sig * (1.0 + k * (1.0 - sig)))).astype(BF16)
    send_out(plan, where, ((gk, gk_hbm), (gv, gv_hbm)), sems)


def split_kernel(plan, keep_ref, got_ref, *outs):
    chip = chip_of()
    for k in range(QUAD):
        here = pl.ds(pl.multiple_of((chip ^ k) * plan.part, plan.part), plan.part)
        outs[k][...] = keep_ref[here, :] + got_ref[here, :]


def before_kernel(reverse, span, *refs):
    parts, got_ref, base, outs = refs[:4], refs[4], refs[5:-4], refs[-4:]
    chip = chip_of()
    far = lax.rem(lax.axis_index("ctx") // span, 2) == (0 if reverse else 1)
    start = jnp.where(far, got_ref[...], 0.0)
    for more in base:
        start = start + more[...]
    for k in range(QUAD):
        total = start
        for m in range(QUAD):
            first = (chip ^ m) > (chip ^ k) if reverse else (chip ^ m) < (chip ^ k)
            total = total + jnp.where(first, parts[m][...], 0.0)
        outs[k][...] = total


def swap(x, distance):
    count = lax.axis_size("ctx")
    return lax.ppermute(x, "ctx", [(i, i ^ distance) for i in range(count)])


def gather_sums(plan, keep, near):
    mine = run(functools.partial(split_kernel, plan), [plan.piece] * QUAD, keep, near)
    return [mine[0]] + [swap(mine[k], 2 * k) for k in range(1, QUAD)]


def across(parts, reverse):
    count = lax.axis_size("ctx")
    total = (parts[0] + parts[1]) + (parts[2] + parts[3])
    base = []
    span = 2 * QUAD
    while True:
        got = swap(total, span)
        if 2 * span >= count:
            return got, base, span
        far = lax.rem(lax.axis_index("ctx") // span, 2) == (0 if reverse else 1)
        term = jnp.where(far, got, 0.0)
        base = [base[0] + term] if base else [term]
        total = total + got
        span *= 2


def hand_out(plan, parts, got, base, span, reverse):
    outs = run(
        functools.partial(before_kernel, reverse, span),
        [plan.piece] * QUAD,
        *parts,
        got,
        *base,
    )
    return [outs[0]] + [swap(outs[k], 2 * k) for k in range(1, QUAD)]


def head_total(sums):
    if lax.axis_size("head") == 2:
        return sums, lax.ppermute(sums, "head", [(0, 1), (1, 0)])
    return lax.psum(sums, "head"), jnp.zeros_like(sums)


def carried(plan, sums_of, work, reverse):
    chunks = range(CHUNKS)
    near = [swap(sums_of[c, 0], 1) for c in chunks]
    parts = [gather_sums(plan, sums_of[c, 1], near[c]) for c in chunks]
    far_add = [swap(after(sums_of[c, 1], near[c]), 1) for c in chunks]
    results = []
    held = parts[-1][0]
    done = [t(held) for t in work[0]]
    results += done
    parts = [after(p, done) for p in parts]
    crossed = [across(p, reverse) for p in parts]
    done = [t(parts[-1][0]) for t in work[1]]
    results += done
    crossed = [(after(got, done), base, span) for got, base, span in crossed]
    pieces = {}
    for c in chunks:
        own = hand_out(plan, parts[c], *crossed[c], reverse)
        pieces[c, 1] = own + [near[c]]
        pieces[c, 0] = [swap(x, 1) for x in own] + [far_add[c]]
    return pieces, results


def per_device(queries, key_rows, value_rows, gate_rows, cotangent):
    plan = Plan(*queries.shape)
    groups = [(c, side) for c in range(CHUNKS) for side in (0, 1)]
    late = [(c, side) for c in range(CHUNKS) for side in (1, 0)]
    count = len(groups)
    k, v, first_sum = run(
        functools.partial(first_kernel, plan, groups),
        [plan.given, plan.given, plan.tall],
        key_rows,
        value_rows,
        scratch=[pltpu.SemaphoreType.DMA((2 * count,))],
        in_specs=[ANY, ANY],
        limit=LARGE,
    )
    sums = {groups[0]: first_sum}
    for where in groups[1:]:
        sums[where] = run(functools.partial(next_kernel, plan, where), plan.tall, k, v)

    def local(where):
        def thunk(held):
            args = after((queries, k, v, gate_rows, cotangent), held)
            return run(
                functools.partial(local_kernel, plan, where),
                [plan.low, plan.low, plan.square, plan.full, plan.full],
                *args,
            )

        return thunk

    thunks = [local(where) for where in groups]
    pieces, made = carried(plan, sums, (thunks[: count // 2], thunks[count // 2 :]), False)
    made = dict(zip(groups, made))
    lq, lk, weights, inside, gated = ({w: made[w][n] for w in groups} for n in range(5))
    state, attended, running = {}, {}, ()
    for n, where in enumerate(late):
        last = n == count - 1
        state[where], attended[where], *running = run(
            functools.partial(attend_kernel, plan, n == 0, last),
            [plan.state, plan.full] + ([plan.sums] if last else [plan.wide] * 2),
            *pieces[where],
            lq[where],
            inside[where],
            gated[where],
            *running,
        )
    scales = head_total(running[0])
    d_attn, sums = {}, {}
    for n, where in enumerate(groups):
        d_attn[where], sums[where], *more = run(
            functools.partial(grad_kernel, plan, n == 0),
            [plan.low, plan.tall] + ([plan.wide] * 2 if n == 0 else []),
            *scales,
            attended[where],
            gated[where],
            lq[where],
        )
        scales = more or scales
    outer = []

    def inner(where):
        def thunk(held):
            first = not outer
            args = after(
                (
                    state[where], scales[0], weights[where], d_attn[where], lq[where], lk[where],
                    attended[where], gated[where], queries, v, gate_rows,
                ),
                held,
            )
            gq, gg, pk, pv = run(
                functools.partial(inside_kernel, plan, where, first),
                [plan.given, plan.given, plan.full, plan.full],
                *args,
                *outer,
                scratch=[pltpu.VMEM((plan.rows, plan.span), BF16)] * 2
                + [pltpu.SemaphoreType.DMA((2,))],
                in_specs=[VMEM] * 11 + [ANY] * len(outer),
                out_specs=[ANY, ANY, VMEM, VMEM],
                aliases={} if first else {11: 0, 12: 1},
            )
            outer[:] = [gq, gg]
            return pk, pv

        return thunk

    thunks = [inner(where) for where in groups]
    pieces, made = carried(plan, sums, (thunks[: count // 2], thunks[count // 2 :]), True)
    made = dict(zip(groups, made))
    ends = []
    for n, where in enumerate(late):
        ends = run(
            functools.partial(finish_kernel, plan, where, n == 0),
            [plan.given, plan.given],
            *pieces[where],
            k,
            v,
            lk[where],
            *made[where],
            *ends,
            scratch=[pltpu.VMEM((plan.span, DH), BF16)]
            + [pltpu.VMEM((plan.rows, plan.span), BF16)] * 2
            + [pltpu.SemaphoreType.DMA((2,))],
            in_specs=[VMEM] * 10 + [ANY] * len(ends),
            out_specs=[ANY, ANY],
            aliases={} if n == 0 else {10: 0, 11: 1},
        )
    return (outer[0], ends[0], ends[1], outer[1])


def solution(mesh):
    spec = P("ctx", "head")
    return jax.shard_map(
        per_device, mesh=mesh, in_specs=(spec,) * 5, out_specs=(spec,) * 4, check_vma=False
    )
```

time: 338 us -> 74.4 us (0.22)
  waiting for transfers between devices: 263 us -> 30.5 us
  other arithmetic: 31.5 us -> 0.06 us
  starting transfers between devices: 0.08 us -> 22.5 us
  Pallas kernels: 0 us -> 17.9 us
  matrix products: 16.5 us -> 0 us
  between operations: 14.2 us -> 0.9 us
  blocking collectives: 4.93 us -> 0 us
  local copies, waits for them, and re-layouts: 6.08 us -> 2.29 us
    all_gather x2 -> x0, waiting for transfers between devices: 263 us -> none  [carried_in(): gathered = lax.all_gather(part, axis)]
    ppermute x0 -> x27, waiting for transfers between devices: none -> 30.5 us  [the longest x26 28.3 us: swap(): return lax.ppermute(x, 'ctx', [(i, i ^ distance) for i in range(count)])]
    ppermute x0 -> x27, starting transfers between devices: none -> 22.5 us  [the longest x26 21 us: swap(): return lax.ppermute(x, 'ctx', [(i, i ^ distance) for i in range(count)])]
    add x15 -> x2, other arithmetic: 22.3 us -> 0.06 us  [across(): total = parts[0] + parts[1] + (parts[2] + parts[3])]
    pallas_call x0 -> x16, Pallas kernels: none -> 17.9 us  [run(): pl.pallas_call(kernel, out_shape=out_shape, scratch_shapes=list(scratch),...]
    dot_general x12 -> x0, matrix products: 16.5 us -> none  [the longest x1 2.23 us: per_device(): jnp.einsum('thd,hde->the', lifted_q, prefix_low, preferred_element_type=j...]
    convert_element_type x3 -> x0, other arithmetic: 6.32 us -> none  [the longest x1 3.36 us: per_device(): grad_gates = (grad_out * normed * sig * (1.0 - sig)).astype(jnp.bfloat16)]
    psum x1 -> x0, blocking collectives: 4.93 us -> none  [per_device(): lax.psum((jnp.sum(attended * attended, axis=1), jnp.sum(gated * attended,...]
  transfers between devices with their start and end apart: 2 -> 27, of which waited for: 2 -> 16; matrix products, arithmetic and copies ran while one was open for 3% -> 0% of each run, Pallas kernels for 0% -> 16%
where the time goes in v2:
time: 74.4 us; the launch traced here: 74.2 us
  waiting for transfers between devices  30.5 us (41%)
  starting transfers between devices  22.5 us (30%)
  Pallas kernels  17.9 us (24%)
  local copies, waits for them, and re-layouts  2.29 us (3%)
  between operations  0.9 us (1%)
    ppermute x26, waiting for transfers between devices, swap(): return lax.ppermute(x, 'ctx', [(i, i ^ distance) for i in range(count)])  28.3 us
    ppermute x26, starting transfers between devices, swap(): return lax.ppermute(x, 'ctx', [(i, i ^ distance) for i in range(count)])  21 us
    pallas_call x16, Pallas kernels, run(): pl.pallas_call(kernel, out_shape=out_shape, scratch_shapes=list(scratch),...  17.9 us
    unnamed x14, local copies, waits for them, and re-layouts  2.29 us
    ppermute x1, waiting for transfers between devices, head_total(): return (sums, lax.ppermute(sums, 'head', [(0, 1), (1, 0)]))  2.13 us
    ppermute x1, starting transfers between devices, head_total(): return (sums, lax.ppermute(sums, 'head', [(0, 1), (1, 0)]))  1.54 us
  transfers between devices with their start and end apart: 27, of which 16 were waited for; matrix products, arithmetic and copies ran while one was open for 0% of the time, Pallas kernels for 16%

profile of v2, /device:TPU:0, one launch (start us, length us, event | category | flops | bytes accessed | tf_op | source)
XLA Modules:
  0.0 74.2 jit_solution(668981050788714341)
XLA Ops:
  0.6 3.0 %shard_map.84 = (bf16[192,2048]{1,0:T(8,128)(2,1)}, bf16[192,2048]{1,0:T(8,128)(2,1)}, f32[1024,128]{1,0:T(8,128)}) custom-call(bf16[192,2048]{1,0:T(8,128)(2,1)} %k_hbm.1, bf16[192,2048]{1,0:T(8,128)(2,1)} %v_hbm.1), custom_call_target="tpu_custom_call" | custom-call | tf_op jit(solution)/shard_map/pallas_call | solution.py:88
  3.6 0.5 collective-permute-start
  4.2 1.1 %copy-done = bf16[192,2048]{1,0:T(8,128)(2,1)S(1)} copy-done((bf16[192,2048]{1,0:T(8,128)(2,1)S(1)}, bf16[192,2048]{1,0:T(8,128)(2,1)}, u32[]{:S(2)}) %copy-start) | copy-done | bytes 786456
  5.3 1.1 %copy-done.2 = bf16[192,2048]{1,0:T(8,128)(2,1)S(1)} copy-done((bf16[192,2048]{1,0:T(8,128)(2,1)S(1)}, bf16[192,2048]{1,0:T(8,128)(2,1)}, u32[]{:S(2)}) %copy-start.2) | copy-done | bytes 786456
  6.4 0.4 shard_map.85.keep_ref
  6.9 0.0 copy-start.1
  6.9 0.0 collective-permute-done.got_ref.refs_4_
  6.9 0.1 shard_map.86
  7.0 2.6 %collective-permute-start.1 = (f32[256,128]{1,0:T(8,128)S(1)}, f32[256,128]{1,0:T(8,128)S(1)}, u32[]{:S(2)}, u32[]{:S(2)}) collective-permute-start(f32[256,128]{1,0:T(8,128)S(1)} %get-tuple-element.106), channel_id=1, source_target_pairs={{0,4},{2,6},{4,0},{6,2},{8,12},{10,14},{12,8},{14,10},{16,20},{18,... | collective-permute-start | bytes 393224 | tf_op jit(solution)/shard_map/ppermute | solution.py:272
  9.6 1.6 %collective-permute-start.2 = (f32[256,128]{1,0:T(8,128)S(1)}, f32[256,128]{1,0:T(8,128)S(1)}, u32[]{:S(2)}, u32[]{:S(2)}) collective-permute-start(f32[256,128]{1,0:T(8,128)S(1)} %get-tuple-element.107), channel_id=1, source_target_pairs={{0,8},{2,10},{4,12},{6,14},{8,0},{10,2},{12,4},{14,6},{16,24},{18,... | collective-permute-start | bytes 393224 | tf_op jit(solution)/shard_map/ppermute | solution.py:272
  11.2 0.0 collective-permute-start.3
  11.2 0.0 collective-permute-start.12
  11.2 1.1 %shard_map.87 = (bf16[192,1024]{1,0:T(8,128)(2,1)S(1)}, bf16[192,1024]{1,0:T(8,128)(2,1)S(1)}, bf16[8,192,192]{2,1,0:T(8,128)(2,1)S(1)}, f32[192,1024]{1,0:T(8,128)S(1)}, f32[192,1024]{1,0:T(8,128)S(1)}) custom-call(bf16[192,2048]{1,0:T(8,128)(2,1)S(1)} %copy-done.4, bf16[192,2048]{1,0:T(8,128)(2,1)S(1)} %copy-done.3, bf16[192,2048]{1,0:T(8,128)(2,1)S(1)} %copy-done.1, ...), custom_call_target="tpu_custom_call" | custom-call | tf_op jit(solution)/shard_map/pallas_call | solution.py:88
  12.4 1.4 %collective-permute-done.1.refs_1_ = f32[256,128]{1,0:T(8,128)S(1)} collective-permute-done((f32[256,128]{1,0:T(8,128)S(1)}, f32[256,128]{1,0:T(8,128)S(1)}, u32[]{:S(2)}, u32[]{:S(2)}) %collective-permute-start.1) | collective-permute-done | bytes 131104 | tf_op jit(solution)/shard_map/ppermute | solution.py:272
  13.7 2.2 %collective-permute-done.2.refs_2_ = f32[256,128]{1,0:T(8,128)S(1)} collective-permute-done((f32[256,128]{1,0:T(8,128)S(1)}, f32[256,128]{1,0:T(8,128)S(1)}, u32[]{:S(2)}, u32[]{:S(2)}) %collective-permute-start.2) | collective-permute-done | bytes 131104 | tf_op jit(solution)/shard_map/ppermute | solution.py:272
  15.9 1.9 %collective-permute-done.3.refs_3_ = f32[256,128]{1,0:T(8,128)S(1)} collective-permute-done((f32[256,128]{1,0:T(8,128)S(1)}, f32[256,128]{1,0:T(8,128)S(1)}, u32[]{:S(2)}, u32[]{:S(2)}) %collective-permute-start.3) | collective-permute-done | bytes 131104 | tf_op jit(solution)/shard_map/ppermute | solution.py:272
  17.8 2.8 %collective-permute-start.4 = (f32[256,128]{1,0:T(8,128)S(1)}, f32[256,128]{1,0:T(8,128)S(1)}, u32[]{:S(2)}, u32[]{:S(2)}) collective-permute-start(f32[256,128]{1,0:T(8,128)S(1)} %add_add_fusion.1), channel_id=1, source_target_pairs={{0,16},{2,18},{4,20},{6,22},{8,24},{10,26},{12,28},{14,30},{16,0},... | collective-permute-start | bytes 393224 | tf_op jit(solution)/shard_map/ppermute | solution.py:272
  20.6 1.1 %shard_map.88 = (bf16[192,1024]{1,0:T(8,128)(2,1)S(1)}, bf16[192,1024]{1,0:T(8,128)(2,1)S(1)}, bf16[8,192,192]{2,1,0:T(8,128)(2,1)S(1)}, f32[192,1024]{1,0:T(8,128)S(1)}, f32[192,1024]{1,0:T(8,128)S(1)}) custom-call(bf16[192,2048]{1,0:T(8,128)(2,1)S(1)} %copy-done.4, bf16[192,2048]{1,0:T(8,128)(2,1)S(1)} %copy-done.3, bf16[192,2048]{1,0:T(8,128)(2,1)S(1)} %copy-done.1, ...), custom_call_target="tpu_custom_call" | custom-call | tf_op jit(solution)/shard_map/pallas_call | solution.py:88
  21.8 4.9 %collective-permute-done.4.refs_4_ = f32[256,128]{1,0:T(8,128)S(1)} collective-permute-done((f32[256,128]{1,0:T(8,128)S(1)}, f32[256,128]{1,0:T(8,128)S(1)}, u32[]{:S(2)}, u32[]{:S(2)}) %collective-permute-start.4) | collective-permute-done | bytes 131104 | tf_op jit(solution)/shard_map/ppermute | solution.py:272
  26.7 0.1 shard_map.89
  26.8 1.4 %collective-permute-start.5 = (f32[256,128]{1,0:T(8,128)S(1)}, f32[256,128]{1,0:T(8,128)S(1)}, u32[]{:S(2)}, u32[]{:S(2)}) collective-permute-start(f32[256,128]{1,0:T(8,128)S(1)} %get-tuple-element.135), channel_id=1, source_target_pairs={{0,4},{2,6},{4,0},{6,2},{8,12},{10,14},{12,8},{14,10},{16,20},{18,... | collective-permute-start | bytes 393224 | tf_op jit(solution)/shard_map/ppermute | solution.py:272
  28.2 0.7 collective-permute-start.6
  28.9 1.5 %collective-permute-start.7 = (f32[256,128]{1,0:T(8,128)S(1)}, f32[256,128]{1,0:T(8,128)S(1)}, u32[]{:S(2)}, u32[]{:S(2)}) collective-permute-start(f32[256,128]{1,0:T(8,128)S(1)} %get-tuple-element.137), channel_id=1, source_target_pairs={{0,12},{2,14},{4,8},{6,10},{8,4},{10,6},{12,0},{14,2},{16,28},{18,... | collective-permute-start | bytes 393224 | tf_op jit(solution)/shard_map/ppermute | solution.py:272
  30.4 0.0 collective-permute-start.8
  30.4 1.7 %collective-permute-done.5.refs_1_ = f32[256,128]{1,0:T(8,128)S(1)} collective-permute-done((f32[256,128]{1,0:T(8,128)S(1)}, f32[256,128]{1,0:T(8,128)S(1)}, u32[]{:S(2)}, u32[]{:S(2)}) %collective-permute-start.5) | collective-permute-done | bytes 131104 | tf_op jit(solution)/shard_map/ppermute | solution.py:272
  32.1 0.0 collective-permute-start.9
  32.1 1.6 %collective-permute-done.6.refs_2_ = f32[256,128]{1,0:T(8,128)S(1)} collective-permute-done((f32[256,128]{1,0:T(8,128)S(1)}, f32[256,128]{1,0:T(8,128)S(1)}, u32[]{:S(2)}, u32[]{:S(2)}) %collective-permute-start.6) | collective-permute-done | bytes 131104 | tf_op jit(solution)/shard_map/ppermute | solution.py:272
  33.8 0.0 collective-permute-start.10
  33.8 2.2 %collective-permute-done.7.refs_3_ = f32[256,128]{1,0:T(8,128)S(1)} collective-permute-done((f32[256,128]{1,0:T(8,128)S(1)}, f32[256,128]{1,0:T(8,128)S(1)}, u32[]{:S(2)}, u32[]{:S(2)}) %collective-permute-start.7) | collective-permute-done | bytes 131104 | tf_op jit(solution)/shard_map/ppermute | solution.py:272
  36.0 0.0 collective-permute-start.11
  36.0 0.4 shard_map.90
  36.4 0.0 collective-permute-done.8.refs_0_
  36.4 0.0 collective-permute-done.9.refs_1_
  36.4 0.9 %collective-permute-done.11.refs_3_ = f32[256,128]{1,0:T(8,128)S(1)} collective-permute-done((f32[256,128]{1,0:T(8,128)S(1)}, f32[256,128]{1,0:T(8,128)S(1)}, u32[]{:S(2)}, u32[]{:S(2)}) %collective-permute-start.11) | collective-permute-done | bytes 131104 | tf_op jit(solution)/shard_map/ppermute | solution.py:272
  37.4 0.8 %shard_map.91 = (bf16[1024,128]{1,0:T(8,128)(2,1)S(1)}, f32[192,1024]{1,0:T(8,128)S(1)}, f32[8,192]{1,0:T(8,128)S(1)}) custom-call(f32[256,128]{1,0:T(8,128)S(1)} %collective-permute-done.8.refs_0_, f32[256,128]{1,0:T(8,128)S(1)} %collective-permute-done.9.refs_1_, f32[256,128]{1,0:T(8,128)S(1)} %collective-permute-done.10.refs_2_, ...), custom_call_target="tpu_custom_call" | custom-call | tf_op jit(solution)/shard_map/pallas_call | solution.py:88
  38.1 1.5 %collective-permute-start.13 = (f32[8,192]{1,0:T(8,128)S(1)}, f32[8,192]{1,0:T(8,128)S(1)}, u32[]{:S(2)}, u32[]{:S(2)}) collective-permute-start(f32[8,192]{1,0:T(8,128)S(1)} %get-tuple-element.142.a_ref), channel_id=1, source_target_pairs={{0,1},{1,0},{2,3},{3,2},{4,5},{5,4},{6,7},{7,6},{8,9},{9,8},{10,11... | collective-permute-start | bytes 18440 | tf_op jit(solution)/shard_map/ppermute | solution.py:309
  39.7 2.1 %collective-permute-done.13.b_ref = f32[8,192]{1,0:T(8,128)S(1)} collective-permute-done((f32[8,192]{1,0:T(8,128)S(1)}, f32[8,192]{1,0:T(8,128)S(1)}, u32[]{:S(2)}, u32[]{:S(2)}) %collective-permute-start.13) | collective-permute-done | bytes 6176 | tf_op jit(solution)/shard_map/ppermute | solution.py:309
  41.8 0.7 shard_map.92
  42.5 0.1 collective-permute-start.14
  42.6 0.4 shard_map.93
  43.0 1.5 %collective-permute-done.14.got_ref.refs_4_ = f32[1024,128]{1,0:T(8,128)S(1)} collective-permute-done((f32[1024,128]{1,0:T(8,128)S(1)}, f32[1024,128]{1,0:T(8,128)S(1)}, u32[]{:S(2)}, u32[]{:S(2)}) %collective-permute-start.14) | collective-permute-done | bytes 524320 | tf_op jit(solution)/shard_map/ppermute | solution.py:272
  44.5 0.1 shard_map.94
  44.6 0.7 collective-permute-start.15
  45.2 1.6 %collective-permute-start.16 = (f32[256,128]{1,0:T(8,128)S(1)}, f32[256,128]{1,0:T(8,128)S(1)}, u32[]{:S(2)}, u32[]{:S(2)}) collective-permute-start(f32[256,128]{1,0:T(8,128)S(1)} %get-tuple-element.152), channel_id=1, source_target_pairs={{0,8},{2,10},{4,12},{6,14},{8,0},{10,2},{12,4},{14,6},{16,24},{18,... | collective-permute-start | bytes 393224 | tf_op jit(solution)/shard_map/ppermute | solution.py:272
  46.9 1.2 %collective-permute-start.17 = (f32[256,128]{1,0:T(8,128)S(1)}, f32[256,128]{1,0:T(8,128)S(1)}, u32[]{:S(2)}, u32[]{:S(2)}) collective-permute-start(f32[256,128]{1,0:T(8,128)S(1)} %get-tuple-element.153), channel_id=1, source_target_pairs={{0,12},{2,14},{4,8},{6,10},{8,4},{10,6},{12,0},{14,2},{16,28},{18,... | collective-permute-start | bytes 393224 | tf_op jit(solution)/shard_map/ppermute | solution.py:272
  48.1 3.3 %shard_map.95 = (bf16[192,2048]{1,0:T(8,128)(2,1)}, bf16[192,2048]{1,0:T(8,128)(2,1)}, f32[192,1024]{1,0:T(8,128)S(1)}, f32[192,1024]{1,0:T(8,128)S(1)}) custom-call(bf16[1024,128]{1,0:T(8,128)(2,1)S(1)} %get-tuple-element.156.refs_0_, f32[192,128]{1,0:T(8,128)S(1)} %get-tuple-element.171.a_ref.refs_1_, bf16[8,192,192]{2,1,0:T(8,128)(2,1)S(1)} %get-tuple-element.158.refs_2_, ...), custom_call_target="tpu_custom_call" | custom-call | tf_op jit(solution)/shard_map/pallas_call | solution.py:88
  51.4 0.2 collective-permute-done.16.refs_2_
  51.6 2.5 %collective-permute-done.17.refs_3_ = f32[256,128]{1,0:T(8,128)S(1)} collective-permute-done((f32[256,128]{1,0:T(8,128)S(1)}, f32[256,128]{1,0:T(8,128)S(1)}, u32[]{:S(2)}, u32[]{:S(2)}) %collective-permute-start.17) | collective-permute-done | bytes 131104 | tf_op jit(solution)/shard_map/ppermute | solution.py:272
  54.2 2.5 %collective-permute-start.18 = (f32[256,128]{1,0:T(8,128)S(1)}, f32[256,128]{1,0:T(8,128)S(1)}, u32[]{:S(2)}, u32[]{:S(2)}) collective-permute-start(f32[256,128]{1,0:T(8,128)S(1)} %add_add_fusion), channel_id=1, source_target_pairs={{0,16},{2,18},{4,20},{6,22},{8,24},{10,26},{12,28},{14,30},{16,0},... | collective-permute-start | bytes 393224 | tf_op jit(solution)/shard_map/ppermute | solution.py:272
  56.7 3.3 %shard_map.96 = (bf16[192,2048]{1,0:T(8,128)(2,1)}, bf16[192,2048]{1,0:T(8,128)(2,1)}, f32[192,1024]{1,0:T(8,128)S(1)}, f32[192,1024]{1,0:T(8,128)S(1)}) custom-call(bf16[1024,128]{1,0:T(8,128)(2,1)S(1)} %get-tuple-element.170.refs_0_, f32[192,128]{1,0:T(8,128)S(1)} %get-tuple-element.171.a_ref.refs_1_, ...), custom_call_target="tpu_custom_call", output_to_operand_aliasing={{0}: (11, {}), {1}: (12, {})} | custom-call | tf_op jit(solution)/shard_map/pallas_call | solution.py:88
  60.0 2.3 %collective-permute-done.18.refs_4_ = f32[256,128]{1,0:T(8,128)S(1)} collective-permute-done((f32[256,128]{1,0:T(8,128)S(1)}, f32[256,128]{1,0:T(8,128)S(1)}, u32[]{:S(2)}, u32[]{:S(2)}) %collective-permute-start.18) | collective-permute-done | bytes 131104 | tf_op jit(solution)/shard_map/ppermute | solution.py:272
  62.4 0.1 shard_map.97
  62.5 1.3 %collective-permute-start.20 = (f32[256,128]{1,0:T(8,128)S(1)}, f32[256,128]{1,0:T(8,128)S(1)}, u32[]{:S(2)}, u32[]{:S(2)}) collective-permute-start(f32[256,128]{1,0:T(8,128)S(1)} %get-tuple-element.191), channel_id=1, source_target_pairs={{0,4},{2,6},{4,0},{6,2},{8,12},{10,14},{12,8},{14,10},{16,20},{18,... | collective-permute-start | bytes 393224 | tf_op jit(solution)/shard_map/ppermute | solution.py:272
  63.8 0.7 collective-permute-start.22
  64.5 1.5 %collective-permute-start.24 = (f32[256,128]{1,0:T(8,128)S(1)}, f32[256,128]{1,0:T(8,128)S(1)}, u32[]{:S(2)}, u32[]{:S(2)}) collective-permute-start(f32[256,128]{1,0:T(8,128)S(1)} %get-tuple-element.193), channel_id=1, source_target_pairs={{0,12},{2,14},{4,8},{6,10},{8,4},{10,6},{12,0},{14,2},{16,28},{18,... | collective-permute-start | bytes 393224 | tf_op jit(solution)/shard_map/ppermute | solution.py:272
  66.0 2.9 %collective-permute-done.20.refs_1_ = f32[256,128]{1,0:T(8,128)S(1)} collective-permute-done((f32[256,128]{1,0:T(8,128)S(1)}, f32[256,128]{1,0:T(8,128)S(1)}, u32[]{:S(2)}, u32[]{:S(2)}) %collective-permute-start.20) | collective-permute-done | bytes 131104 | tf_op jit(solution)/shard_map/ppermute | solution.py:272
  68.9 0.3 collective-permute-done.22.refs_2_
  69.2 0.2 collective-permute-start.23
  69.4 1.6 %collective-permute-done.24.refs_3_ = f32[256,128]{1,0:T(8,128)S(1)} collective-permute-done((f32[256,128]{1,0:T(8,128)S(1)}, f32[256,128]{1,0:T(8,128)S(1)}, u32[]{:S(2)}, u32[]{:S(2)}) %collective-permute-start.24) | collective-permute-done | bytes 131104 | tf_op jit(solution)/shard_map/ppermute | solution.py:272
  71.0 1.5 %shard_map.98 = (bf16[192,2048]{1,0:T(8,128)(2,1)}, bf16[192,2048]{1,0:T(8,128)(2,1)}) custom-call(f32[256,128]{1,0:T(8,128)S(1)} %get-tuple-element.190.refs_0_, f32[256,128]{1,0:T(8,128)S(1)} %collective-permute-done.20.refs_1_, f32[256,128]{1,0:T(8,128)S(1)} %collective-permute-done.22.refs_2_, f32[256,128]{1,0:T(8,128)S(1)} %collective-permute-done.24.refs_3_, ...), custom_call_target="tpu_custom_call" | custom-call | tf_op jit(solution)/shard_map/pallas_call | solution.py:88
  72.6 0.0 collective-permute-done.26.refs_4_
  72.6 0.0 collective-permute-done.21.refs_1_
  72.6 0.0 collective-permute-done.25.refs_3_
  72.6 1.5 %shard_map.99 = (bf16[192,2048]{1,0:T(8,128)(2,1)}, bf16[192,2048]{1,0:T(8,128)(2,1)}) custom-call(f32[256,128]{1,0:T(8,128)S(1)} %collective-permute-done.19.refs_0_, f32[256,128]{1,0:T(8,128)S(1)} %collective-permute-done.21.refs_1_, f32[256,128]{1,0:T(8,128)S(1)} %collective-permute-done.23.refs_2_, ...), custom_call_target="tpu_custom_call", output_to_operand_aliasing={{0}: (10, {}), {1}: (11, {})} | custom-call | tf_op jit(solution)/shard_map/pallas_call | solution.py:88
  (22 shorter events, 0.1 us)
Async XLA Ops:
  0.6 10.5 %copy-start.6 = (bf16[192,2048]{1,0:T(8,128)(2,1)S(1)}, bf16[192,2048]{1,0:T(8,128)(2,1)}, u32[]{:S(2)}) copy-start(bf16[192,2048]{1,0:T(8,128)(2,1)} %cot_ref.1) | copy-start | bytes 2359300
  3.6 3.3 %collective-permute-start = (f32[1024,128]{1,0:T(8,128)}, f32[1024,128]{1,0:T(8,128)S(1)}, u32[]{:S(2)}, u32[]{:S(2)}) collective-permute-start(f32[1024,128]{1,0:T(8,128)} %get-tuple-element.104), channel_id=1, source_target_pairs={{0,2},{2,0},{4,6},{6,4},{8,10},{10,8},{12,14},{14,12},{16,18},{18,... | collective-permute-start | bytes 1572872 | tf_op jit(solution)/shard_map/ppermute | solution.py:272
  4.2 1.1 %copy-start = (bf16[192,2048]{1,0:T(8,128)(2,1)S(1)}, bf16[192,2048]{1,0:T(8,128)(2,1)}, u32[]{:S(2)}) copy-start(bf16[192,2048]{1,0:T(8,128)(2,1)} %get-tuple-element.179.v_ref.refs_9_.refs_6_) | copy-start | bytes 2359300
  5.3 1.1 %copy-start.2 = (bf16[192,2048]{1,0:T(8,128)(2,1)S(1)}, bf16[192,2048]{1,0:T(8,128)(2,1)}, u32[]{:S(2)}) copy-start(bf16[192,2048]{1,0:T(8,128)(2,1)} %get-tuple-element.124.k_ref.refs_5_) | copy-start | bytes 2359300
  6.4 4.7 %copy-start.3 = (bf16[192,2048]{1,0:T(8,128)(2,1)S(1)}, bf16[192,2048]{1,0:T(8,128)(2,1)}, u32[]{:S(2)}) copy-start(bf16[192,2048]{1,0:T(8,128)(2,1)} %get-tuple-element.124.k_ref.refs_5_) | copy-start | bytes 2359300
  6.4 4.7 %copy-start.4 = (bf16[192,2048]{1,0:T(8,128)(2,1)S(1)}, bf16[192,2048]{1,0:T(8,128)(2,1)}, u32[]{:S(2)}) copy-start(bf16[192,2048]{1,0:T(8,128)(2,1)} %refs_8_.1) | copy-start | bytes 2359300
  6.4 4.7 %copy-start.5 = (bf16[192,2048]{1,0:T(8,128)(2,1)S(1)}, bf16[192,2048]{1,0:T(8,128)(2,1)}, u32[]{:S(2)}) copy-start(bf16[192,2048]{1,0:T(8,128)(2,1)} %refs_10_.1) | copy-start | bytes 2359300
  6.9 4.3 %copy-start.1 = (bf16[192,2048]{1,0:T(8,128)(2,1)S(1)}, bf16[192,2048]{1,0:T(8,128)(2,1)}, u32[]{:S(2)}) copy-start(bf16[192,2048]{1,0:T(8,128)(2,1)} %get-tuple-element.179.v_ref.refs_9_.refs_6_) | copy-start | bytes 2359300
  7.0 6.7 %collective-permute-start.1 = (f32[256,128]{1,0:T(8,128)S(1)}, f32[256,128]{1,0:T(8,128)S(1)}, u32[]{:S(2)}, u32[]{:S(2)}) collective-permute-start(f32[256,128]{1,0:T(8,128)S(1)} %get-tuple-element.106), channel_id=1, source_target_pairs={{0,4},{2,6},{4,0},{6,2},{8,12},{10,14},{12,8},{14,10},{16,20},{18,... | collective-permute-start | bytes 393224 | tf_op jit(solution)/shard_map/ppermute | solution.py:272
  9.6 6.3 %collective-permute-start.2 = (f32[256,128]{1,0:T(8,128)S(1)}, f32[256,128]{1,0:T(8,128)S(1)}, u32[]{:S(2)}, u32[]{:S(2)}) collective-permute-start(f32[256,128]{1,0:T(8,128)S(1)} %get-tuple-element.107), channel_id=1, source_target_pairs={{0,8},{2,10},{4,12},{6,14},{8,0},{10,2},{12,4},{14,6},{16,24},{18,... | collective-permute-start | bytes 393224 | tf_op jit(solution)/shard_map/ppermute | solution.py:272
  11.2 6.6 %collective-permute-start.3 = (f32[256,128]{1,0:T(8,128)S(1)}, f32[256,128]{1,0:T(8,128)S(1)}, u32[]{:S(2)}, u32[]{:S(2)}) collective-permute-start(f32[256,128]{1,0:T(8,128)S(1)} %get-tuple-element.108), channel_id=1, source_target_pairs={{0,12},{2,14},{4,8},{6,10},{8,4},{10,6},{12,0},{14,2},{16,28},{18,... | collective-permute-start | bytes 393224 | tf_op jit(solution)/shard_map/ppermute | solution.py:272
  11.2 25.3 %collective-permute-start.12 = (f32[1024,128]{1,0:T(8,128)S(1)}, f32[1024,128]{1,0:T(8,128)S(1)}, u32[]{:S(2)}, u32[]{:S(2)}) collective-permute-start(f32[1024,128]{1,0:T(8,128)S(1)} %shard_map.85.keep_ref), channel_id=1, source_target_pairs={{0,2},{2,0},{4,6},{6,4},{8,10},{10,8},{12,14},{14,12},{16,18},{18,... | collective-permute-start | bytes 1572872 | tf_op jit(solution)/shard_map/ppermute | solution.py:272
  17.8 8.9 %collective-permute-start.4 = (f32[256,128]{1,0:T(8,128)S(1)}, f32[256,128]{1,0:T(8,128)S(1)}, u32[]{:S(2)}, u32[]{:S(2)}) collective-permute-start(f32[256,128]{1,0:T(8,128)S(1)} %add_add_fusion.1), channel_id=1, source_target_pairs={{0,16},{2,18},{4,20},{6,22},{8,24},{10,26},{12,28},{14,30},{16,0},... | collective-permute-start | bytes 393224 | tf_op jit(solution)/shard_map/ppermute | solution.py:272
  26.8 5.3 %collective-permute-start.5 = (f32[256,128]{1,0:T(8,128)S(1)}, f32[256,128]{1,0:T(8,128)S(1)}, u32[]{:S(2)}, u32[]{:S(2)}) collective-permute-start(f32[256,128]{1,0:T(8,128)S(1)} %get-tuple-element.135), channel_id=1, source_target_pairs={{0,4},{2,6},{4,0},{6,2},{8,12},{10,14},{12,8},{14,10},{16,20},{18,... | collective-permute-start | bytes 393224 | tf_op jit(solution)/shard_map/ppermute | solution.py:272
  28.2 5.5 %collective-permute-start.6 = (f32[256,128]{1,0:T(8,128)S(1)}, f32[256,128]{1,0:T(8,128)S(1)}, u32[]{:S(2)}, u32[]{:S(2)}) collective-permute-start(f32[256,128]{1,0:T(8,128)S(1)} %get-tuple-element.136), channel_id=1, source_target_pairs={{0,8},{2,10},{4,12},{6,14},{8,0},{10,2},{12,4},{14,6},{16,24},{18,... | collective-permute-start | bytes 393224 | tf_op jit(solution)/shard_map/ppermute | solution.py:272
  28.9 7.1 %collective-permute-start.7 = (f32[256,128]{1,0:T(8,128)S(1)}, f32[256,128]{1,0:T(8,128)S(1)}, u32[]{:S(2)}, u32[]{:S(2)}) collective-permute-start(f32[256,128]{1,0:T(8,128)S(1)} %get-tuple-element.137), channel_id=1, source_target_pairs={{0,12},{2,14},{4,8},{6,10},{8,4},{10,6},{12,0},{14,2},{16,28},{18,... | collective-permute-start | bytes 393224 | tf_op jit(solution)/shard_map/ppermute | solution.py:272
  30.4 6.0 %collective-permute-start.8 = (f32[256,128]{1,0:T(8,128)S(1)}, f32[256,128]{1,0:T(8,128)S(1)}, u32[]{:S(2)}, u32[]{:S(2)}) collective-permute-start(f32[256,128]{1,0:T(8,128)S(1)} %get-tuple-element.134.refs_0_), channel_id=1, source_target_pairs={{0,2},{2,0},{4,6},{6,4},{8,10},{10,8},{12,14},{14,12},{16,18},{18,... | collective-permute-start | bytes 393224 | tf_op jit(solution)/shard_map/ppermute | solution.py:272
  32.1 4.3 %collective-permute-start.9 = (f32[256,128]{1,0:T(8,128)S(1)}, f32[256,128]{1,0:T(8,128)S(1)}, u32[]{:S(2)}, u32[]{:S(2)}) collective-permute-start(f32[256,128]{1,0:T(8,128)S(1)} %collective-permute-done.5.refs_1_), channel_id=1, source_target_pairs={{0,2},{2,0},{4,6},{6,4},{8,10},{10,8},{12,14},{14,12},{16,18},{18,... | collective-permute-start | bytes 393224 | tf_op jit(solution)/shard_map/ppermute | solution.py:272
  33.8 2.7 %collective-permute-start.10 = (f32[256,128]{1,0:T(8,128)S(1)}, f32[256,128]{1,0:T(8,128)S(1)}, u32[]{:S(2)}, u32[]{:S(2)}) collective-permute-start(f32[256,128]{1,0:T(8,128)S(1)} %collective-permute-done.6.refs_2_), channel_id=1, source_target_pairs={{0,2},{2,0},{4,6},{6,4},{8,10},{10,8},{12,14},{14,12},{16,18},{18,... | collective-permute-start | bytes 393224 | tf_op jit(solution)/shard_map/ppermute | solution.py:272
  36.0 1.3 %collective-permute-start.11 = (f32[256,128]{1,0:T(8,128)S(1)}, f32[256,128]{1,0:T(8,128)S(1)}, u32[]{:S(2)}, u32[]{:S(2)}) collective-permute-start(f32[256,128]{1,0:T(8,128)S(1)} %collective-permute-done.7.refs_3_), channel_id=1, source_target_pairs={{0,2},{2,0},{4,6},{6,4},{8,10},{10,8},{12,14},{14,12},{16,18},{18,... | collective-permute-start | bytes 393224 | tf_op jit(solution)/shard_map/ppermute | solution.py:272
  38.1 3.7 %collective-permute-start.13 = (f32[8,192]{1,0:T(8,128)S(1)}, f32[8,192]{1,0:T(8,128)S(1)}, u32[]{:S(2)}, u32[]{:S(2)}) collective-permute-start(f32[8,192]{1,0:T(8,128)S(1)} %get-tuple-element.142.a_ref), channel_id=1, source_target_pairs={{0,1},{1,0},{2,3},{3,2},{4,5},{5,4},{6,7},{7,6},{8,9},{9,8},{10,11... | collective-permute-start | bytes 18440 | tf_op jit(solution)/shard_map/ppermute | solution.py:309
  42.5 2.0 %collective-permute-start.14 = (f32[1024,128]{1,0:T(8,128)S(1)}, f32[1024,128]{1,0:T(8,128)S(1)}, u32[]{:S(2)}, u32[]{:S(2)}) collective-permute-start(f32[1024,128]{1,0:T(8,128)S(1)} %get-tuple-element.149), channel_id=1, source_target_pairs={{0,2},{2,0},{4,6},{6,4},{8,10},{10,8},{12,14},{14,12},{16,18},{18,... | collective-permute-start | bytes 1572872 | tf_op jit(solution)/shard_map/ppermute | solution.py:272
  44.6 6.8 %collective-permute-start.15 = (f32[256,128]{1,0:T(8,128)S(1)}, f32[256,128]{1,0:T(8,128)S(1)}, u32[]{:S(2)}, u32[]{:S(2)}) collective-permute-start(f32[256,128]{1,0:T(8,128)S(1)} %get-tuple-element.151), channel_id=1, source_target_pairs={{0,4},{2,6},{4,0},{6,2},{8,12},{10,14},{12,8},{14,10},{16,20},{18,... | collective-permute-start | bytes 393224 | tf_op jit(solution)/shard_map/ppermute | solution.py:272
  45.2 6.4 %collective-permute-start.16 = (f32[256,128]{1,0:T(8,128)S(1)}, f32[256,128]{1,0:T(8,128)S(1)}, u32[]{:S(2)}, u32[]{:S(2)}) collective-permute-start(f32[256,128]{1,0:T(8,128)S(1)} %get-tuple-element.152), channel_id=1, source_target_pairs={{0,8},{2,10},{4,12},{6,14},{8,0},{10,2},{12,4},{14,6},{16,24},{18,... | collective-permute-start | bytes 393224 | tf_op jit(solution)/shard_map/ppermute | solution.py:272
  46.9 7.3 %collective-permute-start.17 = (f32[256,128]{1,0:T(8,128)S(1)}, f32[256,128]{1,0:T(8,128)S(1)}, u32[]{:S(2)}, u32[]{:S(2)}) collective-permute-start(f32[256,128]{1,0:T(8,128)S(1)} %get-tuple-element.153), channel_id=1, source_target_pairs={{0,12},{2,14},{4,8},{6,10},{8,4},{10,6},{12,0},{14,2},{16,28},{18,... | collective-permute-start | bytes 393224 | tf_op jit(solution)/shard_map/ppermute | solution.py:272
  48.1 24.5 %collective-permute-start.26 = (f32[1024,128]{1,0:T(8,128)S(1)}, f32[1024,128]{1,0:T(8,128)S(1)}, u32[]{:S(2)}, u32[]{:S(2)}) collective-permute-start(f32[1024,128]{1,0:T(8,128)S(1)} %get-tuple-element.194.keep_ref), channel_id=1, source_target_pairs={{0,2},{2,0},{4,6},{6,4},{8,10},{10,8},{12,14},{14,12},{16,18},{18,... | collective-permute-start | bytes 1572872 | tf_op jit(solution)/shard_map/ppermute | solution.py:272
  54.2 8.2 %collective-permute-start.18 = (f32[256,128]{1,0:T(8,128)S(1)}, f32[256,128]{1,0:T(8,128)S(1)}, u32[]{:S(2)}, u32[]{:S(2)}) collective-permute-start(f32[256,128]{1,0:T(8,128)S(1)} %add_add_fusion), channel_id=1, source_target_pairs={{0,16},{2,18},{4,20},{6,22},{8,24},{10,26},{12,28},{14,30},{16,0},... | collective-permute-start | bytes 393224 | tf_op jit(solution)/shard_map/ppermute | solution.py:272
  62.5 6.4 %collective-permute-start.20 = (f32[256,128]{1,0:T(8,128)S(1)}, f32[256,128]{1,0:T(8,128)S(1)}, u32[]{:S(2)}, u32[]{:S(2)}) collective-permute-start(f32[256,128]{1,0:T(8,128)S(1)} %get-tuple-element.191), channel_id=1, source_target_pairs={{0,4},{2,6},{4,0},{6,2},{8,12},{10,14},{12,8},{14,10},{16,20},{18,... | collective-permute-start | bytes 393224 | tf_op jit(solution)/shard_map/ppermute | solution.py:272
  63.8 5.4 %collective-permute-start.22 = (f32[256,128]{1,0:T(8,128)S(1)}, f32[256,128]{1,0:T(8,128)S(1)}, u32[]{:S(2)}, u32[]{:S(2)}) collective-permute-start(f32[256,128]{1,0:T(8,128)S(1)} %get-tuple-element.192), channel_id=1, source_target_pairs={{0,8},{2,10},{4,12},{6,14},{8,0},{10,2},{12,4},{14,6},{16,24},{18,... | collective-permute-start | bytes 393224 | tf_op jit(solution)/shard_map/ppermute | solution.py:272
  64.5 6.5 %collective-permute-start.24 = (f32[256,128]{1,0:T(8,128)S(1)}, f32[256,128]{1,0:T(8,128)S(1)}, u32[]{:S(2)}, u32[]{:S(2)}) collective-permute-start(f32[256,128]{1,0:T(8,128)S(1)} %get-tuple-element.193), channel_id=1, source_target_pairs={{0,12},{2,14},{4,8},{6,10},{8,4},{10,6},{12,0},{14,2},{16,28},{18,... | collective-permute-start | bytes 393224 | tf_op jit(solution)/shard_map/ppermute | solution.py:272
  66.0 6.5 %collective-permute-start.19 = (f32[256,128]{1,0:T(8,128)S(1)}, f32[256,128]{1,0:T(8,128)S(1)}, u32[]{:S(2)}, u32[]{:S(2)}) collective-permute-start(f32[256,128]{1,0:T(8,128)S(1)} %get-tuple-element.190.refs_0_), channel_id=1, source_target_pairs={{0,2},{2,0},{4,6},{6,4},{8,10},{10,8},{12,14},{14,12},{16,18},{18,... | collective-permute-start | bytes 393224 | tf_op jit(solution)/shard_map/ppermute | solution.py:272
  68.9 3.7 %collective-permute-start.21 = (f32[256,128]{1,0:T(8,128)S(1)}, f32[256,128]{1,0:T(8,128)S(1)}, u32[]{:S(2)}, u32[]{:S(2)}) collective-permute-start(f32[256,128]{1,0:T(8,128)S(1)} %collective-permute-done.20.refs_1_), channel_id=1, source_target_pairs={{0,2},{2,0},{4,6},{6,4},{8,10},{10,8},{12,14},{14,12},{16,18},{18,... | collective-permute-start | bytes 393224 | tf_op jit(solution)/shard_map/ppermute | solution.py:272
  69.2 3.4 %collective-permute-start.23 = (f32[256,128]{1,0:T(8,128)S(1)}, f32[256,128]{1,0:T(8,128)S(1)}, u32[]{:S(2)}, u32[]{:S(2)}) collective-permute-start(f32[256,128]{1,0:T(8,128)S(1)} %collective-permute-done.22.refs_2_), channel_id=1, source_target_pairs={{0,2},{2,0},{4,6},{6,4},{8,10},{10,8},{12,14},{14,12},{16,18},{18,... | collective-permute-start | bytes 393224 | tf_op jit(solution)/shard_map/ppermute | solution.py:272
  71.0 1.6 %collective-permute-start.25 = (f32[256,128]{1,0:T(8,128)S(1)}, f32[256,128]{1,0:T(8,128)S(1)}, u32[]{:S(2)}, u32[]{:S(2)}) collective-permute-start(f32[256,128]{1,0:T(8,128)S(1)} %collective-permute-done.24.refs_3_), channel_id=1, source_target_pairs={{0,2},{2,0},{4,6},{6,4},{8,10},{10,8},{12,14},{14,12},{16,18},{18,... | collective-permute-start | bytes 393224 | tf_op jit(solution)/shard_map/ppermute | solution.py:272

commit v3 on v2

--- a/solution.py
+++ b/solution.py
@@ -11,32 +11,50 @@
 DH = 128
 EPSILON = 1e-06
 QUAD = 4
+GATHER = ((0,1,2,3),(0,2,1,3))
+HAND = ((0,1,2,3),(0,3,2,1))
 CHUNKS = 1
+BATCH = 4
 F32 = jnp.float32
 BF16 = jnp.bfloat16
-EXACT = lax.Precision.HIGHEST
 SMALL = 16 * 1024 * 1024
 LARGE = 60 * 1024 * 1024
 ANY = pl.BlockSpec(memory_space=pl.ANY)
 VMEM = pl.BlockSpec(memory_space=pltpu.VMEM)
 
 
-def dot(a, b, ca, cb, precision=None):
-    return lax.dot_general(
-        a, b, (((ca,), (cb,)), ((), ())), precision=precision, preferred_element_type=F32
-    )
+def dot(a, b, ca, cb):
+    return lax.dot_general(a, b, (((ca,), (cb,)), ((), ())), preferred_element_type=F32)
 
 
 def sigmoid(x):
     return 0.5 + 0.5 * jnp.tanh(0.5 * x)
 
 
+def thirds(x):
+    first = x.astype(BF16)
+    rest = x - first.astype(F32)
+    second = rest.astype(BF16)
+    return [first, second, (rest - second.astype(F32)).astype(BF16)]
+
+
+def chooser(rows, width):
+    line = lax.broadcasted_iota(jnp.int32, (rows, width), 0)
+    column = lax.broadcasted_iota(jnp.int32, (rows, width), 1)
+    return jnp.where(line == column // DH, 1.0, 0.0).astype(BF16)
+
+
 def core_of():
     return lax.rem(lax.axis_index("ctx"), 2)
 
 
 def chip_of():
     return lax.rem(lax.axis_index("ctx") // 2, QUAD)
+
+
+def mate(orders, n, other=0):
+    first, second = orders[0][n], orders[1][n]
+    return first + (core_of() ^ other) * (second - first)
 
 
 def head(g):
@@ -55,6 +73,7 @@
         self.heads = width // DH
         self.group = self.heads // (2 * CHUNKS)
         self.span = self.group * DH
+        self.batch = BATCH if self.group % BATCH == 0 else 1
         self.part = self.span // QUAD
         self.tall = jax.ShapeDtypeStruct((self.span, DH), F32)
         self.piece = jax.ShapeDtypeStruct((self.part, DH), F32)
@@ -143,23 +162,27 @@
         gated_ref[:, head(g)] = cot_ref[:, at].astype(F32) * sigmoid(gate_ref[:, at].astype(F32))
 
 
-def place_state(plan, reverse, pieces, add_ref, state_ref):
+def place_state(plan, reverse, side, pieces, add_ref, state_ref):
     add = core_of() == (0 if reverse else 1)
     chip = chip_of()
     for k in range(QUAD):
-        here = pl.ds(pl.multiple_of((chip ^ k) * plan.part, plan.part), plan.part)
-        state_ref[here, :] = (pieces[k][...] + jnp.where(add, add_ref[here, :], 0.0)).astype(BF16)
-
-
-def attend_kernel(plan, first, last, *refs):
-    pieces, add_ref = refs[:4], refs[4]
-    lq_ref, local_ref, gated_ref = refs[5:8]
-    refs = refs[8:]
+        here = pl.ds(pl.multiple_of((chip ^ mate(HAND, k, 1 - side)) * plan.part, plan.part), plan.part)
+        piece = pieces[k][...]
+        for more in add_ref:
+            piece = piece + jnp.where(add, more[here, :], 0.0)
+        state_ref[here, :] = piece.astype(BF16)
+
+
+def attend_kernel(plan, side, first, last, *refs):
+    pieces, add_ref = refs[:4], refs[4 : 4 + side]
+    refs = refs[4 + side :]
+    lq_ref, local_ref, gated_ref = refs[:3]
+    refs = refs[3:]
     if not first:
         square, inner = refs[0][...], refs[1][...]
         refs = refs[2:]
     state_ref, att_ref = refs[:2]
-    place_state(plan, False, pieces, add_ref, state_ref)
+    place_state(plan, False, side, pieces, add_ref, state_ref)
     for g in range(plan.group):
         att = local_ref[:, head(g)] + dot(lq_ref[:, head(g)], state_ref[head(g), :], 1, 0)
         att_ref[:, head(g)] = att
@@ -168,10 +191,9 @@
         else:
             square, inner = square + att * att, inner + gated_ref[:, head(g)] * att
     if last:
-        line = lax.broadcasted_iota(jnp.int32, (8, DH), 0)
-        refs[2][...] = dot(jnp.where(line == 0, 1.0, 0.0), square, 1, 1, EXACT) + dot(
-            jnp.where(line == 1, 1.0, 0.0), inner, 1, 1, EXACT
-        )
+        pick = chooser(8, 2 * DH)
+        terms = thirds(jnp.concatenate([square, inner], axis=1))
+        refs[2][...] = sum(dot(pick, term, 1, 1) for term in terms)
     else:
         refs[2][...] = square
         refs[3][...] = inner
@@ -180,11 +202,14 @@
 def grad_kernel(plan, first, a_ref, b_ref, att_ref, gated_ref, lq_ref, d_ref, sum_ref, *more):
     if first:
         total = a_ref[...] + b_ref[...]
-        line = lax.broadcasted_iota(jnp.int32, (8, DH), 0)
-        sumsq = dot(total, jnp.where(line == 0, 1.0, 0.0), 0, 0, EXACT)
-        raw = dot(total, jnp.where(line == 1, 1.0, 0.0), 0, 0, EXACT)
+        sumsq, raw = total[0:1, :], total[1:2, :]
         inv = 1.0 / jnp.sqrt(sumsq * (1.0 / (H * DH)) + EPSILON)
         coef = raw * inv * (1.0 / (H * DH)) * inv * inv
+        line = lax.broadcasted_iota(jnp.int32, total.shape, 0)
+        rows = jnp.where(line == 0, inv, jnp.where(line == 1, coef, 0.0))
+        pick = chooser(8, 2 * DH)
+        both = sum(dot(term, pick, 0, 0) for term in thirds(rows))
+        inv, coef = both[:, :DH], both[:, DH:]
         more[0][...] = inv
         more[1][...] = coef
     else:
@@ -229,11 +254,26 @@
         copy.wait()
 
 
-def finish_kernel(plan, where, first, *refs):
-    pieces, add_ref = refs[:4], refs[4]
-    k_ref, v_ref, lk_ref, pk_ref, pv_ref = refs[5:10]
-    gk_hbm, gv_hbm, state_ref, gk, gv, sems = refs[10 if first else 12 :]
-    place_state(plan, True, pieces, add_ref, state_ref)
+def finish_kernel(plan, where, *refs):
+    side = where[1]
+    pieces, add_ref = refs[:4], refs[4 : 4 + side]
+    refs = refs[4 + side :]
+    k_ref, v_ref, lk_ref, pk_ref, pv_ref = refs[:5]
+    if side:
+        gk, gv, state_ref = refs[5:]
+    else:
+        gk_done, gv_done, gk_hbm, gv_hbm, state_ref, gk, gv, sems = refs[5:]
+    copies = []
+
+    def send(pairs, at):
+        for source, target in pairs:
+            copy = pltpu.make_async_copy(source, target.at[:, at], sems.at[len(copies)])
+            copy.start()
+            copies.append(copy)
+
+    if not side:
+        send(((gk_done, gk_hbm), (gv_done, gv_hbm)), plan.columns(where[0], 1))
+    place_state(plan, True, side, pieces, add_ref, state_ref)
     for g in range(plan.group):
         at = plan.columns(*where, g)
         state = state_ref[head(g), :]
@@ -242,14 +282,27 @@
         gv[:, head(g)] = (pv_ref[:, head(g)] + dot(lk_ref[:, head(g)], state, 1, 0)).astype(BF16)
         glk = pk_ref[:, head(g)] + dot(v_ref[:, at], state, 1, 1)
         gk[:, head(g)] = (glk * (sig * (1.0 + k * (1.0 - sig)))).astype(BF16)
-    send_out(plan, where, ((gk, gk_hbm), (gv, gv_hbm)), sems)
+        if not side and (g + 1) % plan.batch == 0:
+            first = g + 1 - plan.batch
+            here = slice(first * DH, (g + 1) * DH)
+            start = pl.multiple_of(plan.start(*where) + first * DH, DH)
+            pairs = ((gk.at[:, here], gk_hbm), (gv.at[:, here], gv_hbm))
+            send(pairs, pl.ds(start, plan.batch * DH))
+    for copy in copies:
+        copy.wait()
 
 
 def split_kernel(plan, keep_ref, got_ref, *outs):
     chip = chip_of()
     for k in range(QUAD):
-        here = pl.ds(pl.multiple_of((chip ^ k) * plan.part, plan.part), plan.part)
+        here = pl.ds(pl.multiple_of((chip ^ mate(GATHER, k)) * plan.part, plan.part), plan.part)
         outs[k][...] = keep_ref[here, :] + got_ref[here, :]
+
+
+def onward_kernel(plan, reverse, k, piece_ref, keep_ref, out_ref):
+    here = pl.ds(pl.multiple_of((chip_of() ^ mate(HAND, k)) * plan.part, plan.part), plan.part)
+    add = core_of() == (1 if reverse else 0)
+    out_ref[...] = piece_ref[...] + jnp.where(add, keep_ref[here, :], 0.0)
 
 
 def before_kernel(reverse, span, *refs):
@@ -262,7 +315,8 @@
     for k in range(QUAD):
         total = start
         for m in range(QUAD):
-            first = (chip ^ m) > (chip ^ k) if reverse else (chip ^ m) < (chip ^ k)
+            here, there = chip ^ mate(GATHER, m), chip ^ mate(HAND, k)
+            first = here > there if reverse else here < there
             total = total + jnp.where(first, parts[m][...], 0.0)
         outs[k][...] = total
 
@@ -272,20 +326,26 @@
     return lax.ppermute(x, "ctx", [(i, i ^ distance) for i in range(count)])
 
 
+def quad_swap(x, slot, orders):
+    count = lax.axis_size("ctx")
+    return lax.ppermute(x, "ctx", [(i, i ^ 2 * orders[i % 2][slot]) for i in range(count)])
+
+
 def gather_sums(plan, keep, near):
     mine = run(functools.partial(split_kernel, plan), [plan.piece] * QUAD, keep, near)
-    return [mine[0]] + [swap(mine[k], 2 * k) for k in range(1, QUAD)]
+    return [mine[0]], [quad_swap(mine[k], k, GATHER) for k in range(1, QUAD)]
 
 
 def across(parts, reverse):
     count = lax.axis_size("ctx")
     total = (parts[0] + parts[1]) + (parts[2] + parts[3])
+    held = total
     base = []
     span = 2 * QUAD
     while True:
         got = swap(total, span)
         if 2 * span >= count:
-            return got, base, span
+            return held, (got, base, span)
         far = lax.rem(lax.axis_index("ctx") // span, 2) == (0 if reverse else 1)
         term = jnp.where(far, got, 0.0)
         base = [base[0] + term] if base else [term]
@@ -301,35 +361,38 @@
         got,
         *base,
     )
-    return [outs[0]] + [swap(outs[k], 2 * k) for k in range(1, QUAD)]
+    return outs, [quad_swap(outs[k], k, HAND) for k in range(1, QUAD)]
+
+
+def carried(plan, sums_of, work, reverse):
+    near = swap(sums_of[0, 0], 1)
+    keep = sums_of[0, 1]
+    own, came = gather_sums(plan, keep, near)
+    results = []
+
+    def meanwhile(thunks, held, values):
+        done = [t(held) for t in thunks]
+        results.extend(done)
+        return after(values, done) if done else values
+
+    parts = own + meanwhile(work[0], own[0], came)
+    held, (got, base, span) = across(parts, reverse)
+    got = meanwhile(work[1], held, got)
+    outs, came = hand_out(plan, parts, got, base, span, reverse)
+    came = meanwhile(work[2], outs[0], came)
+    own = [outs[0]] + came
+    pieces = {(0, 1): own + [near]}
+    pieces[0, 0] = [
+        swap(run(functools.partial(onward_kernel, plan, reverse, k), plan.piece, x, keep), 1)
+        for k, x in enumerate(own)
+    ]
+    return pieces, results
 
 
 def head_total(sums):
     if lax.axis_size("head") == 2:
         return sums, lax.ppermute(sums, "head", [(0, 1), (1, 0)])
     return lax.psum(sums, "head"), jnp.zeros_like(sums)
-
-
-def carried(plan, sums_of, work, reverse):
-    chunks = range(CHUNKS)
-    near = [swap(sums_of[c, 0], 1) for c in chunks]
-    parts = [gather_sums(plan, sums_of[c, 1], near[c]) for c in chunks]
-    far_add = [swap(after(sums_of[c, 1], near[c]), 1) for c in chunks]
-    results = []
-    held = parts[-1][0]
-    done = [t(held) for t in work[0]]
-    results += done
-    parts = [after(p, done) for p in parts]
-    crossed = [across(p, reverse) for p in parts]
-    done = [t(parts[-1][0]) for t in work[1]]
-    results += done
-    crossed = [(after(got, done), base, span) for got, base, span in crossed]
-    pieces = {}
-    for c in chunks:
-        own = hand_out(plan, parts[c], *crossed[c], reverse)
-        pieces[c, 1] = own + [near[c]]
-        pieces[c, 0] = [swap(x, 1) for x in own] + [far_add[c]]
-    return pieces, results
 
 
 def per_device(queries, key_rows, value_rows, gate_rows, cotangent):
@@ -340,11 +403,10 @@
     k, v, first_sum = run(
         functools.partial(first_kernel, plan, groups),
         [plan.given, plan.given, plan.tall],
-        key_rows,
-        value_rows,
+        pltpu.with_memory_space_constraint(key_rows, pltpu.HBM),
+        pltpu.with_memory_space_constraint(value_rows, pltpu.HBM),
         scratch=[pltpu.SemaphoreType.DMA((2 * count,))],
         in_specs=[ANY, ANY],
-        limit=LARGE,
     )
     sums = {groups[0]: first_sum}
     for where in groups[1:]:
@@ -362,14 +424,14 @@
         return thunk
 
     thunks = [local(where) for where in groups]
-    pieces, made = carried(plan, sums, (thunks[: count // 2], thunks[count // 2 :]), False)
+    pieces, made = carried(plan, sums, ([], thunks, []), False)
     made = dict(zip(groups, made))
     lq, lk, weights, inside, gated = ({w: made[w][n] for w in groups} for n in range(5))
     state, attended, running = {}, {}, ()
     for n, where in enumerate(late):
         last = n == count - 1
         state[where], attended[where], *running = run(
-            functools.partial(attend_kernel, plan, n == 0, last),
+            functools.partial(attend_kernel, plan, where[1], n == 0, last),
             [plan.state, plan.full] + ([plan.sums] if last else [plan.wide] * 2),
             *pieces[where],
             lq[where],
@@ -418,26 +480,36 @@
         return thunk
 
     thunks = [inner(where) for where in groups]
-    pieces, made = carried(plan, sums, (thunks[: count // 2], thunks[count // 2 :]), True)
+    pieces, made = carried(plan, sums, ([], thunks[:1], thunks[1:]), True)
     made = dict(zip(groups, made))
-    ends = []
-    for n, where in enumerate(late):
-        ends = run(
-            functools.partial(finish_kernel, plan, where, n == 0),
-            [plan.given, plan.given],
-            *pieces[where],
-            k,
-            v,
-            lk[where],
-            *made[where],
-            *ends,
-            scratch=[pltpu.VMEM((plan.span, DH), BF16)]
-            + [pltpu.VMEM((plan.rows, plan.span), BF16)] * 2
-            + [pltpu.SemaphoreType.DMA((2,))],
-            in_specs=[VMEM] * 10 + [ANY] * len(ends),
-            out_specs=[ANY, ANY],
-            aliases={} if n == 0 else {10: 0, 11: 1},
-        )
+    where = (0, 1)
+    state_scratch = pltpu.VMEM((plan.span, DH), BF16)
+    ends = run(
+        functools.partial(finish_kernel, plan, where),
+        [plan.low, plan.low],
+        *pieces[where],
+        k,
+        v,
+        lk[where],
+        *made[where],
+        scratch=[state_scratch],
+    )
+    where = (0, 0)
+    ends = run(
+        functools.partial(finish_kernel, plan, where),
+        [plan.given, plan.given],
+        *pieces[where],
+        k,
+        v,
+        lk[where],
+        *made[where],
+        *ends,
+        scratch=[state_scratch]
+        + [pltpu.VMEM((plan.rows, plan.span), BF16)] * 2
+        + [pltpu.SemaphoreType.DMA((2 + 2 * plan.group // plan.batch,))],
+        in_specs=[VMEM] * 11,
+        out_specs=[ANY, ANY],
+    )
     return (outer[0], ends[0], ends[1], outer[1])
 
 

time: 74.4 us -> 68.9 us (0.926)
  waiting for transfers between devices: 30.5 us -> 28.1 us
  local copies, waits for them, and re-layouts: 2.29 us -> 0.02 us
  Pallas kernels: 17.9 us -> 15.7 us
  starting transfers between devices: 22.5 us -> 23.8 us
    ppermute x26 -> x12, waiting for transfers between devices: 28.3 us -> 9.34 us  [swap(): return lax.ppermute(x, 'ctx', [(i, i ^ distance) for i in range(count)])]
    ppermute x0 -> x12, waiting for transfers between devices: none -> 16.6 us  [quad_swap(): lax.ppermute(x, 'ctx', [(i, i ^ 2 * orders[i % 2][slot]) for i in range(c...]
    ppermute x0 -> x12, starting transfers between devices: none -> 15.3 us  [quad_swap(): lax.ppermute(x, 'ctx', [(i, i ^ 2 * orders[i % 2][slot]) for i in range(c...]
    ppermute x26 -> x12, starting transfers between devices: 21 us -> 6.92 us  [swap(): return lax.ppermute(x, 'ctx', [(i, i ^ distance) for i in range(count)])]
    unnamed x14 -> x6, local copies, waits for them, and re-layouts: 2.29 us -> 0.02 us
    pallas_call x16 -> x24, Pallas kernels: 17.9 us -> 15.7 us  [run(): pl.pallas_call(kernel, out_shape=out_shape, scratch_shapes=list(scratch),...]
  transfers between devices with their start and end apart: 27 -> 25, of which waited for: 16 -> 18; matrix products, arithmetic and copies ran while one was open for 0% -> 0% of each run, Pallas kernels for 16% -> 16%
where the time goes in v3:
time: 68.9 us; the launch traced here: 68.5 us
  waiting for transfers between devices  28.1 us (41%)
  starting transfers between devices  23.8 us (35%)
  Pallas kernels  15.7 us (23%)
  between operations  0.9 us (1%)
    ppermute x12, waiting for transfers between devices, quad_swap(): lax.ppermute(x, 'ctx', [(i, i ^ 2 * orders[i % 2][slot]) for i in range(c...  16.6 us
    pallas_call x24, Pallas kernels, run(): pl.pallas_call(kernel, out_shape=out_shape, scratch_shapes=list(scratch),...  15.7 us
    ppermute x12, starting transfers between devices, quad_swap(): lax.ppermute(x, 'ctx', [(i, i ^ 2 * orders[i % 2][slot]) for i in range(c...  15.3 us
    ppermute x12, waiting for transfers between devices, swap(): return lax.ppermute(x, 'ctx', [(i, i ^ distance) for i in range(count)])  9.34 us
    ppermute x12, starting transfers between devices, swap(): return lax.ppermute(x, 'ctx', [(i, i ^ distance) for i in range(count)])  6.92 us
    ppermute x1, waiting for transfers between devices, head_total(): return (sums, lax.ppermute(sums, 'head', [(0, 1), (1, 0)]))  2.13 us
    ppermute x1, starting transfers between devices, head_total(): return (sums, lax.ppermute(sums, 'head', [(0, 1), (1, 0)]))  1.6 us
  transfers between devices with their start and end apart: 25, of which 18 were waited for; matrix products, arithmetic and copies ran while one was open for 0% of the time, Pallas kernels for 16%

profile of v3, /device:TPU:0, one launch (start us, length us, event | category | flops | bytes accessed | tf_op | source)
XLA Modules:
  0.0 68.5 jit_solution(5812279019729399685)
XLA Ops:
  0.6 1.6 %shard_map.84 = (bf16[192,2048]{1,0:T(8,128)(2,1)S(1)}, bf16[192,2048]{1,0:T(8,128)(2,1)S(1)}, f32[1024,128]{1,0:T(8,128)S(1)}) custom-call(bf16[192,2048]{1,0:T(8,128)(2,1)} %k_hbm.1, bf16[192,2048]{1,0:T(8,128)(2,1)} %v_hbm.1), custom_call_target="tpu_custom_call" | custom-call | tf_op jit(solution)/shard_map/pallas_call | solution.py:107
  2.3 0.5 collective-permute-start
  2.8 0.5 shard_map.85.keep_ref
  3.2 0.0 copy-start
  3.3 0.0 copy-start.1
  3.3 1.1 %collective-permute-done.got_ref.refs_4_ = f32[1024,128]{1,0:T(8,128)S(1)} collective-permute-done((f32[1024,128]{1,0:T(8,128)S(1)}, f32[1024,128]{1,0:T(8,128)S(1)}, u32[]{:S(2)}, u32[]{:S(2)}) %collective-permute-start) | collective-permute-done | bytes 524320 | tf_op jit(solution)/shard_map/ppermute | solution.py:326
  4.3 0.1 shard_map.86
  4.4 2.9 %collective-permute-start.1 = (f32[256,128]{1,0:T(8,128)S(1)}, f32[256,128]{1,0:T(8,128)S(1)}, u32[]{:S(2)}, u32[]{:S(2)}) collective-permute-start(f32[256,128]{1,0:T(8,128)S(1)} %get-tuple-element.94), channel_id=1, source_target_pairs={{0,4},{2,10},{4,0},{6,14},{8,12},{10,2},{12,8},{14,6},{16,20},{18,... | collective-permute-start | bytes 393224 | tf_op jit(solution)/shard_map/ppermute | solution.py:331
  7.3 1.6 %collective-permute-start.2 = (f32[256,128]{1,0:T(8,128)S(1)}, f32[256,128]{1,0:T(8,128)S(1)}, u32[]{:S(2)}, u32[]{:S(2)}) collective-permute-start(f32[256,128]{1,0:T(8,128)S(1)} %get-tuple-element.95), channel_id=1, source_target_pairs={{0,8},{2,6},{4,12},{6,2},{8,0},{10,14},{12,4},{14,10},{16,24},{18,... | collective-permute-start | bytes 393224 | tf_op jit(solution)/shard_map/ppermute | solution.py:331
  8.9 0.0 collective-permute-start.3
  8.9 2.2 %collective-permute-done.1.refs_1_ = f32[256,128]{1,0:T(8,128)S(1)} collective-permute-done((f32[256,128]{1,0:T(8,128)S(1)}, f32[256,128]{1,0:T(8,128)S(1)}, u32[]{:S(2)}, u32[]{:S(2)}) %collective-permute-start.1) | collective-permute-done | bytes 131104 | tf_op jit(solution)/shard_map/ppermute | solution.py:331
  11.1 2.4 %collective-permute-done.2.refs_2_ = f32[256,128]{1,0:T(8,128)S(1)} collective-permute-done((f32[256,128]{1,0:T(8,128)S(1)}, f32[256,128]{1,0:T(8,128)S(1)}, u32[]{:S(2)}, u32[]{:S(2)}) %collective-permute-start.2) | collective-permute-done | bytes 131104 | tf_op jit(solution)/shard_map/ppermute | solution.py:331
  13.5 1.6 %collective-permute-done.3.refs_3_ = f32[256,128]{1,0:T(8,128)S(1)} collective-permute-done((f32[256,128]{1,0:T(8,128)S(1)}, f32[256,128]{1,0:T(8,128)S(1)}, u32[]{:S(2)}, u32[]{:S(2)}) %collective-permute-start.3) | collective-permute-done | bytes 131104 | tf_op jit(solution)/shard_map/ppermute | solution.py:331
  15.1 2.7 %collective-permute-start.4 = (f32[256,128]{1,0:T(8,128)S(1)}, f32[256,128]{1,0:T(8,128)S(1)}, u32[]{:S(2)}, u32[]{:S(2)}) collective-permute-start(f32[256,128]{1,0:T(8,128)S(1)} %add_add_fusion.1), channel_id=1, source_target_pairs={{0,16},{2,18},{4,20},{6,22},{8,24},{10,26},{12,28},{14,30},{16,0},... | collective-permute-start | bytes 393224 | tf_op jit(solution)/shard_map/ppermute | solution.py:326
  17.8 1.1 %shard_map.88 = (bf16[192,1024]{1,0:T(8,128)(2,1)S(1)}, bf16[192,1024]{1,0:T(8,128)(2,1)S(1)}, bf16[8,192,192]{2,1,0:T(8,128)(2,1)S(1)}, f32[192,1024]{1,0:T(8,128)S(1)}, f32[192,1024]{1,0:T(8,128)S(1)}) custom-call(bf16[192,2048]{1,0:T(8,128)(2,1)S(1)} %copy-done, bf16[192,2048]{1,0:T(8,128)(2,1)S(1)} %get-tuple-element.98.k_ref.refs_5_.refs_4_, ...), custom_call_target="tpu_custom_call" | custom-call | tf_op jit(solution)/shard_map/pallas_call | solution.py:107
  18.9 1.1 %shard_map.87 = (bf16[192,1024]{1,0:T(8,128)(2,1)S(1)}, bf16[192,1024]{1,0:T(8,128)(2,1)S(1)}, bf16[8,192,192]{2,1,0:T(8,128)(2,1)S(1)}, f32[192,1024]{1,0:T(8,128)S(1)}, f32[192,1024]{1,0:T(8,128)S(1)}) custom-call(bf16[192,2048]{1,0:T(8,128)(2,1)S(1)} %copy-done, bf16[192,2048]{1,0:T(8,128)(2,1)S(1)} %get-tuple-element.98.k_ref.refs_5_.refs_4_, ...), custom_call_target="tpu_custom_call" | custom-call | tf_op jit(solution)/shard_map/pallas_call | solution.py:107
  20.1 3.2 %collective-permute-done.4.refs_4_ = f32[256,128]{1,0:T(8,128)S(1)} collective-permute-done((f32[256,128]{1,0:T(8,128)S(1)}, f32[256,128]{1,0:T(8,128)S(1)}, u32[]{:S(2)}, u32[]{:S(2)}) %collective-permute-start.4) | collective-permute-done | bytes 131104 | tf_op jit(solution)/shard_map/ppermute | solution.py:326
  23.3 0.1 shard_map.89
  23.4 0.9 %collective-permute-start.5 = (f32[256,128]{1,0:T(8,128)S(1)}, f32[256,128]{1,0:T(8,128)S(1)}, u32[]{:S(2)}, u32[]{:S(2)}) collective-permute-start(f32[256,128]{1,0:T(8,128)S(1)} %get-tuple-element.114), channel_id=1, source_target_pairs={{0,4},{2,14},{4,0},{6,10},{8,12},{10,6},{12,8},{14,2},{16,20},{18,... | collective-permute-start | bytes 393224 | tf_op jit(solution)/shard_map/ppermute | solution.py:331
  24.3 0.0 collective-permute-start.6
  24.4 2.6 %collective-permute-start.7 = (f32[256,128]{1,0:T(8,128)S(1)}, f32[256,128]{1,0:T(8,128)S(1)}, u32[]{:S(2)}, u32[]{:S(2)}) collective-permute-start(f32[256,128]{1,0:T(8,128)S(1)} %get-tuple-element.116), channel_id=1, source_target_pairs={{0,12},{2,6},{4,8},{6,2},{8,4},{10,14},{12,0},{14,10},{16,28},{18,... | collective-permute-start | bytes 393224 | tf_op jit(solution)/shard_map/ppermute | solution.py:331
  27.0 0.1 collective-permute-start.8
  27.1 3.6 %collective-permute-done.5.refs_1_.piece_ref = f32[256,128]{1,0:T(8,128)S(1)} collective-permute-done((f32[256,128]{1,0:T(8,128)S(1)}, f32[256,128]{1,0:T(8,128)S(1)}, u32[]{:S(2)}, u32[]{:S(2)}) %collective-permute-start.5) | collective-permute-done | bytes 131104 | tf_op jit(solution)/shard_map/ppermute | solution.py:331
  30.7 0.1 collective-permute-start.9
  30.8 0.0 collective-permute-done.6.refs_2_.piece_ref
  30.8 0.5 collective-permute-start.10
  31.4 0.7 %collective-permute-done.7.refs_3_.piece_ref = f32[256,128]{1,0:T(8,128)S(1)} collective-permute-done((f32[256,128]{1,0:T(8,128)S(1)}, f32[256,128]{1,0:T(8,128)S(1)}, u32[]{:S(2)}, u32[]{:S(2)}) %collective-permute-start.7) | collective-permute-done | bytes 131104 | tf_op jit(solution)/shard_map/ppermute | solution.py:331
  32.1 0.1 collective-permute-start.11
  32.2 0.4 shard_map.90
  32.6 0.0 collective-permute-done.8.refs_0_
  32.6 0.0 collective-permute-done.9.refs_1_
  32.6 0.9 %collective-permute-done.11.refs_3_ = f32[256,128]{1,0:T(8,128)S(1)} collective-permute-done((f32[256,128]{1,0:T(8,128)S(1)}, f32[256,128]{1,0:T(8,128)S(1)}, u32[]{:S(2)}, u32[]{:S(2)}) %collective-permute-start.11) | collective-permute-done | bytes 131104 | tf_op jit(solution)/shard_map/ppermute | solution.py:326
  33.5 0.5 shard_map.95
  34.0 1.6 %collective-permute-start.12 = (f32[8,192]{1,0:T(8,128)S(1)}, f32[8,192]{1,0:T(8,128)S(1)}, u32[]{:S(2)}, u32[]{:S(2)}) collective-permute-start(f32[8,192]{1,0:T(8,128)S(1)} %get-tuple-element.120.a_ref), channel_id=1, source_target_pairs={{0,1},{1,0},{2,3},{3,2},{4,5},{5,4},{6,7},{7,6},{8,9},{9,8},{10,11... | collective-permute-start | bytes 18440 | tf_op jit(solution)/shard_map/ppermute | solution.py:394
  35.6 2.1 %collective-permute-done.12.b_ref = f32[8,192]{1,0:T(8,128)S(1)} collective-permute-done((f32[8,192]{1,0:T(8,128)S(1)}, f32[8,192]{1,0:T(8,128)S(1)}, u32[]{:S(2)}, u32[]{:S(2)}) %collective-permute-start.12) | collective-permute-done | bytes 6176 | tf_op jit(solution)/shard_map/ppermute | solution.py:394
  37.8 0.7 %shard_map.96 = (bf16[192,1024]{1,0:T(8,128)(2,1)S(1)}, f32[1024,128]{1,0:T(8,128)S(1)}, f32[192,128]{1,0:T(8,128)S(1)}, f32[192,128]{1,0:T(8,128)S(1)}) custom-call(f32[8,192]{1,0:T(8,128)S(1)} %get-tuple-element.120.a_ref, f32[8,192]{1,0:T(8,128)S(1)} %collective-permute-done.12.b_ref, f32[192,1024]{1,0:T(8,128)S(1)} %get-tuple-element.140.att_ref.refs_6_, ...), custom_call_target="tpu_custom_call" | custom-call | tf_op jit(solution)/shard_map/pallas_call | solution.py:107
  38.5 0.1 collective-permute-start.13
  38.6 0.4 shard_map.97
  39.0 1.5 %collective-permute-done.13.got_ref.refs_4_ = f32[1024,128]{1,0:T(8,128)S(1)} collective-permute-done((f32[1024,128]{1,0:T(8,128)S(1)}, f32[1024,128]{1,0:T(8,128)S(1)}, u32[]{:S(2)}, u32[]{:S(2)}) %collective-permute-start.13) | collective-permute-done | bytes 524320 | tf_op jit(solution)/shard_map/ppermute | solution.py:326
  40.5 0.1 shard_map.98
  40.5 0.2 collective-permute-start.14
  40.7 1.2 %collective-permute-start.15 = (f32[256,128]{1,0:T(8,128)S(1)}, f32[256,128]{1,0:T(8,128)S(1)}, u32[]{:S(2)}, u32[]{:S(2)}) collective-permute-start(f32[256,128]{1,0:T(8,128)S(1)} %get-tuple-element.130), channel_id=1, source_target_pairs={{0,8},{2,6},{4,12},{6,2},{8,0},{10,14},{12,4},{14,10},{16,24},{18,... | collective-permute-start | bytes 393224 | tf_op jit(solution)/shard_map/ppermute | solution.py:331
  41.9 2.2 %collective-permute-start.16 = (f32[256,128]{1,0:T(8,128)S(1)}, f32[256,128]{1,0:T(8,128)S(1)}, u32[]{:S(2)}, u32[]{:S(2)}) collective-permute-start(f32[256,128]{1,0:T(8,128)S(1)} %get-tuple-element.131), channel_id=1, source_target_pairs={{0,12},{2,14},{4,8},{6,10},{8,4},{10,6},{12,0},{14,2},{16,28},{18,... | collective-permute-start | bytes 393224 | tf_op jit(solution)/shard_map/ppermute | solution.py:331
  44.1 3.5 %collective-permute-done.14.refs_1_ = f32[256,128]{1,0:T(8,128)S(1)} collective-permute-done((f32[256,128]{1,0:T(8,128)S(1)}, f32[256,128]{1,0:T(8,128)S(1)}, u32[]{:S(2)}, u32[]{:S(2)}) %collective-permute-start.14) | collective-permute-done | bytes 131104 | tf_op jit(solution)/shard_map/ppermute | solution.py:331
  47.6 1.6 %collective-permute-done.16.refs_3_ = f32[256,128]{1,0:T(8,128)S(1)} collective-permute-done((f32[256,128]{1,0:T(8,128)S(1)}, f32[256,128]{1,0:T(8,128)S(1)}, u32[]{:S(2)}, u32[]{:S(2)}) %collective-permute-start.16) | collective-permute-done | bytes 131104 | tf_op jit(solution)/shard_map/ppermute | solution.py:331
  49.3 2.2 %collective-permute-start.17 = (f32[256,128]{1,0:T(8,128)S(1)}, f32[256,128]{1,0:T(8,128)S(1)}, u32[]{:S(2)}, u32[]{:S(2)}) collective-permute-start(f32[256,128]{1,0:T(8,128)S(1)} %add_add_fusion), channel_id=1, source_target_pairs={{0,16},{2,18},{4,20},{6,22},{8,24},{10,26},{12,28},{14,30},{16,0},... | collective-permute-start | bytes 393224 | tf_op jit(solution)/shard_map/ppermute | solution.py:326
  51.5 3.3 %shard_map.99 = (bf16[192,2048]{1,0:T(8,128)(2,1)}, bf16[192,2048]{1,0:T(8,128)(2,1)}, f32[192,1024]{1,0:T(8,128)S(1)}, f32[192,1024]{1,0:T(8,128)S(1)}) custom-call(bf16[1024,128]{1,0:T(8,128)(2,1)S(1)} %get-tuple-element.134.refs_0_, f32[192,128]{1,0:T(8,128)S(1)} %get-tuple-element.150.a_ref.refs_1_, bf16[8,192,192]{2,1,0:T(8,128)(2,1)S(1)} %get-tuple-element.136.refs_2_, ...), custom_call_target="tpu_custom_call" | custom-call | tf_op jit(solution)/shard_map/pallas_call | solution.py:107
  54.8 2.0 %collective-permute-done.17.refs_4_ = f32[256,128]{1,0:T(8,128)S(1)} collective-permute-done((f32[256,128]{1,0:T(8,128)S(1)}, f32[256,128]{1,0:T(8,128)S(1)}, u32[]{:S(2)}, u32[]{:S(2)}) %collective-permute-start.17) | collective-permute-done | bytes 131104 | tf_op jit(solution)/shard_map/ppermute | solution.py:326
  56.8 0.1 shard_map.100
  56.9 2.1 %collective-permute-start.19 = (f32[256,128]{1,0:T(8,128)S(1)}, f32[256,128]{1,0:T(8,128)S(1)}, u32[]{:S(2)}, u32[]{:S(2)}) collective-permute-start(f32[256,128]{1,0:T(8,128)S(1)} %get-tuple-element.163), channel_id=1, source_target_pairs={{0,4},{2,14},{4,0},{6,10},{8,12},{10,6},{12,8},{14,2},{16,20},{18,... | collective-permute-start | bytes 393224 | tf_op jit(solution)/shard_map/ppermute | solution.py:331
  59.1 1.5 %collective-permute-start.21 = (f32[256,128]{1,0:T(8,128)S(1)}, f32[256,128]{1,0:T(8,128)S(1)}, u32[]{:S(2)}, u32[]{:S(2)}) collective-permute-start(f32[256,128]{1,0:T(8,128)S(1)} %get-tuple-element.165), channel_id=1, source_target_pairs={{0,12},{2,6},{4,8},{6,2},{8,4},{10,14},{12,0},{14,10},{16,28},{18,... | collective-permute-start | bytes 393224 | tf_op jit(solution)/shard_map/ppermute | solution.py:331
  60.6 0.1 collective-permute-start.18
  60.7 3.3 %shard_map.101 = (bf16[192,2048]{1,0:T(8,128)(2,1)}, bf16[192,2048]{1,0:T(8,128)(2,1)}, f32[192,1024]{1,0:T(8,128)S(1)}, f32[192,1024]{1,0:T(8,128)S(1)}) custom-call(bf16[1024,128]{1,0:T(8,128)(2,1)S(1)} %get-tuple-element.149.refs_0_, f32[192,128]{1,0:T(8,128)S(1)} %get-tuple-element.150.a_ref.refs_1_, ...), custom_call_target="tpu_custom_call", output_to_operand_aliasing={{0}: (11, {}), {1}: (12, {})} | custom-call | tf_op jit(solution)/shard_map/pallas_call | solution.py:107
  64.0 0.9 %collective-permute-done.20.piece_ref.refs_2_ = f32[256,128]{1,0:T(8,128)S(1)} collective-permute-done((f32[256,128]{1,0:T(8,128)S(1)}, f32[256,128]{1,0:T(8,128)S(1)}, u32[]{:S(2)}, u32[]{:S(2)}) %collective-permute-start.20) | collective-permute-done | bytes 131104 | tf_op jit(solution)/shard_map/ppermute | solution.py:331
  64.9 0.1 collective-permute-done.21.piece_ref.refs_3_
  65.1 0.1 collective-permute-start.22
  65.2 0.5 collective-permute-start.23
  65.7 0.1 collective-permute-start.24
  65.7 0.6 shard_map.106
  66.4 0.0 collective-permute-done.18.refs_0_
  66.4 0.1 collective-permute-done.22.refs_1_
  66.5 0.2 collective-permute-done.23.refs_2_
  66.7 0.3 collective-permute-done.24.refs_3_
  67.0 1.5 %shard_map.107 = (bf16[192,2048]{1,0:T(8,128)(2,1)}, bf16[192,2048]{1,0:T(8,128)(2,1)}) custom-call(f32[256,128]{1,0:T(8,128)S(1)} %collective-permute-done.18.refs_0_, f32[256,128]{1,0:T(8,128)S(1)} %collective-permute-done.22.refs_1_, f32[256,128]{1,0:T(8,128)S(1)} %collective-permute-done.23.refs_2_, f32[256,128]{1,0:T(8,128)S(1)} %collective-permute-done.24.refs_3_, ...), custom_call_target="tpu_custom_call" | custom-call | tf_op jit(solution)/shard_map/pallas_call | solution.py:107
  (18 shorter events, 0.3 us)
Async XLA Ops:
  2.3 2.1 %collective-permute-start = (f32[1024,128]{1,0:T(8,128)S(1)}, f32[1024,128]{1,0:T(8,128)S(1)}, u32[]{:S(2)}, u32[]{:S(2)}) collective-permute-start(f32[1024,128]{1,0:T(8,128)S(1)} %get-tuple-element.92), channel_id=1, source_target_pairs={{0,2},{2,0},{4,6},{6,4},{8,10},{10,8},{12,14},{14,12},{16,18},{18,... | collective-permute-start | bytes 1572872 | tf_op jit(solution)/shard_map/ppermute | solution.py:326
  2.8 15.0 %copy-start.2 = (bf16[192,2048]{1,0:T(8,128)(2,1)S(1)}, bf16[192,2048]{1,0:T(8,128)(2,1)}, u32[]{:S(2)}) copy-start(bf16[192,2048]{1,0:T(8,128)(2,1)} %cot_ref.1) | copy-start | bytes 2359300
  3.2 14.5 %copy-start = (bf16[192,2048]{1,0:T(8,128)(2,1)S(1)}, bf16[192,2048]{1,0:T(8,128)(2,1)}, u32[]{:S(2)}) copy-start(bf16[192,2048]{1,0:T(8,128)(2,1)} %refs_8_.1) | copy-start | bytes 2359300
  3.3 14.5 %copy-start.1 = (bf16[192,2048]{1,0:T(8,128)(2,1)S(1)}, bf16[192,2048]{1,0:T(8,128)(2,1)}, u32[]{:S(2)}) copy-start(bf16[192,2048]{1,0:T(8,128)(2,1)} %refs_10_.1) | copy-start | bytes 2359300
  4.4 6.7 %collective-permute-start.1 = (f32[256,128]{1,0:T(8,128)S(1)}, f32[256,128]{1,0:T(8,128)S(1)}, u32[]{:S(2)}, u32[]{:S(2)}) collective-permute-start(f32[256,128]{1,0:T(8,128)S(1)} %get-tuple-element.94), channel_id=1, source_target_pairs={{0,4},{2,10},{4,0},{6,14},{8,12},{10,2},{12,8},{14,6},{16,20},{18,... | collective-permute-start | bytes 393224 | tf_op jit(solution)/shard_map/ppermute | solution.py:331
  7.3 6.2 %collective-permute-start.2 = (f32[256,128]{1,0:T(8,128)S(1)}, f32[256,128]{1,0:T(8,128)S(1)}, u32[]{:S(2)}, u32[]{:S(2)}) collective-permute-start(f32[256,128]{1,0:T(8,128)S(1)} %get-tuple-element.95), channel_id=1, source_target_pairs={{0,8},{2,6},{4,12},{6,2},{8,0},{10,14},{12,4},{14,10},{16,24},{18,... | collective-permute-start | bytes 393224 | tf_op jit(solution)/shard_map/ppermute | solution.py:331
  8.9 6.2 %collective-permute-start.3 = (f32[256,128]{1,0:T(8,128)S(1)}, f32[256,128]{1,0:T(8,128)S(1)}, u32[]{:S(2)}, u32[]{:S(2)}) collective-permute-start(f32[256,128]{1,0:T(8,128)S(1)} %get-tuple-element.96), channel_id=1, source_target_pairs={{0,12},{2,14},{4,8},{6,10},{8,4},{10,6},{12,0},{14,2},{16,28},{18,... | collective-permute-start | bytes 393224 | tf_op jit(solution)/shard_map/ppermute | solution.py:331
  15.1 8.2 %collective-permute-start.4 = (f32[256,128]{1,0:T(8,128)S(1)}, f32[256,128]{1,0:T(8,128)S(1)}, u32[]{:S(2)}, u32[]{:S(2)}) collective-permute-start(f32[256,128]{1,0:T(8,128)S(1)} %add_add_fusion.1), channel_id=1, source_target_pairs={{0,16},{2,18},{4,20},{6,22},{8,24},{10,26},{12,28},{14,30},{16,0},... | collective-permute-start | bytes 393224 | tf_op jit(solution)/shard_map/ppermute | solution.py:326
  23.4 7.2 %collective-permute-start.5 = (f32[256,128]{1,0:T(8,128)S(1)}, f32[256,128]{1,0:T(8,128)S(1)}, u32[]{:S(2)}, u32[]{:S(2)}) collective-permute-start(f32[256,128]{1,0:T(8,128)S(1)} %get-tuple-element.114), channel_id=1, source_target_pairs={{0,4},{2,14},{4,0},{6,10},{8,12},{10,6},{12,8},{14,2},{16,20},{18,... | collective-permute-start | bytes 393224 | tf_op jit(solution)/shard_map/ppermute | solution.py:331
  24.3 6.4 %collective-permute-start.6 = (f32[256,128]{1,0:T(8,128)S(1)}, f32[256,128]{1,0:T(8,128)S(1)}, u32[]{:S(2)}, u32[]{:S(2)}) collective-permute-start(f32[256,128]{1,0:T(8,128)S(1)} %get-tuple-element.115), channel_id=1, source_target_pairs={{0,8},{2,10},{4,12},{6,14},{8,0},{10,2},{12,4},{14,6},{16,24},{18,... | collective-permute-start | bytes 393224 | tf_op jit(solution)/shard_map/ppermute | solution.py:331
  24.4 7.7 %collective-permute-start.7 = (f32[256,128]{1,0:T(8,128)S(1)}, f32[256,128]{1,0:T(8,128)S(1)}, u32[]{:S(2)}, u32[]{:S(2)}) collective-permute-start(f32[256,128]{1,0:T(8,128)S(1)} %get-tuple-element.116), channel_id=1, source_target_pairs={{0,12},{2,6},{4,8},{6,2},{8,4},{10,14},{12,0},{14,10},{16,28},{18,... | collective-permute-start | bytes 393224 | tf_op jit(solution)/shard_map/ppermute | solution.py:331
  27.0 5.6 %collective-permute-start.8 = (f32[256,128]{1,0:T(8,128)S(1)}, f32[256,128]{1,0:T(8,128)S(1)}, u32[]{:S(2)}, u32[]{:S(2)}) collective-permute-start(f32[256,128]{1,0:T(8,128)S(1)} %shard_map.91), channel_id=1, source_target_pairs={{0,2},{2,0},{4,6},{6,4},{8,10},{10,8},{12,14},{14,12},{16,18},{18,... | collective-permute-start | bytes 393224 | tf_op jit(solution)/shard_map/ppermute | solution.py:326
  30.7 1.9 %collective-permute-start.9 = (f32[256,128]{1,0:T(8,128)S(1)}, f32[256,128]{1,0:T(8,128)S(1)}, u32[]{:S(2)}, u32[]{:S(2)}) collective-permute-start(f32[256,128]{1,0:T(8,128)S(1)} %shard_map.92), channel_id=1, source_target_pairs={{0,2},{2,0},{4,6},{6,4},{8,10},{10,8},{12,14},{14,12},{16,18},{18,... | collective-permute-start | bytes 393224 | tf_op jit(solution)/shard_map/ppermute | solution.py:326
  30.8 1.8 %collective-permute-start.10 = (f32[256,128]{1,0:T(8,128)S(1)}, f32[256,128]{1,0:T(8,128)S(1)}, u32[]{:S(2)}, u32[]{:S(2)}) collective-permute-start(f32[256,128]{1,0:T(8,128)S(1)} %shard_map.93), channel_id=1, source_target_pairs={{0,2},{2,0},{4,6},{6,4},{8,10},{10,8},{12,14},{14,12},{16,18},{18,... | collective-permute-start | bytes 393224 | tf_op jit(solution)/shard_map/ppermute | solution.py:326
  32.1 1.4 %collective-permute-start.11 = (f32[256,128]{1,0:T(8,128)S(1)}, f32[256,128]{1,0:T(8,128)S(1)}, u32[]{:S(2)}, u32[]{:S(2)}) collective-permute-start(f32[256,128]{1,0:T(8,128)S(1)} %shard_map.94), channel_id=1, source_target_pairs={{0,2},{2,0},{4,6},{6,4},{8,10},{10,8},{12,14},{14,12},{16,18},{18,... | collective-permute-start | bytes 393224 | tf_op jit(solution)/shard_map/ppermute | solution.py:326
  34.0 3.7 %collective-permute-start.12 = (f32[8,192]{1,0:T(8,128)S(1)}, f32[8,192]{1,0:T(8,128)S(1)}, u32[]{:S(2)}, u32[]{:S(2)}) collective-permute-start(f32[8,192]{1,0:T(8,128)S(1)} %get-tuple-element.120.a_ref), channel_id=1, source_target_pairs={{0,1},{1,0},{2,3},{3,2},{4,5},{5,4},{6,7},{7,6},{8,9},{9,8},{10,11... | collective-permute-start | bytes 18440 | tf_op jit(solution)/shard_map/ppermute | solution.py:394
  38.5 2.0 %collective-permute-start.13 = (f32[1024,128]{1,0:T(8,128)S(1)}, f32[1024,128]{1,0:T(8,128)S(1)}, u32[]{:S(2)}, u32[]{:S(2)}) collective-permute-start(f32[1024,128]{1,0:T(8,128)S(1)} %get-tuple-element.127), channel_id=1, source_target_pairs={{0,2},{2,0},{4,6},{6,4},{8,10},{10,8},{12,14},{14,12},{16,18},{18,... | collective-permute-start | bytes 1572872 | tf_op jit(solution)/shard_map/ppermute | solution.py:326
  40.5 7.1 %collective-permute-start.14 = (f32[256,128]{1,0:T(8,128)S(1)}, f32[256,128]{1,0:T(8,128)S(1)}, u32[]{:S(2)}, u32[]{:S(2)}) collective-permute-start(f32[256,128]{1,0:T(8,128)S(1)} %get-tuple-element.129), channel_id=1, source_target_pairs={{0,4},{2,10},{4,0},{6,14},{8,12},{10,2},{12,8},{14,6},{16,20},{18,... | collective-permute-start | bytes 393224 | tf_op jit(solution)/shard_map/ppermute | solution.py:331
  40.7 6.9 %collective-permute-start.15 = (f32[256,128]{1,0:T(8,128)S(1)}, f32[256,128]{1,0:T(8,128)S(1)}, u32[]{:S(2)}, u32[]{:S(2)}) collective-permute-start(f32[256,128]{1,0:T(8,128)S(1)} %get-tuple-element.130), channel_id=1, source_target_pairs={{0,8},{2,6},{4,12},{6,2},{8,0},{10,14},{12,4},{14,10},{16,24},{18,... | collective-permute-start | bytes 393224 | tf_op jit(solution)/shard_map/ppermute | solution.py:331
  41.9 7.3 %collective-permute-start.16 = (f32[256,128]{1,0:T(8,128)S(1)}, f32[256,128]{1,0:T(8,128)S(1)}, u32[]{:S(2)}, u32[]{:S(2)}) collective-permute-start(f32[256,128]{1,0:T(8,128)S(1)} %get-tuple-element.131), channel_id=1, source_target_pairs={{0,12},{2,14},{4,8},{6,10},{8,4},{10,6},{12,0},{14,2},{16,28},{18,... | collective-permute-start | bytes 393224 | tf_op jit(solution)/shard_map/ppermute | solution.py:331
  49.3 7.5 %collective-permute-start.17 = (f32[256,128]{1,0:T(8,128)S(1)}, f32[256,128]{1,0:T(8,128)S(1)}, u32[]{:S(2)}, u32[]{:S(2)}) collective-permute-start(f32[256,128]{1,0:T(8,128)S(1)} %add_add_fusion), channel_id=1, source_target_pairs={{0,16},{2,18},{4,20},{6,22},{8,24},{10,26},{12,28},{14,30},{16,0},... | collective-permute-start | bytes 393224 | tf_op jit(solution)/shard_map/ppermute | solution.py:326
  56.9 7.1 %collective-permute-start.19 = (f32[256,128]{1,0:T(8,128)S(1)}, f32[256,128]{1,0:T(8,128)S(1)}, u32[]{:S(2)}, u32[]{:S(2)}) collective-permute-start(f32[256,128]{1,0:T(8,128)S(1)} %get-tuple-element.163), channel_id=1, source_target_pairs={{0,4},{2,14},{4,0},{6,10},{8,12},{10,6},{12,8},{14,2},{16,20},{18,... | collective-permute-start | bytes 393224 | tf_op jit(solution)/shard_map/ppermute | solution.py:331
  59.0 5.8 %collective-permute-start.20 = (f32[256,128]{1,0:T(8,128)S(1)}, f32[256,128]{1,0:T(8,128)S(1)}, u32[]{:S(2)}, u32[]{:S(2)}) collective-permute-start(f32[256,128]{1,0:T(8,128)S(1)} %get-tuple-element.164), channel_id=1, source_target_pairs={{0,8},{2,10},{4,12},{6,14},{8,0},{10,2},{12,4},{14,6},{16,24},{18,... | collective-permute-start | bytes 393224 | tf_op jit(solution)/shard_map/ppermute | solution.py:331
  59.1 5.9 %collective-permute-start.21 = (f32[256,128]{1,0:T(8,128)S(1)}, f32[256,128]{1,0:T(8,128)S(1)}, u32[]{:S(2)}, u32[]{:S(2)}) collective-permute-start(f32[256,128]{1,0:T(8,128)S(1)} %get-tuple-element.165), channel_id=1, source_target_pairs={{0,12},{2,6},{4,8},{6,2},{8,4},{10,14},{12,0},{14,10},{16,28},{18,... | collective-permute-start | bytes 393224 | tf_op jit(solution)/shard_map/ppermute | solution.py:331
  60.6 5.8 %collective-permute-start.18 = (f32[256,128]{1,0:T(8,128)S(1)}, f32[256,128]{1,0:T(8,128)S(1)}, u32[]{:S(2)}, u32[]{:S(2)}) collective-permute-start(f32[256,128]{1,0:T(8,128)S(1)} %shard_map.102), channel_id=1, source_target_pairs={{0,2},{2,0},{4,6},{6,4},{8,10},{10,8},{12,14},{14,12},{16,18},{18,... | collective-permute-start | bytes 393224 | tf_op jit(solution)/shard_map/ppermute | solution.py:326
  65.1 1.4 %collective-permute-start.22 = (f32[256,128]{1,0:T(8,128)S(1)}, f32[256,128]{1,0:T(8,128)S(1)}, u32[]{:S(2)}, u32[]{:S(2)}) collective-permute-start(f32[256,128]{1,0:T(8,128)S(1)} %shard_map.103), channel_id=1, source_target_pairs={{0,2},{2,0},{4,6},{6,4},{8,10},{10,8},{12,14},{14,12},{16,18},{18,... | collective-permute-start | bytes 393224 | tf_op jit(solution)/shard_map/ppermute | solution.py:326
  65.2 1.5 %collective-permute-start.23 = (f32[256,128]{1,0:T(8,128)S(1)}, f32[256,128]{1,0:T(8,128)S(1)}, u32[]{:S(2)}, u32[]{:S(2)}) collective-permute-start(f32[256,128]{1,0:T(8,128)S(1)} %shard_map.104), channel_id=1, source_target_pairs={{0,2},{2,0},{4,6},{6,4},{8,10},{10,8},{12,14},{14,12},{16,18},{18,... | collective-permute-start | bytes 393224 | tf_op jit(solution)/shard_map/ppermute | solution.py:326
  65.7 1.3 %collective-permute-start.24 = (f32[256,128]{1,0:T(8,128)S(1)}, f32[256,128]{1,0:T(8,128)S(1)}, u32[]{:S(2)}, u32[]{:S(2)}) collective-permute-start(f32[256,128]{1,0:T(8,128)S(1)} %shard_map.105), channel_id=1, source_target_pairs={{0,2},{2,0},{4,6},{6,4},{8,10},{10,8},{12,14},{14,12},{16,18},{18,... | collective-permute-start | bytes 393224 | tf_op jit(solution)/shard_map/ppermute | solution.py:326

commit v4 on v3

--- a/solution.py
+++ b/solution.py
@@ -11,8 +11,9 @@
 DH = 128
 EPSILON = 1e-06
 QUAD = 4
-GATHER = ((0,1,2,3),(0,2,1,3))
-HAND = ((0,1,2,3),(0,3,2,1))
+SECTIONS = ((1, 2), (3, 0))
+GATHER = ((0, 1, 2, 3), (0, 1, 2, 3))
+HAND = ((0, 1, 2, 3), (0, 1, 2, 3))
 CHUNKS = 1
 BATCH = 4
 F32 = jnp.float32
@@ -75,6 +76,8 @@
         self.span = self.group * DH
         self.batch = BATCH if self.group % BATCH == 0 else 1
         self.part = self.span // QUAD
+        self.split = self.part % DH == 0
+        self.block = jax.ShapeDtypeStruct((2 * self.part, DH), F32)
         self.tall = jax.ShapeDtypeStruct((self.span, DH), F32)
         self.piece = jax.ShapeDtypeStruct((self.part, DH), F32)
         self.low = jax.ShapeDtypeStruct((rows, self.span), BF16)
@@ -94,6 +97,15 @@
         if g is None:
             return pl.ds(start, self.span)
         return pl.ds(pl.multiple_of(start + g * DH, DH), DH)
+
+
+    def section(self, n):
+        count = self.part // DH
+        chip = chip_of()
+        return [(chip ^ k) * count + h for k in SECTIONS[n] for h in range(count)]
+
+    def own_part(self, k):
+        return pl.ds(pl.multiple_of((chip_of() ^ k) * self.part, self.part), self.part)
 
 
 def run(kernel, out_shape, *args, scratch=(), in_specs=None, out_specs=None, limit=SMALL, aliases=None):
@@ -127,17 +139,16 @@
             copies.append(copy)
     copies[0].wait()
     copies[1].wait()
-    for g in range(plan.group):
-        at = plan.columns(*order[0], g)
-        out_ref[head(g), :] = key_state(k_ref[:, at].astype(F32), v_ref[:, at])
+    next_kernel(plan, order[0], 0 if plan.split else None, k_ref, v_ref, out_ref)
     for copy in copies[2:]:
         copy.wait()
 
 
-def next_kernel(plan, where, k_ref, v_ref, out_ref):
-    for g in range(plan.group):
+def next_kernel(plan, where, section, k_ref, v_ref, out_ref):
+    heads = range(plan.group) if section is None else plan.section(section)
+    for n, g in enumerate(heads):
         at = plan.columns(*where, g)
-        out_ref[head(g), :] = key_state(k_ref[:, at].astype(F32), v_ref[:, at])
+        out_ref[head(n), :] = key_state(k_ref[:, at].astype(F32), v_ref[:, at])
 
 
 def causal_mask(rows):
@@ -146,36 +157,84 @@
     )
 
 
-def local_kernel(plan, where, q_ref, k_ref, v_ref, gate_ref, cot_ref, lq_ref, lk_ref, w_ref, att_ref, gated_ref):
+def key_part(plan, where, k_ref, lk_ref, slope_ref):
+    for g in range(plan.group):
+        k = k_ref[:, plan.columns(*where, g)].astype(F32)
+        sig = sigmoid(k)
+        lk_ref[:, head(g)] = (k * sig).astype(BF16)
+        slope_ref[:, head(g)] = sig * (1.0 + k * (1.0 - sig))
+
+
+def early_key_kernel(plan, groups, k_ref, *outs):
+    @pl.when(core_of() == 0)
+    def _():
+        for n, where in enumerate(groups):
+            key_part(plan, where, k_ref, *outs[2 * n : 2 * n + 2])
+
+
+def local_kernel(plan, where, q_ref, k_ref, v_ref, gate_ref, cot_ref, *refs):
+    early, keys, (lq_ref, w_ref, att_ref, gated_ref) = refs[:2], refs[2:4], refs[4:]
+
+    @pl.when(core_of() == 0)
+    def _():
+        for made, out in zip(early, keys):
+            out[...] = made[...]
+
+    @pl.when(core_of() == 1)
+    def _():
+        key_part(plan, where, k_ref, *keys)
+
     causal = causal_mask(plan.rows)
     for g in range(plan.group):
         at = plan.columns(*where, g)
         q = q_ref[:, at].astype(F32)
-        k = k_ref[:, at].astype(F32)
         lq = (q * sigmoid(q)).astype(BF16)
-        lk = (k * sigmoid(k)).astype(BF16)
         lq_ref[:, head(g)] = lq
-        lk_ref[:, head(g)] = lk
-        weights = jnp.where(causal, dot(lq, lk, 1, 1), 0.0).astype(BF16)
+        weights = jnp.where(causal, dot(lq, keys[0][:, head(g)], 1, 1), 0.0).astype(BF16)
         w_ref[g] = weights
         att_ref[:, head(g)] = dot(weights, v_ref[:, at], 1, 0)
         gated_ref[:, head(g)] = cot_ref[:, at].astype(F32) * sigmoid(gate_ref[:, at].astype(F32))
 
 
+def gate_part(plan, where, inv_ref, gate_ref, att_ref, gated_ref, out_ref):
+    for g in range(plan.group):
+        gate = sigmoid(gate_ref[:, plan.columns(*where, g)].astype(F32))
+        normed = att_ref[:, head(g)] * inv_ref[...]
+        out_ref[:, head(g)] = (gated_ref[:, head(g)] * normed * (1.0 - gate)).astype(BF16)
+
+
+def early_gate_kernel(plan, groups, inv_ref, gate_ref, *refs):
+    count = len(groups)
+
+    @pl.when(core_of() == 0)
+    def _():
+        for n, where in enumerate(groups):
+            att_ref, gated_ref, out_ref = refs[n::count]
+            gate_part(plan, where, inv_ref, gate_ref, att_ref, gated_ref, out_ref)
+
+
 def place_state(plan, reverse, side, pieces, add_ref, state_ref):
     add = core_of() == (0 if reverse else 1)
-    chip = chip_of()
-    for k in range(QUAD):
-        here = pl.ds(pl.multiple_of((chip ^ mate(HAND, k, 1 - side)) * plan.part, plan.part), plan.part)
-        piece = pieces[k][...]
-        for more in add_ref:
-            piece = piece + jnp.where(add, more[here, :], 0.0)
-        state_ref[here, :] = piece.astype(BF16)
+    for slot in range(QUAD):
+        k = mate(HAND, slot, 1 - side)
+        piece = pieces[slot][...]
+        if add_ref:
+            piece = piece + jnp.where(add, near_part(plan, add_ref, k), 0.0)
+        state_ref[plan.own_part(k), :] = piece.astype(BF16)
+
+
+def near_part(plan, refs, k):
+    if len(refs) == 1:
+        return refs[0][plan.own_part(k), :]
+    place = lax.rem(k + QUAD - 1, QUAD)
+    here = pl.ds(pl.multiple_of(lax.rem(place, 2) * plan.part, plan.part), plan.part)
+    return jnp.where(place < 2, refs[0][here, :], refs[1][here, :])
 
 
 def attend_kernel(plan, side, first, last, *refs):
-    pieces, add_ref = refs[:4], refs[4 : 4 + side]
-    refs = refs[4 + side :]
+    extra = side * (1 + plan.split)
+    pieces, add_ref = refs[:4], refs[4 : 4 + extra]
+    refs = refs[4 + extra :]
     lq_ref, local_ref, gated_ref = refs[:3]
     refs = refs[3:]
     if not first:
@@ -199,6 +258,12 @@
         refs[3][...] = inner
 
 
+def section_kernel(plan, n, lq_ref, d_ref, sum_ref):
+    for place, g in enumerate(plan.section(n)):
+        at = pl.ds(pl.multiple_of(g * DH, DH), DH)
+        sum_ref[head(place), :] = dot(lq_ref[:, at], d_ref[:, at], 0, 0)
+
+
 def grad_kernel(plan, first, a_ref, b_ref, att_ref, gated_ref, lq_ref, d_ref, sum_ref, *more):
     if first:
         total = a_ref[...] + b_ref[...]
@@ -217,13 +282,25 @@
     for g in range(plan.group):
         d = (gated_ref[:, head(g)] * inv - att_ref[:, head(g)] * coef).astype(BF16)
         d_ref[:, head(g)] = d
-        sum_ref[head(g), :] = dot(lq_ref[:, head(g)], d, 0, 0)
+        if not (first and plan.split):
+            sum_ref[head(g), :] = dot(lq_ref[:, head(g)], d, 0, 0)
+    if first and plan.split:
+        section_kernel(plan, 0, lq_ref, d_ref, sum_ref)
 
 
 def inside_kernel(plan, where, first, *refs):
     (state_ref, inv_ref, w_ref, d_ref, lq_ref, lk_ref, att_ref, gated_ref) = refs[:8]
-    q_ref, v_ref, gate_ref = refs[8:11]
-    gq_hbm, gg_hbm, pk_ref, pv_ref, gq, gg, sems = refs[11 if first else 13 :]
+    q_ref, v_ref, gate_ref, early_ref = refs[8:12]
+    gq_hbm, gg_hbm, pk_ref, pv_ref, gq, gg, sems = refs[12 if first else 14 :]
+
+    @pl.when(core_of() == 0)
+    def _():
+        gg[...] = early_ref[...]
+
+    @pl.when(core_of() == 1)
+    def _():
+        gate_part(plan, where, inv_ref, gate_ref, att_ref, gated_ref, gg)
+
     causal = causal_mask(plan.rows)
     for g in range(plan.group):
         at = plan.columns(*where, g)
@@ -235,10 +312,6 @@
         gq[:, head(g)] = (glq * (sig * (1.0 + q * (1.0 - sig)))).astype(BF16)
         pk_ref[:, head(g)] = dot(dw, lq_ref[:, head(g)], 0, 0)
         pv_ref[:, head(g)] = dot(w_ref[g], d, 0, 0)
-        gate = sigmoid(gate_ref[:, at].astype(F32))
-        gg[:, head(g)] = (
-            gated_ref[:, head(g)] * (att_ref[:, head(g)] * inv_ref[...]) * (1.0 - gate)
-        ).astype(BF16)
     send_out(plan, where, ((gq, gq_hbm), (gg, gg_hbm)), sems)
 
 
@@ -256,9 +329,10 @@
 
 def finish_kernel(plan, where, *refs):
     side = where[1]
-    pieces, add_ref = refs[:4], refs[4 : 4 + side]
-    refs = refs[4 + side :]
-    k_ref, v_ref, lk_ref, pk_ref, pv_ref = refs[:5]
+    extra = side * (1 + plan.split)
+    pieces, add_ref = refs[:4], refs[4 : 4 + extra]
+    refs = refs[4 + extra :]
+    slope_ref, v_ref, lk_ref, pk_ref, pv_ref = refs[:5]
     if side:
         gk, gv, state_ref = refs[5:]
     else:
@@ -277,11 +351,9 @@
     for g in range(plan.group):
         at = plan.columns(*where, g)
         state = state_ref[head(g), :]
-        k = k_ref[:, at].astype(F32)
-        sig = sigmoid(k)
         gv[:, head(g)] = (pv_ref[:, head(g)] + dot(lk_ref[:, head(g)], state, 1, 0)).astype(BF16)
         glk = pk_ref[:, head(g)] + dot(v_ref[:, at], state, 1, 1)
-        gk[:, head(g)] = (glk * (sig * (1.0 + k * (1.0 - sig)))).astype(BF16)
+        gk[:, head(g)] = (glk * slope_ref[:, head(g)]).astype(BF16)
         if not side and (g + 1) % plan.batch == 0:
             first = g + 1 - plan.batch
             here = slice(first * DH, (g + 1) * DH)
@@ -292,17 +364,19 @@
         copy.wait()
 
 
-def split_kernel(plan, keep_ref, got_ref, *outs):
-    chip = chip_of()
-    for k in range(QUAD):
-        here = pl.ds(pl.multiple_of((chip ^ mate(GATHER, k)) * plan.part, plan.part), plan.part)
-        outs[k][...] = keep_ref[here, :] + got_ref[here, :]
+def split_kernel(plan, slots, keep_ref, got_ref, *outs):
+    for n, slot in enumerate(slots):
+        k = mate(GATHER, slot)
+        if len(slots) == QUAD:
+            here = plan.own_part(k)
+        else:
+            here = pl.ds(pl.multiple_of(lax.rem(k + 1, 2) * plan.part, plan.part), plan.part)
+        outs[n][...] = keep_ref[plan.own_part(k), :] + got_ref[here, :]
 
 
 def onward_kernel(plan, reverse, k, piece_ref, keep_ref, out_ref):
-    here = pl.ds(pl.multiple_of((chip_of() ^ mate(HAND, k)) * plan.part, plan.part), plan.part)
     add = core_of() == (1 if reverse else 0)
-    out_ref[...] = piece_ref[...] + jnp.where(add, keep_ref[here, :], 0.0)
+    out_ref[...] = piece_ref[...] + jnp.where(add, keep_ref[plan.own_part(mate(HAND, k)), :], 0.0)
 
 
 def before_kernel(reverse, span, *refs):
@@ -331,9 +405,19 @@
     return lax.ppermute(x, "ctx", [(i, i ^ 2 * orders[i % 2][slot]) for i in range(count)])
 
 
-def gather_sums(plan, keep, near):
-    mine = run(functools.partial(split_kernel, plan), [plan.piece] * QUAD, keep, near)
-    return [mine[0]], [quad_swap(mine[k], k, GATHER) for k in range(1, QUAD)]
+def gather_sums(plan, keep, near, early):
+    first = after(near[0], early(near[0]))
+    mine, came = {}, {}
+    for slots, got in zip(SECTIONS if plan.split else [range(QUAD)], [first] + near[1:]):
+        keep, got = after((keep, got), mine)
+        made = run(
+            functools.partial(split_kernel, plan, slots), [plan.piece] * len(slots), keep, got
+        )
+        for slot, x in zip(slots, made):
+            mine[slot] = x
+            if slot:
+                came[slot] = quad_swap(x, slot, GATHER)
+    return [mine[0]], [came[slot] for slot in range(1, QUAD)]
 
 
 def across(parts, reverse):
@@ -364,10 +448,10 @@
     return outs, [quad_swap(outs[k], k, HAND) for k in range(1, QUAD)]
 
 
-def carried(plan, sums_of, work, reverse):
-    near = swap(sums_of[0, 0], 1)
+def carried(plan, sums_of, early, work, reverse):
+    near = [swap(x, 1) for x in sums_of[0, 0]]
     keep = sums_of[0, 1]
-    own, came = gather_sums(plan, keep, near)
+    own, came = gather_sums(plan, keep, near, early)
     results = []
 
     def meanwhile(thunks, held, values):
@@ -381,7 +465,7 @@
     outs, came = hand_out(plan, parts, got, base, span, reverse)
     came = meanwhile(work[2], outs[0], came)
     own = [outs[0]] + came
-    pieces = {(0, 1): own + [near]}
+    pieces = {(0, 1): own + near}
     pieces[0, 0] = [
         swap(run(functools.partial(onward_kernel, plan, reverse, k), plan.piece, x, keep), 1)
         for k, x in enumerate(own)
@@ -402,31 +486,42 @@
     count = len(groups)
     k, v, first_sum = run(
         functools.partial(first_kernel, plan, groups),
-        [plan.given, plan.given, plan.tall],
+        [plan.given, plan.given, plan.block if plan.split else plan.tall],
         pltpu.with_memory_space_constraint(key_rows, pltpu.HBM),
         pltpu.with_memory_space_constraint(value_rows, pltpu.HBM),
         scratch=[pltpu.SemaphoreType.DMA((2 * count,))],
         in_specs=[ANY, ANY],
     )
-    sums = {groups[0]: first_sum}
-    for where in groups[1:]:
-        sums[where] = run(functools.partial(next_kernel, plan, where), plan.tall, k, v)
+    sums = {groups[0]: [first_sum]}
+    if plan.split:
+        second = functools.partial(next_kernel, plan, groups[0], 1)
+        sums[groups[0]].append(run(second, plan.block, k, v))
+    sums[groups[1]] = run(functools.partial(next_kernel, plan, groups[1], None), plan.tall, k, v)
+
+    ahead = []
+
+    def early(held):
+        kernel = functools.partial(early_key_kernel, plan, groups)
+        ahead[:] = run(kernel, [plan.low, plan.full] * count, after(k, held))
+        return ahead
 
     def local(where):
         def thunk(held):
+            n = 2 * groups.index(where)
             args = after((queries, k, v, gate_rows, cotangent), held)
             return run(
                 functools.partial(local_kernel, plan, where),
-                [plan.low, plan.low, plan.square, plan.full, plan.full],
+                [plan.low, plan.full, plan.low, plan.square, plan.full, plan.full],
                 *args,
+                *ahead[n : n + 2],
             )
 
         return thunk
 
     thunks = [local(where) for where in groups]
-    pieces, made = carried(plan, sums, ([], thunks, []), False)
+    pieces, made = carried(plan, sums, early, ([], thunks, []), False)
     made = dict(zip(groups, made))
-    lq, lk, weights, inside, gated = ({w: made[w][n] for w in groups} for n in range(5))
+    lk, slope, lq, weights, inside, gated = ({w: made[w][n] for w in groups} for n in range(6))
     state, attended, running = {}, {}, ()
     for n, where in enumerate(late):
         last = n == count - 1
@@ -442,15 +537,29 @@
     scales = head_total(running[0])
     d_attn, sums = {}, {}
     for n, where in enumerate(groups):
+        total = plan.block if n == 0 and plan.split else plan.tall
         d_attn[where], sums[where], *more = run(
             functools.partial(grad_kernel, plan, n == 0),
-            [plan.low, plan.tall] + ([plan.wide] * 2 if n == 0 else []),
+            [plan.low, total] + ([plan.wide] * 2 if n == 0 else []),
             *scales,
             attended[where],
             gated[where],
             lq[where],
         )
         scales = more or scales
+        if n == 0:
+            sums[where] = [sums[where]]
+            if plan.split:
+                second = functools.partial(section_kernel, plan, 1)
+                sums[where].append(run(second, plan.block, lq[where], d_attn[where]))
+    gates = []
+
+    def early_gates(held):
+        args = (scales[0], gate_rows, *(attended[w] for w in groups), *(gated[w] for w in groups))
+        kernel = functools.partial(early_gate_kernel, plan, groups)
+        gates[:] = run(kernel, [plan.low] * count, *after(args, held))
+        return gates
+
     outer = []
 
     def inner(where):
@@ -460,6 +569,7 @@
                 (
                     state[where], scales[0], weights[where], d_attn[where], lq[where], lk[where],
                     attended[where], gated[where], queries, v, gate_rows,
+                    gates[groups.index(where)],
                 ),
                 held,
             )
@@ -470,9 +580,9 @@
                 *outer,
                 scratch=[pltpu.VMEM((plan.rows, plan.span), BF16)] * 2
                 + [pltpu.SemaphoreType.DMA((2,))],
-                in_specs=[VMEM] * 11 + [ANY] * len(outer),
+                in_specs=[VMEM] * 12 + [ANY] * len(outer),
                 out_specs=[ANY, ANY, VMEM, VMEM],
-                aliases={} if first else {11: 0, 12: 1},
+                aliases={} if first else {12: 0, 13: 1},
             )
             outer[:] = [gq, gg]
             return pk, pv
@@ -480,7 +590,7 @@
         return thunk
 
     thunks = [inner(where) for where in groups]
-    pieces, made = carried(plan, sums, ([], thunks[:1], thunks[1:]), True)
+    pieces, made = carried(plan, sums, early_gates, ([], thunks[:1], thunks[1:]), True)
     made = dict(zip(groups, made))
     where = (0, 1)
     state_scratch = pltpu.VMEM((plan.span, DH), BF16)
@@ -488,7 +598,7 @@
         functools.partial(finish_kernel, plan, where),
         [plan.low, plan.low],
         *pieces[where],
-        k,
+        slope[where],
         v,
         lk[where],
         *made[where],
@@ -499,7 +609,7 @@
         functools.partial(finish_kernel, plan, where),
         [plan.given, plan.given],
         *pieces[where],
-        k,
+        slope[where],
         v,
         lk[where],
         *made[where],

time: 68.9 us -> 68.4 us (level)
  waiting for transfers between devices: 28.1 us -> 26.3 us
  Pallas kernels: 15.7 us -> 16.9 us
    ppermute x12 -> x14, waiting for transfers between devices: 9.34 us -> 7.27 us  [swap(): return lax.ppermute(x, 'ctx', [(i, i ^ distance) for i in range(count)])]
    pallas_call x24 -> x30, Pallas kernels: 15.7 us -> 16.9 us  [run(): pl.pallas_call(kernel, out_shape=out_shape, scratch_shapes=list(scratch),...]
    ppermute x12 -> x14, starting transfers between devices: 6.92 us -> 7.14 us  [swap(): return lax.ppermute(x, 'ctx', [(i, i ^ distance) for i in range(count)])]
  transfers between devices with their start and end apart: 25 -> 27, of which waited for: 18 -> 19; matrix products, arithmetic and copies ran while one was open for 0% -> 0% of each run, Pallas kernels for 16% -> 19%
where the time goes in v4:
time: 68.4 us; the launch traced here: 68.3 us
  waiting for transfers between devices  26.3 us (38%)
  starting transfers between devices  23.8 us (35%)
  Pallas kernels  16.9 us (25%)
  between operations  1.11 us (2%)
    pallas_call x30, Pallas kernels, run(): pl.pallas_call(kernel, out_shape=out_shape, scratch_shapes=list(scratch),...  16.9 us
    ppermute x12, waiting for transfers between devices, quad_swap(): lax.ppermute(x, 'ctx', [(i, i ^ 2 * orders[i % 2][slot]) for i in range(c...  16.8 us
    ppermute x12, starting transfers between devices, quad_swap(): lax.ppermute(x, 'ctx', [(i, i ^ 2 * orders[i % 2][slot]) for i in range(c...  15.3 us
    ppermute x14, waiting for transfers between devices, swap(): return lax.ppermute(x, 'ctx', [(i, i ^ distance) for i in range(count)])  7.27 us
    ppermute x14, starting transfers between devices, swap(): return lax.ppermute(x, 'ctx', [(i, i ^ distance) for i in range(count)])  7.14 us
    ppermute x1, waiting for transfers between devices, head_total(): return (sums, lax.ppermute(sums, 'head', [(0, 1), (1, 0)]))  2.32 us
    ppermute x1, starting transfers between devices, head_total(): return (sums, lax.ppermute(sums, 'head', [(0, 1), (1, 0)]))  1.41 us
  transfers between devices with their start and end apart: 27, of which 19 were waited for; matrix products, arithmetic and copies ran while one was open for 0% of the time, Pallas kernels for 19%

profile of v4, /device:TPU:0, one launch (start us, length us, event | category | flops | bytes accessed | tf_op | source)
XLA Modules:
  0.0 68.3 jit_solution(11284465791347734764)
XLA Ops:
  0.6 1.5 %shard_map.84 = (bf16[192,2048]{1,0:T(8,128)(2,1)S(1)}, bf16[192,2048]{1,0:T(8,128)(2,1)S(1)}, f32[512,128]{1,0:T(8,128)S(1)}) custom-call(bf16[192,2048]{1,0:T(8,128)(2,1)} %k_hbm.1, bf16[192,2048]{1,0:T(8,128)(2,1)} %v_hbm.1), custom_call_target="tpu_custom_call" | custom-call | tf_op jit(solution)/shard_map/pallas_call | solution.py:119
  2.1 0.5 collective-permute-start
  2.6 0.3 shard_map.87
  2.9 0.1 collective-permute-start.1
  3.1 0.4 shard_map.85.keep_ref
  3.5 0.3 collective-permute-done.got_ref.refs_4_
  3.8 0.6 shard_map.86
  4.5 2.9 %collective-permute-start.2 = (f32[256,128]{1,0:T(8,128)S(1)}, f32[256,128]{1,0:T(8,128)S(1)}, u32[]{:S(2)}, u32[]{:S(2)}) collective-permute-start(f32[256,128]{1,0:T(8,128)S(1)} %get-tuple-element.128), channel_id=1, source_target_pairs={{0,4},{2,6},{4,0},{6,2},{8,12},{10,14},{12,8},{14,10},{16,20},{18,... | collective-permute-start | bytes 393224 | tf_op jit(solution)/shard_map/ppermute | solution.py:405
  7.4 1.6 %collective-permute-start.3 = (f32[256,128]{1,0:T(8,128)S(1)}, f32[256,128]{1,0:T(8,128)S(1)}, u32[]{:S(2)}, u32[]{:S(2)}) collective-permute-start(f32[256,128]{1,0:T(8,128)S(1)} %get-tuple-element.129), channel_id=1, source_target_pairs={{0,8},{2,10},{4,12},{6,14},{8,0},{10,2},{12,4},{14,6},{16,24},{18,... | collective-permute-start | bytes 393224 | tf_op jit(solution)/shard_map/ppermute | solution.py:405
  9.0 0.1 collective-permute-start.4
  9.1 1.5 %collective-permute-done.2.refs_1_ = f32[256,128]{1,0:T(8,128)S(1)} collective-permute-done((f32[256,128]{1,0:T(8,128)S(1)}, f32[256,128]{1,0:T(8,128)S(1)}, u32[]{:S(2)}, u32[]{:S(2)}) %collective-permute-start.2) | collective-permute-done | bytes 131104 | tf_op jit(solution)/shard_map/ppermute | solution.py:405
  10.6 2.9 %collective-permute-done.3.refs_2_ = f32[256,128]{1,0:T(8,128)S(1)} collective-permute-done((f32[256,128]{1,0:T(8,128)S(1)}, f32[256,128]{1,0:T(8,128)S(1)}, u32[]{:S(2)}, u32[]{:S(2)}) %collective-permute-start.3) | collective-permute-done | bytes 131104 | tf_op jit(solution)/shard_map/ppermute | solution.py:405
  13.4 1.5 %collective-permute-done.4.refs_3_ = f32[256,128]{1,0:T(8,128)S(1)} collective-permute-done((f32[256,128]{1,0:T(8,128)S(1)}, f32[256,128]{1,0:T(8,128)S(1)}, u32[]{:S(2)}, u32[]{:S(2)}) %collective-permute-start.4) | collective-permute-done | bytes 131104 | tf_op jit(solution)/shard_map/ppermute | solution.py:405
  15.0 2.8 %collective-permute-start.5 = (f32[256,128]{1,0:T(8,128)S(1)}, f32[256,128]{1,0:T(8,128)S(1)}, u32[]{:S(2)}, u32[]{:S(2)}) collective-permute-start(f32[256,128]{1,0:T(8,128)S(1)} %add_add_fusion.1), channel_id=1, source_target_pairs={{0,16},{2,18},{4,20},{6,22},{8,24},{10,26},{12,28},{14,30},{16,0},... | collective-permute-start | bytes 393224 | tf_op jit(solution)/shard_map/ppermute | solution.py:400
  17.8 1.1 %shard_map.91 = (bf16[192,1024]{1,0:T(8,128)(2,1)S(1)}, f32[192,1024]{1,0:T(8,128)S(1)}, bf16[192,1024]{1,0:T(8,128)(2,1)S(1)}, bf16[8,192,192]{2,1,0:T(8,128)(2...) custom-call(bf16[192,2048]{1,0:T(8,128)(2,1)S(1)} %copy-done.1, ...), custom_call_target="tpu_custom_call" | custom-call | tf_op jit(solution)/shard_map/pallas_call | solution.py:119
  18.9 1.1 %shard_map.90 = (bf16[192,1024]{1,0:T(8,128)(2,1)S(1)}, f32[192,1024]{1,0:T(8,128)S(1)}, bf16[192,1024]{1,0:T(8,128)(2,1)S(1)}, bf16[8,192,192]{2,1,0:T(8,128)(2...) custom-call(bf16[192,2048]{1,0:T(8,128)(2,1)S(1)} %copy-done.1, ...), custom_call_target="tpu_custom_call" | custom-call | tf_op jit(solution)/shard_map/pallas_call | solution.py:119
  20.1 3.0 %collective-permute-done.5.refs_4_ = f32[256,128]{1,0:T(8,128)S(1)} collective-permute-done((f32[256,128]{1,0:T(8,128)S(1)}, f32[256,128]{1,0:T(8,128)S(1)}, u32[]{:S(2)}, u32[]{:S(2)}) %collective-permute-start.5) | collective-permute-done | bytes 131104 | tf_op jit(solution)/shard_map/ppermute | solution.py:400
  23.1 0.1 shard_map.92
  23.2 0.7 collective-permute-start.6
  23.9 0.7 collective-permute-start.7
  24.5 2.2 %collective-permute-start.8 = (f32[256,128]{1,0:T(8,128)S(1)}, f32[256,128]{1,0:T(8,128)S(1)}, u32[]{:S(2)}, u32[]{:S(2)}) collective-permute-start(f32[256,128]{1,0:T(8,128)S(1)} %get-tuple-element.155), channel_id=1, source_target_pairs={{0,12},{2,14},{4,8},{6,10},{8,4},{10,6},{12,0},{14,2},{16,28},{18,... | collective-permute-start | bytes 393224 | tf_op jit(solution)/shard_map/ppermute | solution.py:405
  26.8 0.1 collective-permute-start.9
  26.8 2.3 %collective-permute-done.6.refs_1_.piece_ref = f32[256,128]{1,0:T(8,128)S(1)} collective-permute-done((f32[256,128]{1,0:T(8,128)S(1)}, f32[256,128]{1,0:T(8,128)S(1)}, u32[]{:S(2)}, u32[]{:S(2)}) %collective-permute-start.6) | collective-permute-done | bytes 131104 | tf_op jit(solution)/shard_map/ppermute | solution.py:405
  29.2 0.1 collective-permute-start.10
  29.2 0.3 collective-permute-done.7.refs_2_.piece_ref
  29.6 0.3 collective-permute-start.11
  29.8 2.2 %collective-permute-done.8.refs_3_.piece_ref = f32[256,128]{1,0:T(8,128)S(1)} collective-permute-done((f32[256,128]{1,0:T(8,128)S(1)}, f32[256,128]{1,0:T(8,128)S(1)}, u32[]{:S(2)}, u32[]{:S(2)}) %collective-permute-start.8) | collective-permute-done | bytes 131104 | tf_op jit(solution)/shard_map/ppermute | solution.py:405
  32.1 0.1 collective-permute-start.12
  32.1 0.4 shard_map.93
  32.6 0.9 %collective-permute-done.12.refs_3_ = f32[256,128]{1,0:T(8,128)S(1)} collective-permute-done((f32[256,128]{1,0:T(8,128)S(1)}, f32[256,128]{1,0:T(8,128)S(1)}, u32[]{:S(2)}, u32[]{:S(2)}) %collective-permute-start.12) | collective-permute-done | bytes 131104 | tf_op jit(solution)/shard_map/ppermute | solution.py:400
  33.5 0.5 shard_map.98
  34.0 1.4 %collective-permute-start.13 = (f32[8,192]{1,0:T(8,128)S(1)}, f32[8,192]{1,0:T(8,128)S(1)}, u32[]{:S(2)}, u32[]{:S(2)}) collective-permute-start(f32[8,192]{1,0:T(8,128)S(1)} %get-tuple-element.159.a_ref), channel_id=1, source_target_pairs={{0,1},{1,0},{2,3},{3,2},{4,5},{5,4},{6,7},{7,6},{8,9},{9,8},{10,11... | collective-permute-start | bytes 18440 | tf_op jit(solution)/shard_map/ppermute | solution.py:478
  35.4 2.3 %collective-permute-done.13.b_ref = f32[8,192]{1,0:T(8,128)S(1)} collective-permute-done((f32[8,192]{1,0:T(8,128)S(1)}, f32[8,192]{1,0:T(8,128)S(1)}, u32[]{:S(2)}, u32[]{:S(2)}) %collective-permute-start.13) | collective-permute-done | bytes 6176 | tf_op jit(solution)/shard_map/ppermute | solution.py:478
  37.7 0.7 %shard_map.99 = (bf16[192,1024]{1,0:T(8,128)(2,1)S(1)}, f32[512,128]{1,0:T(8,128)S(1)}, f32[192,128]{1,0:T(8,128)S(1)}, f32[192,128]{1,0:T(8,128)S(1)}) custom-call(f32[8,192]{1,0:T(8,128)S(1)} %get-tuple-element.159.a_ref, f32[8,192]{1,0:T(8,128)S(1)} %collective-permute-done.13.b_ref, f32[192,1024]{1,0:T(8,128)S(1)} %get-tuple-element.192.att_ref.refs_0_.refs_6_, ...), custom_call_target="tpu_custom_call" | custom-call | tf_op jit(solution)/shard_map/pallas_call | solution.py:119
  38.4 0.1 collective-permute-start.14
  38.5 0.3 shard_map.102
  38.8 0.5 collective-permute-start.15
  39.4 0.4 shard_map.100
  39.7 0.3 collective-permute-done.14.got_ref.refs_4_
  40.0 0.6 shard_map.101
  40.6 0.4 collective-permute-start.16
  41.1 1.4 %collective-permute-start.17 = (f32[256,128]{1,0:T(8,128)S(1)}, f32[256,128]{1,0:T(8,128)S(1)}, u32[]{:S(2)}, u32[]{:S(2)}) collective-permute-start(f32[256,128]{1,0:T(8,128)S(1)} %get-tuple-element.180), channel_id=1, source_target_pairs={{0,8},{2,10},{4,12},{6,14},{8,0},{10,2},{12,4},{14,6},{16,24},{18,... | collective-permute-start | bytes 393224 | tf_op jit(solution)/shard_map/ppermute | solution.py:405
  42.5 1.8 %collective-permute-start.18 = (f32[256,128]{1,0:T(8,128)S(1)}, f32[256,128]{1,0:T(8,128)S(1)}, u32[]{:S(2)}, u32[]{:S(2)}) collective-permute-start(f32[256,128]{1,0:T(8,128)S(1)} %get-tuple-element.184), channel_id=1, source_target_pairs={{0,12},{2,14},{4,8},{6,10},{8,4},{10,6},{12,0},{14,2},{16,28},{18,... | collective-permute-start | bytes 393224 | tf_op jit(solution)/shard_map/ppermute | solution.py:405
  44.3 2.0 %collective-permute-done.16.refs_1_ = f32[256,128]{1,0:T(8,128)S(1)} collective-permute-done((f32[256,128]{1,0:T(8,128)S(1)}, f32[256,128]{1,0:T(8,128)S(1)}, u32[]{:S(2)}, u32[]{:S(2)}) %collective-permute-start.16) | collective-permute-done | bytes 131104 | tf_op jit(solution)/shard_map/ppermute | solution.py:405
  46.3 0.9 %collective-permute-done.17.refs_2_ = f32[256,128]{1,0:T(8,128)S(1)} collective-permute-done((f32[256,128]{1,0:T(8,128)S(1)}, f32[256,128]{1,0:T(8,128)S(1)}, u32[]{:S(2)}, u32[]{:S(2)}) %collective-permute-start.17) | collective-permute-done | bytes 131104 | tf_op jit(solution)/shard_map/ppermute | solution.py:405
  47.1 2.5 %collective-permute-done.18.refs_3_ = f32[256,128]{1,0:T(8,128)S(1)} collective-permute-done((f32[256,128]{1,0:T(8,128)S(1)}, f32[256,128]{1,0:T(8,128)S(1)}, u32[]{:S(2)}, u32[]{:S(2)}) %collective-permute-start.18) | collective-permute-done | bytes 131104 | tf_op jit(solution)/shard_map/ppermute | solution.py:405
  49.7 1.8 %collective-permute-start.19 = (f32[256,128]{1,0:T(8,128)S(1)}, f32[256,128]{1,0:T(8,128)S(1)}, u32[]{:S(2)}, u32[]{:S(2)}) collective-permute-start(f32[256,128]{1,0:T(8,128)S(1)} %add_add_fusion), channel_id=1, source_target_pairs={{0,16},{2,18},{4,20},{6,22},{8,24},{10,26},{12,28},{14,30},{16,0},... | collective-permute-start | bytes 393224 | tf_op jit(solution)/shard_map/ppermute | solution.py:400
  51.5 3.2 %shard_map.105 = (bf16[192,2048]{1,0:T(8,128)(2,1)}, bf16[192,2048]{1,0:T(8,128)(2,1)}, f32[192,1024]{1,0:T(8,128)S(1)}, f32[192,1024]{1,0:T(8,128)S(1)}) custom-call(bf16[1024,128]{1,0:T(8,128)(2,1)S(1)} %get-tuple-element.186.refs_0_, f32[192,128]{1,0:T(8,128)S(1)} %get-tuple-element.203.a_ref.inv_ref.refs_1_, ...), custom_call_target="tpu_custom_call" | custom-call | tf_op jit(solution)/shard_map/pallas_call | solution.py:119
  54.7 2.0 %collective-permute-done.19.refs_4_ = f32[256,128]{1,0:T(8,128)S(1)} collective-permute-done((f32[256,128]{1,0:T(8,128)S(1)}, f32[256,128]{1,0:T(8,128)S(1)}, u32[]{:S(2)}, u32[]{:S(2)}) %collective-permute-start.19) | collective-permute-done | bytes 131104 | tf_op jit(solution)/shard_map/ppermute | solution.py:400
  56.7 0.1 shard_map.106
  56.9 0.7 %collective-permute-start.21 = (f32[256,128]{1,0:T(8,128)S(1)}, f32[256,128]{1,0:T(8,128)S(1)}, u32[]{:S(2)}, u32[]{:S(2)}) collective-permute-start(f32[256,128]{1,0:T(8,128)S(1)} %get-tuple-element.217), channel_id=1, source_target_pairs={{0,4},{2,6},{4,0},{6,2},{8,12},{10,14},{12,8},{14,10},{16,20},{18,... | collective-permute-start | bytes 393224 | tf_op jit(solution)/shard_map/ppermute | solution.py:405
  57.6 0.3 collective-permute-start.22
  57.8 2.6 %collective-permute-start.23 = (f32[256,128]{1,0:T(8,128)S(1)}, f32[256,128]{1,0:T(8,128)S(1)}, u32[]{:S(2)}, u32[]{:S(2)}) collective-permute-start(f32[256,128]{1,0:T(8,128)S(1)} %get-tuple-element.219), channel_id=1, source_target_pairs={{0,12},{2,14},{4,8},{6,10},{8,4},{10,6},{12,0},{14,2},{16,28},{18,... | collective-permute-start | bytes 393224 | tf_op jit(solution)/shard_map/ppermute | solution.py:405
  60.4 0.1 collective-permute-start.20
  60.5 3.4 %shard_map.107 = (bf16[192,2048]{1,0:T(8,128)(2,1)}, bf16[192,2048]{1,0:T(8,128)(2,1)}, f32[192,1024]{1,0:T(8,128)S(1)}, f32[192,1024]{1,0:T(8,128)S(1)}) custom-call(bf16[1024,128]{1,0:T(8,128)(2,1)S(1)} %get-tuple-element.202.refs_0_, f32[192,128]{1,0:T(8,128)S(1)} %get-tuple-element.203.a_ref.inv_ref.refs_1_, ...), custom_call_target="tpu_custom_call", output_to_operand_aliasing={{0}: (12, {}), {1}: (13, {})} | custom-call | tf_op jit(solution)/shard_map/pallas_call | solution.py:119
  64.0 0.8 %collective-permute-done.23.piece_ref.refs_3_ = f32[256,128]{1,0:T(8,128)S(1)} collective-permute-done((f32[256,128]{1,0:T(8,128)S(1)}, f32[256,128]{1,0:T(8,128)S(1)}, u32[]{:S(2)}, u32[]{:S(2)}) %collective-permute-start.23) | collective-permute-done | bytes 131104 | tf_op jit(solution)/shard_map/ppermute | solution.py:405
  64.9 0.1 collective-permute-start.24
  65.0 0.5 collective-permute-start.25
  65.5 0.1 collective-permute-start.26
  65.5 0.5 shard_map.112
  66.0 0.2 collective-permute-done.24.refs_1_
  66.3 0.2 collective-permute-done.25.refs_2_
  66.5 0.3 collective-permute-done.26.refs_3_
  66.8 1.3 %shard_map.113 = (bf16[192,2048]{1,0:T(8,128)(2,1)}, bf16[192,2048]{1,0:T(8,128)(2,1)}) custom-call(f32[256,128]{1,0:T(8,128)S(1)} %collective-permute-done.20.refs_0_, f32[256,128]{1,0:T(8,128)S(1)} %collective-permute-done.24.refs_1_, f32[256,128]{1,0:T(8,128)S(1)} %collective-permute-done.25.refs_2_, f32[256,128]{1,0:T(8,128)S(1)} %collective-permute-done.26.refs_3_, ...), custom_call_target="tpu_custom_call" | custom-call | tf_op jit(solution)/shard_map/pallas_call | solution.py:119
  (28 shorter events, 0.5 us)
Async XLA Ops:
  2.1 1.7 %collective-permute-start = (f32[512,128]{1,0:T(8,128)S(1)}, f32[512,128]{1,0:T(8,128)S(1)}, u32[]{:S(2)}, u32[]{:S(2)}) collective-permute-start(f32[512,128]{1,0:T(8,128)S(1)} %get-tuple-element.119), channel_id=1, source_target_pairs={{0,2},{2,0},{4,6},{6,4},{8,10},{10,8},{12,14},{14,12},{16,18},{18,... | collective-permute-start | bytes 786440 | tf_op jit(solution)/shard_map/ppermute | solution.py:400
  2.9 6.0 %collective-permute-start.1 = (f32[512,128]{1,0:T(8,128)S(1)}, f32[512,128]{1,0:T(8,128)S(1)}, u32[]{:S(2)}, u32[]{:S(2)}) collective-permute-start(f32[512,128]{1,0:T(8,128)S(1)} %shard_map.87), channel_id=1, source_target_pairs={{0,2},{2,0},{4,6},{6,4},{8,10},{10,8},{12,14},{14,12},{16,18},{18,... | collective-permute-start | bytes 786440 | tf_op jit(solution)/shard_map/ppermute | solution.py:400
  3.8 14.0 %copy-start.2 = (bf16[192,2048]{1,0:T(8,128)(2,1)S(1)}, bf16[192,2048]{1,0:T(8,128)(2,1)}, u32[]{:S(2)}) copy-start(bf16[192,2048]{1,0:T(8,128)(2,1)} %cot_ref.1) | copy-start | bytes 2359300
  4.4 13.4 %copy-start.1 = (bf16[192,2048]{1,0:T(8,128)(2,1)S(1)}, bf16[192,2048]{1,0:T(8,128)(2,1)}, u32[]{:S(2)}) copy-start(bf16[192,2048]{1,0:T(8,128)(2,1)} %refs_8_.1) | copy-start | bytes 2359300
  4.5 13.4 %copy-start = (bf16[192,2048]{1,0:T(8,128)(2,1)S(1)}, bf16[192,2048]{1,0:T(8,128)(2,1)}, u32[]{:S(2)}) copy-start(bf16[192,2048]{1,0:T(8,128)(2,1)} %refs_10_.1) | copy-start | bytes 2359300
  4.5 6.1 %collective-permute-start.2 = (f32[256,128]{1,0:T(8,128)S(1)}, f32[256,128]{1,0:T(8,128)S(1)}, u32[]{:S(2)}, u32[]{:S(2)}) collective-permute-start(f32[256,128]{1,0:T(8,128)S(1)} %get-tuple-element.128), channel_id=1, source_target_pairs={{0,4},{2,6},{4,0},{6,2},{8,12},{10,14},{12,8},{14,10},{16,20},{18,... | collective-permute-start | bytes 393224 | tf_op jit(solution)/shard_map/ppermute | solution.py:405
  7.4 6.0 %collective-permute-start.3 = (f32[256,128]{1,0:T(8,128)S(1)}, f32[256,128]{1,0:T(8,128)S(1)}, u32[]{:S(2)}, u32[]{:S(2)}) collective-permute-start(f32[256,128]{1,0:T(8,128)S(1)} %get-tuple-element.129), channel_id=1, source_target_pairs={{0,8},{2,10},{4,12},{6,14},{8,0},{10,2},{12,4},{14,6},{16,24},{18,... | collective-permute-start | bytes 393224 | tf_op jit(solution)/shard_map/ppermute | solution.py:405
  9.0 5.9 %collective-permute-start.4 = (f32[256,128]{1,0:T(8,128)S(1)}, f32[256,128]{1,0:T(8,128)S(1)}, u32[]{:S(2)}, u32[]{:S(2)}) collective-permute-start(f32[256,128]{1,0:T(8,128)S(1)} %get-tuple-element.133), channel_id=1, source_target_pairs={{0,12},{2,14},{4,8},{6,10},{8,4},{10,6},{12,0},{14,2},{16,28},{18,... | collective-permute-start | bytes 393224 | tf_op jit(solution)/shard_map/ppermute | solution.py:405
  15.0 8.1 %collective-permute-start.5 = (f32[256,128]{1,0:T(8,128)S(1)}, f32[256,128]{1,0:T(8,128)S(1)}, u32[]{:S(2)}, u32[]{:S(2)}) collective-permute-start(f32[256,128]{1,0:T(8,128)S(1)} %add_add_fusion.1), channel_id=1, source_target_pairs={{0,16},{2,18},{4,20},{6,22},{8,24},{10,26},{12,28},{14,30},{16,0},... | collective-permute-start | bytes 393224 | tf_op jit(solution)/shard_map/ppermute | solution.py:400
  23.2 6.0 %collective-permute-start.6 = (f32[256,128]{1,0:T(8,128)S(1)}, f32[256,128]{1,0:T(8,128)S(1)}, u32[]{:S(2)}, u32[]{:S(2)}) collective-permute-start(f32[256,128]{1,0:T(8,128)S(1)} %get-tuple-element.153), channel_id=1, source_target_pairs={{0,4},{2,6},{4,0},{6,2},{8,12},{10,14},{12,8},{14,10},{16,20},{18,... | collective-permute-start | bytes 393224 | tf_op jit(solution)/shard_map/ppermute | solution.py:405
  23.9 5.7 %collective-permute-start.7 = (f32[256,128]{1,0:T(8,128)S(1)}, f32[256,128]{1,0:T(8,128)S(1)}, u32[]{:S(2)}, u32[]{:S(2)}) collective-permute-start(f32[256,128]{1,0:T(8,128)S(1)} %get-tuple-element.154), channel_id=1, source_target_pairs={{0,8},{2,10},{4,12},{6,14},{8,0},{10,2},{12,4},{14,6},{16,24},{18,... | collective-permute-start | bytes 393224 | tf_op jit(solution)/shard_map/ppermute | solution.py:405
  24.5 7.5 %collective-permute-start.8 = (f32[256,128]{1,0:T(8,128)S(1)}, f32[256,128]{1,0:T(8,128)S(1)}, u32[]{:S(2)}, u32[]{:S(2)}) collective-permute-start(f32[256,128]{1,0:T(8,128)S(1)} %get-tuple-element.155), channel_id=1, source_target_pairs={{0,12},{2,14},{4,8},{6,10},{8,4},{10,6},{12,0},{14,2},{16,28},{18,... | collective-permute-start | bytes 393224 | tf_op jit(solution)/shard_map/ppermute | solution.py:405
  26.8 5.8 %collective-permute-start.9 = (f32[256,128]{1,0:T(8,128)S(1)}, f32[256,128]{1,0:T(8,128)S(1)}, u32[]{:S(2)}, u32[]{:S(2)}) collective-permute-start(f32[256,128]{1,0:T(8,128)S(1)} %shard_map.94), channel_id=1, source_target_pairs={{0,2},{2,0},{4,6},{6,4},{8,10},{10,8},{12,14},{14,12},{16,18},{18,... | collective-permute-start | bytes 393224 | tf_op jit(solution)/shard_map/ppermute | solution.py:400
  29.2 3.4 %collective-permute-start.10 = (f32[256,128]{1,0:T(8,128)S(1)}, f32[256,128]{1,0:T(8,128)S(1)}, u32[]{:S(2)}, u32[]{:S(2)}) collective-permute-start(f32[256,128]{1,0:T(8,128)S(1)} %shard_map.95), channel_id=1, source_target_pairs={{0,2},{2,0},{4,6},{6,4},{8,10},{10,8},{12,14},{14,12},{16,18},{18,... | collective-permute-start | bytes 393224 | tf_op jit(solution)/shard_map/ppermute | solution.py:400
  29.6 3.0 %collective-permute-start.11 = (f32[256,128]{1,0:T(8,128)S(1)}, f32[256,128]{1,0:T(8,128)S(1)}, u32[]{:S(2)}, u32[]{:S(2)}) collective-permute-start(f32[256,128]{1,0:T(8,128)S(1)} %shard_map.96), channel_id=1, source_target_pairs={{0,2},{2,0},{4,6},{6,4},{8,10},{10,8},{12,14},{14,12},{16,18},{18,... | collective-permute-start | bytes 393224 | tf_op jit(solution)/shard_map/ppermute | solution.py:400
  32.1 1.4 %collective-permute-start.12 = (f32[256,128]{1,0:T(8,128)S(1)}, f32[256,128]{1,0:T(8,128)S(1)}, u32[]{:S(2)}, u32[]{:S(2)}) collective-permute-start(f32[256,128]{1,0:T(8,128)S(1)} %shard_map.97), channel_id=1, source_target_pairs={{0,2},{2,0},{4,6},{6,4},{8,10},{10,8},{12,14},{14,12},{16,18},{18,... | collective-permute-start | bytes 393224 | tf_op jit(solution)/shard_map/ppermute | solution.py:400
  34.0 3.7 %collective-permute-start.13 = (f32[8,192]{1,0:T(8,128)S(1)}, f32[8,192]{1,0:T(8,128)S(1)}, u32[]{:S(2)}, u32[]{:S(2)}) collective-permute-start(f32[8,192]{1,0:T(8,128)S(1)} %get-tuple-element.159.a_ref), channel_id=1, source_target_pairs={{0,1},{1,0},{2,3},{3,2},{4,5},{5,4},{6,7},{7,6},{8,9},{9,8},{10,11... | collective-permute-start | bytes 18440 | tf_op jit(solution)/shard_map/ppermute | solution.py:478
  38.4 1.6 %collective-permute-start.14 = (f32[512,128]{1,0:T(8,128)S(1)}, f32[512,128]{1,0:T(8,128)S(1)}, u32[]{:S(2)}, u32[]{:S(2)}) collective-permute-start(f32[512,128]{1,0:T(8,128)S(1)} %get-tuple-element.165), channel_id=1, source_target_pairs={{0,2},{2,0},{4,6},{6,4},{8,10},{10,8},{12,14},{14,12},{16,18},{18,... | collective-permute-start | bytes 786440 | tf_op jit(solution)/shard_map/ppermute | solution.py:400
  38.8 3.6 %collective-permute-start.15 = (f32[512,128]{1,0:T(8,128)S(1)}, f32[512,128]{1,0:T(8,128)S(1)}, u32[]{:S(2)}, u32[]{:S(2)}) collective-permute-start(f32[512,128]{1,0:T(8,128)S(1)} %shard_map.102), channel_id=1, source_target_pairs={{0,2},{2,0},{4,6},{6,4},{8,10},{10,8},{12,14},{14,12},{16,18},{18,... | collective-permute-start | bytes 786440 | tf_op jit(solution)/shard_map/ppermute | solution.py:400
  40.6 5.6 %collective-permute-start.16 = (f32[256,128]{1,0:T(8,128)S(1)}, f32[256,128]{1,0:T(8,128)S(1)}, u32[]{:S(2)}, u32[]{:S(2)}) collective-permute-start(f32[256,128]{1,0:T(8,128)S(1)} %get-tuple-element.179), channel_id=1, source_target_pairs={{0,4},{2,6},{4,0},{6,2},{8,12},{10,14},{12,8},{14,10},{16,20},{18,... | collective-permute-start | bytes 393224 | tf_op jit(solution)/shard_map/ppermute | solution.py:405
  41.1 6.1 %collective-permute-start.17 = (f32[256,128]{1,0:T(8,128)S(1)}, f32[256,128]{1,0:T(8,128)S(1)}, u32[]{:S(2)}, u32[]{:S(2)}) collective-permute-start(f32[256,128]{1,0:T(8,128)S(1)} %get-tuple-element.180), channel_id=1, source_target_pairs={{0,8},{2,10},{4,12},{6,14},{8,0},{10,2},{12,4},{14,6},{16,24},{18,... | collective-permute-start | bytes 393224 | tf_op jit(solution)/shard_map/ppermute | solution.py:405
  42.5 7.1 %collective-permute-start.18 = (f32[256,128]{1,0:T(8,128)S(1)}, f32[256,128]{1,0:T(8,128)S(1)}, u32[]{:S(2)}, u32[]{:S(2)}) collective-permute-start(f32[256,128]{1,0:T(8,128)S(1)} %get-tuple-element.184), channel_id=1, source_target_pairs={{0,12},{2,14},{4,8},{6,10},{8,4},{10,6},{12,0},{14,2},{16,28},{18,... | collective-permute-start | bytes 393224 | tf_op jit(solution)/shard_map/ppermute | solution.py:405
  49.7 7.1 %collective-permute-start.19 = (f32[256,128]{1,0:T(8,128)S(1)}, f32[256,128]{1,0:T(8,128)S(1)}, u32[]{:S(2)}, u32[]{:S(2)}) collective-permute-start(f32[256,128]{1,0:T(8,128)S(1)} %add_add_fusion), channel_id=1, source_target_pairs={{0,16},{2,18},{4,20},{6,22},{8,24},{10,26},{12,28},{14,30},{16,0},... | collective-permute-start | bytes 393224 | tf_op jit(solution)/shard_map/ppermute | solution.py:400
  56.9 7.1 %collective-permute-start.21 = (f32[256,128]{1,0:T(8,128)S(1)}, f32[256,128]{1,0:T(8,128)S(1)}, u32[]{:S(2)}, u32[]{:S(2)}) collective-permute-start(f32[256,128]{1,0:T(8,128)S(1)} %get-tuple-element.217), channel_id=1, source_target_pairs={{0,4},{2,6},{4,0},{6,2},{8,12},{10,14},{12,8},{14,10},{16,20},{18,... | collective-permute-start | bytes 393224 | tf_op jit(solution)/shard_map/ppermute | solution.py:405
  57.6 6.4 %collective-permute-start.22 = (f32[256,128]{1,0:T(8,128)S(1)}, f32[256,128]{1,0:T(8,128)S(1)}, u32[]{:S(2)}, u32[]{:S(2)}) collective-permute-start(f32[256,128]{1,0:T(8,128)S(1)} %get-tuple-element.218), channel_id=1, source_target_pairs={{0,8},{2,10},{4,12},{6,14},{8,0},{10,2},{12,4},{14,6},{16,24},{18,... | collective-permute-start | bytes 393224 | tf_op jit(solution)/shard_map/ppermute | solution.py:405
  57.8 6.9 %collective-permute-start.23 = (f32[256,128]{1,0:T(8,128)S(1)}, f32[256,128]{1,0:T(8,128)S(1)}, u32[]{:S(2)}, u32[]{:S(2)}) collective-permute-start(f32[256,128]{1,0:T(8,128)S(1)} %get-tuple-element.219), channel_id=1, source_target_pairs={{0,12},{2,14},{4,8},{6,10},{8,4},{10,6},{12,0},{14,2},{16,28},{18,... | collective-permute-start | bytes 393224 | tf_op jit(solution)/shard_map/ppermute | solution.py:405
  60.4 5.6 %collective-permute-start.20 = (f32[256,128]{1,0:T(8,128)S(1)}, f32[256,128]{1,0:T(8,128)S(1)}, u32[]{:S(2)}, u32[]{:S(2)}) collective-permute-start(f32[256,128]{1,0:T(8,128)S(1)} %shard_map.108), channel_id=1, source_target_pairs={{0,2},{2,0},{4,6},{6,4},{8,10},{10,8},{12,14},{14,12},{16,18},{18,... | collective-permute-start | bytes 393224 | tf_op jit(solution)/shard_map/ppermute | solution.py:400
  64.9 1.4 %collective-permute-start.24 = (f32[256,128]{1,0:T(8,128)S(1)}, f32[256,128]{1,0:T(8,128)S(1)}, u32[]{:S(2)}, u32[]{:S(2)}) collective-permute-start(f32[256,128]{1,0:T(8,128)S(1)} %shard_map.109), channel_id=1, source_target_pairs={{0,2},{2,0},{4,6},{6,4},{8,10},{10,8},{12,14},{14,12},{16,18},{18,... | collective-permute-start | bytes 393224 | tf_op jit(solution)/shard_map/ppermute | solution.py:400
  65.0 1.5 %collective-permute-start.25 = (f32[256,128]{1,0:T(8,128)S(1)}, f32[256,128]{1,0:T(8,128)S(1)}, u32[]{:S(2)}, u32[]{:S(2)}) collective-permute-start(f32[256,128]{1,0:T(8,128)S(1)} %shard_map.110), channel_id=1, source_target_pairs={{0,2},{2,0},{4,6},{6,4},{8,10},{10,8},{12,14},{14,12},{16,18},{18,... | collective-permute-start | bytes 393224 | tf_op jit(solution)/shard_map/ppermute | solution.py:400
  65.5 1.3 %collective-permute-start.26 = (f32[256,128]{1,0:T(8,128)S(1)}, f32[256,128]{1,0:T(8,128)S(1)}, u32[]{:S(2)}, u32[]{:S(2)}) collective-permute-start(f32[256,128]{1,0:T(8,128)S(1)} %shard_map.111), channel_id=1, source_target_pairs={{0,2},{2,0},{4,6},{6,4},{8,10},{10,8},{12,14},{14,12},{16,18},{18,... | collective-permute-start | bytes 393224 | tf_op jit(solution)/shard_map/ppermute | solution.py:400

commit v5 on v4

--- a/solution.py
+++ b/solution.py
@@ -13,7 +13,7 @@
 QUAD = 4
 SECTIONS = ((1, 2), (3, 0))
 GATHER = ((0, 1, 2, 3), (0, 1, 2, 3))
-HAND = ((0, 1, 2, 3), (0, 1, 2, 3))
+HAND = ((0, 1, 2, 3), (0, 3, 1, 2))
 CHUNKS = 1
 BATCH = 4
 F32 = jnp.float32
@@ -590,7 +590,7 @@
         return thunk
 
     thunks = [inner(where) for where in groups]
-    pieces, made = carried(plan, sums, early_gates, ([], thunks[:1], thunks[1:]), True)
+    pieces, made = carried(plan, sums, early_gates, (thunks[:1], thunks[1:], []), True)
     made = dict(zip(groups, made))
     where = (0, 1)
     state_scratch = pltpu.VMEM((plan.span, DH), BF16)

time: 68.4 us -> 67.7 us (0.990)
  waiting for transfers between devices: 26.3 us -> 25.4 us
  transfers between devices with their start and end apart: 27 -> 27, of which waited for: 19 -> 16; matrix products, arithmetic and copies ran while one was open for 0% -> 0% of each run, Pallas kernels for 19% -> 19%
where the time goes in v5:
time: 67.7 us; the launch traced here: 67.5 us
  waiting for transfers between devices  25.4 us (38%)
  starting transfers between devices  23.9 us (35%)
  Pallas kernels  16.9 us (25%)
  between operations  1.14 us (2%)
    pallas_call x30, Pallas kernels, run(): pl.pallas_call(kernel, out_shape=out_shape, scratch_shapes=list(scratch),...  16.9 us
    ppermute x12, waiting for transfers between devices, quad_swap(): lax.ppermute(x, 'ctx', [(i, i ^ 2 * orders[i % 2][slot]) for i in range(c...  16.2 us
    ppermute x12, starting transfers between devices, quad_swap(): lax.ppermute(x, 'ctx', [(i, i ^ 2 * orders[i % 2][slot]) for i in range(c...  15.3 us
    ppermute x14, starting transfers between devices, swap(): return lax.ppermute(x, 'ctx', [(i, i ^ distance) for i in range(count)])  7.23 us
    ppermute x14, waiting for transfers between devices, swap(): return lax.ppermute(x, 'ctx', [(i, i ^ distance) for i in range(count)])  6.92 us
    ppermute x1, waiting for transfers between devices, head_total(): return (sums, lax.ppermute(sums, 'head', [(0, 1), (1, 0)]))  2.31 us
    ppermute x1, starting transfers between devices, head_total(): return (sums, lax.ppermute(sums, 'head', [(0, 1), (1, 0)]))  1.42 us
  transfers between devices with their start and end apart: 27, of which 16 were waited for; matrix products, arithmetic and copies ran while one was open for 0% of the time, Pallas kernels for 19%

profile of v5, /device:TPU:0, one launch (start us, length us, event | category | flops | bytes accessed | tf_op | source)
XLA Modules:
  0.0 67.5 jit_solution(12874841598285752583)
XLA Ops:
  0.6 1.5 %shard_map.84 = (bf16[192,2048]{1,0:T(8,128)(2,1)S(1)}, bf16[192,2048]{1,0:T(8,128)(2,1)S(1)}, f32[512,128]{1,0:T(8,128)S(1)}) custom-call(bf16[192,2048]{1,0:T(8,128)(2,1)} %k_hbm.1, bf16[192,2048]{1,0:T(8,128)(2,1)} %v_hbm.1), custom_call_target="tpu_custom_call" | custom-call | tf_op jit(solution)/shard_map/pallas_call | solution.py:119
  2.1 0.5 collective-permute-start
  2.6 0.3 shard_map.87
  2.9 0.1 collective-permute-start.1
  3.1 0.4 shard_map.85.keep_ref
  3.5 0.3 collective-permute-done.got_ref.refs_4_
  3.8 0.6 shard_map.86
  4.4 0.0 copy-start.1
  4.5 0.0 copy-start
  4.5 2.9 %collective-permute-start.2 = (f32[256,128]{1,0:T(8,128)S(1)}, f32[256,128]{1,0:T(8,128)S(1)}, u32[]{:S(2)}, u32[]{:S(2)}) collective-permute-start(f32[256,128]{1,0:T(8,128)S(1)} %get-tuple-element.128), channel_id=1, source_target_pairs={{0,4},{2,6},{4,0},{6,2},{8,12},{10,14},{12,8},{14,10},{16,20},{18,... | collective-permute-start | bytes 393224 | tf_op jit(solution)/shard_map/ppermute | solution.py:405
  7.4 1.6 %collective-permute-start.3 = (f32[256,128]{1,0:T(8,128)S(1)}, f32[256,128]{1,0:T(8,128)S(1)}, u32[]{:S(2)}, u32[]{:S(2)}) collective-permute-start(f32[256,128]{1,0:T(8,128)S(1)} %get-tuple-element.129), channel_id=1, source_target_pairs={{0,8},{2,10},{4,12},{6,14},{8,0},{10,2},{12,4},{14,6},{16,24},{18,... | collective-permute-start | bytes 393224 | tf_op jit(solution)/shard_map/ppermute | solution.py:405
  9.0 0.1 collective-permute-start.4
  9.1 1.5 %collective-permute-done.2.refs_1_ = f32[256,128]{1,0:T(8,128)S(1)} collective-permute-done((f32[256,128]{1,0:T(8,128)S(1)}, f32[256,128]{1,0:T(8,128)S(1)}, u32[]{:S(2)}, u32[]{:S(2)}) %collective-permute-start.2) | collective-permute-done | bytes 131104 | tf_op jit(solution)/shard_map/ppermute | solution.py:405
  10.6 2.9 %collective-permute-done.3.refs_2_ = f32[256,128]{1,0:T(8,128)S(1)} collective-permute-done((f32[256,128]{1,0:T(8,128)S(1)}, f32[256,128]{1,0:T(8,128)S(1)}, u32[]{:S(2)}, u32[]{:S(2)}) %collective-permute-start.3) | collective-permute-done | bytes 131104 | tf_op jit(solution)/shard_map/ppermute | solution.py:405
  13.4 1.5 %collective-permute-done.4.refs_3_ = f32[256,128]{1,0:T(8,128)S(1)} collective-permute-done((f32[256,128]{1,0:T(8,128)S(1)}, f32[256,128]{1,0:T(8,128)S(1)}, u32[]{:S(2)}, u32[]{:S(2)}) %collective-permute-start.4) | collective-permute-done | bytes 131104 | tf_op jit(solution)/shard_map/ppermute | solution.py:405
  15.0 2.8 %collective-permute-start.5 = (f32[256,128]{1,0:T(8,128)S(1)}, f32[256,128]{1,0:T(8,128)S(1)}, u32[]{:S(2)}, u32[]{:S(2)}) collective-permute-start(f32[256,128]{1,0:T(8,128)S(1)} %add_add_fusion.1), channel_id=1, source_target_pairs={{0,16},{2,18},{4,20},{6,22},{8,24},{10,26},{12,28},{14,30},{16,0},... | collective-permute-start | bytes 393224 | tf_op jit(solution)/shard_map/ppermute | solution.py:400
  17.8 1.1 %shard_map.91 = (bf16[192,1024]{1,0:T(8,128)(2,1)S(1)}, f32[192,1024]{1,0:T(8,128)S(1)}, bf16[192,1024]{1,0:T(8,128)(2,1)S(1)}, bf16[8,192,192]{2,1,0:T(8,128)(2...) custom-call(bf16[192,2048]{1,0:T(8,128)(2,1)S(1)} %copy-done.1, ...), custom_call_target="tpu_custom_call" | custom-call | tf_op jit(solution)/shard_map/pallas_call | solution.py:119
  18.9 1.1 %shard_map.90 = (bf16[192,1024]{1,0:T(8,128)(2,1)S(1)}, f32[192,1024]{1,0:T(8,128)S(1)}, bf16[192,1024]{1,0:T(8,128)(2,1)S(1)}, bf16[8,192,192]{2,1,0:T(8,128)(2...) custom-call(bf16[192,2048]{1,0:T(8,128)(2,1)S(1)} %copy-done.1, ...), custom_call_target="tpu_custom_call" | custom-call | tf_op jit(solution)/shard_map/pallas_call | solution.py:119
  20.1 3.0 %collective-permute-done.5.refs_4_ = f32[256,128]{1,0:T(8,128)S(1)} collective-permute-done((f32[256,128]{1,0:T(8,128)S(1)}, f32[256,128]{1,0:T(8,128)S(1)}, u32[]{:S(2)}, u32[]{:S(2)}) %collective-permute-start.5) | collective-permute-done | bytes 131104 | tf_op jit(solution)/shard_map/ppermute | solution.py:400
  23.1 0.1 shard_map.92
  23.2 0.7 collective-permute-start.6
  23.9 0.7 collective-permute-start.7
  24.6 2.2 %collective-permute-start.8 = (f32[256,128]{1,0:T(8,128)S(1)}, f32[256,128]{1,0:T(8,128)S(1)}, u32[]{:S(2)}, u32[]{:S(2)}) collective-permute-start(f32[256,128]{1,0:T(8,128)S(1)} %get-tuple-element.155), channel_id=1, source_target_pairs={{0,12},{2,10},{4,8},{6,14},{8,4},{10,2},{12,0},{14,6},{16,28},{18,... | collective-permute-start | bytes 393224 | tf_op jit(solution)/shard_map/ppermute | solution.py:405
  26.8 0.1 collective-permute-start.9
  26.9 2.7 %collective-permute-done.6.refs_1_.piece_ref = f32[256,128]{1,0:T(8,128)S(1)} collective-permute-done((f32[256,128]{1,0:T(8,128)S(1)}, f32[256,128]{1,0:T(8,128)S(1)}, u32[]{:S(2)}, u32[]{:S(2)}) %collective-permute-start.6) | collective-permute-done | bytes 131104 | tf_op jit(solution)/shard_map/ppermute | solution.py:405
  29.6 0.1 collective-permute-start.10
  29.7 0.0 collective-permute-done.7.refs_2_.piece_ref
  29.7 0.5 collective-permute-start.11
  30.3 1.6 %collective-permute-done.8.refs_3_.piece_ref = f32[256,128]{1,0:T(8,128)S(1)} collective-permute-done((f32[256,128]{1,0:T(8,128)S(1)}, f32[256,128]{1,0:T(8,128)S(1)}, u32[]{:S(2)}, u32[]{:S(2)}) %collective-permute-start.8) | collective-permute-done | bytes 131104 | tf_op jit(solution)/shard_map/ppermute | solution.py:405
  31.9 0.1 collective-permute-start.12
  31.9 0.4 shard_map.93
  32.4 0.9 %collective-permute-done.12.refs_3_ = f32[256,128]{1,0:T(8,128)S(1)} collective-permute-done((f32[256,128]{1,0:T(8,128)S(1)}, f32[256,128]{1,0:T(8,128)S(1)}, u32[]{:S(2)}, u32[]{:S(2)}) %collective-permute-start.12) | collective-permute-done | bytes 131104 | tf_op jit(solution)/shard_map/ppermute | solution.py:400
  33.3 0.5 shard_map.98
  33.8 1.4 %collective-permute-start.13 = (f32[8,192]{1,0:T(8,128)S(1)}, f32[8,192]{1,0:T(8,128)S(1)}, u32[]{:S(2)}, u32[]{:S(2)}) collective-permute-start(f32[8,192]{1,0:T(8,128)S(1)} %get-tuple-element.159.a_ref), channel_id=1, source_target_pairs={{0,1},{1,0},{2,3},{3,2},{4,5},{5,4},{6,7},{7,6},{8,9},{9,8},{10,11... | collective-permute-start | bytes 18440 | tf_op jit(solution)/shard_map/ppermute | solution.py:478
  35.2 2.3 %collective-permute-done.13.b_ref = f32[8,192]{1,0:T(8,128)S(1)} collective-permute-done((f32[8,192]{1,0:T(8,128)S(1)}, f32[8,192]{1,0:T(8,128)S(1)}, u32[]{:S(2)}, u32[]{:S(2)}) %collective-permute-start.13) | collective-permute-done | bytes 6176 | tf_op jit(solution)/shard_map/ppermute | solution.py:478
  37.5 0.7 %shard_map.99 = (bf16[192,1024]{1,0:T(8,128)(2,1)S(1)}, f32[512,128]{1,0:T(8,128)S(1)}, f32[192,128]{1,0:T(8,128)S(1)}, f32[192,128]{1,0:T(8,128)S(1)}) custom-call(f32[8,192]{1,0:T(8,128)S(1)} %get-tuple-element.159.a_ref, f32[8,192]{1,0:T(8,128)S(1)} %collective-permute-done.13.b_ref, f32[192,1024]{1,0:T(8,128)S(1)} %get-tuple-element.192.att_ref.refs_0_.refs_6_, ...), custom_call_target="tpu_custom_call" | custom-call | tf_op jit(solution)/shard_map/pallas_call | solution.py:119
  38.2 0.1 collective-permute-start.14
  38.3 0.3 shard_map.102
  38.6 0.5 collective-permute-start.15
  39.1 0.4 shard_map.100
  39.5 0.3 collective-permute-done.14.got_ref.refs_4_
  39.8 0.6 shard_map.101
  40.4 0.4 collective-permute-start.16
  40.8 1.7 %collective-permute-start.17 = (f32[256,128]{1,0:T(8,128)S(1)}, f32[256,128]{1,0:T(8,128)S(1)}, u32[]{:S(2)}, u32[]{:S(2)}) collective-permute-start(f32[256,128]{1,0:T(8,128)S(1)} %get-tuple-element.180), channel_id=1, source_target_pairs={{0,8},{2,10},{4,12},{6,14},{8,0},{10,2},{12,4},{14,6},{16,24},{18,... | collective-permute-start | bytes 393224 | tf_op jit(solution)/shard_map/ppermute | solution.py:405
  42.5 1.6 %collective-permute-start.18 = (f32[256,128]{1,0:T(8,128)S(1)}, f32[256,128]{1,0:T(8,128)S(1)}, u32[]{:S(2)}, u32[]{:S(2)}) collective-permute-start(f32[256,128]{1,0:T(8,128)S(1)} %get-tuple-element.184), channel_id=1, source_target_pairs={{0,12},{2,14},{4,8},{6,10},{8,4},{10,6},{12,0},{14,2},{16,28},{18,... | collective-permute-start | bytes 393224 | tf_op jit(solution)/shard_map/ppermute | solution.py:405
  44.1 3.2 %shard_map.105 = (bf16[192,2048]{1,0:T(8,128)(2,1)}, bf16[192,2048]{1,0:T(8,128)(2,1)}, f32[192,1024]{1,0:T(8,128)S(1)}, f32[192,1024]{1,0:T(8,128)S(1)}) custom-call(bf16[1024,128]{1,0:T(8,128)(2,1)S(1)} %get-tuple-element.186.refs_0_, f32[192,128]{1,0:T(8,128)S(1)} %get-tuple-element.204.a_ref.inv_ref.refs_1_, ...), custom_call_target="tpu_custom_call" | custom-call | tf_op jit(solution)/shard_map/pallas_call | solution.py:119
  47.3 2.1 %collective-permute-done.18.refs_3_ = f32[256,128]{1,0:T(8,128)S(1)} collective-permute-done((f32[256,128]{1,0:T(8,128)S(1)}, f32[256,128]{1,0:T(8,128)S(1)}, u32[]{:S(2)}, u32[]{:S(2)}) %collective-permute-start.18) | collective-permute-done | bytes 131104 | tf_op jit(solution)/shard_map/ppermute | solution.py:405
  49.5 2.1 %collective-permute-start.19 = (f32[256,128]{1,0:T(8,128)S(1)}, f32[256,128]{1,0:T(8,128)S(1)}, u32[]{:S(2)}, u32[]{:S(2)}) collective-permute-start(f32[256,128]{1,0:T(8,128)S(1)} %add_add_fusion), channel_id=1, source_target_pairs={{0,16},{2,18},{4,20},{6,22},{8,24},{10,26},{12,28},{14,30},{16,0},... | collective-permute-start | bytes 393224 | tf_op jit(solution)/shard_map/ppermute | solution.py:400
  51.6 3.4 %shard_map.106 = (bf16[192,2048]{1,0:T(8,128)(2,1)}, bf16[192,2048]{1,0:T(8,128)(2,1)}, f32[192,1024]{1,0:T(8,128)S(1)}, f32[192,1024]{1,0:T(8,128)S(1)}) custom-call(bf16[1024,128]{1,0:T(8,128)(2,1)S(1)} %get-tuple-element.203.refs_0_, f32[192,128]{1,0:T(8,128)S(1)} %get-tuple-element.204.a_ref.inv_ref.refs_1_, ...), custom_call_target="tpu_custom_call", output_to_operand_aliasing={{0}: (12, {}), {1}: (13, {})} | custom-call | tf_op jit(solution)/shard_map/pallas_call | solution.py:119
  55.0 1.6 %collective-permute-done.19.refs_4_ = f32[256,128]{1,0:T(8,128)S(1)} collective-permute-done((f32[256,128]{1,0:T(8,128)S(1)}, f32[256,128]{1,0:T(8,128)S(1)}, u32[]{:S(2)}, u32[]{:S(2)}) %collective-permute-start.19) | collective-permute-done | bytes 131104 | tf_op jit(solution)/shard_map/ppermute | solution.py:400
  56.6 0.1 shard_map.107
  56.7 0.6 collective-permute-start.21
  57.4 0.3 collective-permute-start.23
  57.7 2.6 %collective-permute-start.25 = (f32[256,128]{1,0:T(8,128)S(1)}, f32[256,128]{1,0:T(8,128)S(1)}, u32[]{:S(2)}, u32[]{:S(2)}) collective-permute-start(f32[256,128]{1,0:T(8,128)S(1)} %get-tuple-element.224), channel_id=1, source_target_pairs={{0,12},{2,10},{4,8},{6,14},{8,4},{10,2},{12,0},{14,6},{16,28},{18,... | collective-permute-start | bytes 393224 | tf_op jit(solution)/shard_map/ppermute | solution.py:405
  60.3 0.1 collective-permute-start.20
  60.4 1.4 %collective-permute-done.21.piece_ref.refs_1_ = f32[256,128]{1,0:T(8,128)S(1)} collective-permute-done((f32[256,128]{1,0:T(8,128)S(1)}, f32[256,128]{1,0:T(8,128)S(1)}, u32[]{:S(2)}, u32[]{:S(2)}) %collective-permute-start.21) | collective-permute-done | bytes 131104 | tf_op jit(solution)/shard_map/ppermute | solution.py:405
  61.8 0.1 collective-permute-start.22
  61.9 0.5 collective-permute-done.23.piece_ref.refs_2_
  62.4 0.1 collective-permute-start.24
  62.5 2.2 %collective-permute-done.25.piece_ref.refs_3_ = f32[256,128]{1,0:T(8,128)S(1)} collective-permute-done((f32[256,128]{1,0:T(8,128)S(1)}, f32[256,128]{1,0:T(8,128)S(1)}, u32[]{:S(2)}, u32[]{:S(2)}) %collective-permute-start.25) | collective-permute-done | bytes 131104 | tf_op jit(solution)/shard_map/ppermute | solution.py:405
  64.7 0.1 collective-permute-start.26
  64.7 0.5 shard_map.112
  65.3 0.8 %collective-permute-done.26.refs_3_ = f32[256,128]{1,0:T(8,128)S(1)} collective-permute-done((f32[256,128]{1,0:T(8,128)S(1)}, f32[256,128]{1,0:T(8,128)S(1)}, u32[]{:S(2)}, u32[]{:S(2)}) %collective-permute-start.26) | collective-permute-done | bytes 131104 | tf_op jit(solution)/shard_map/ppermute | solution.py:400
  66.1 1.3 %shard_map.113 = (bf16[192,2048]{1,0:T(8,128)(2,1)}, bf16[192,2048]{1,0:T(8,128)(2,1)}) custom-call(f32[256,128]{1,0:T(8,128)S(1)} %collective-permute-done.20.refs_0_, f32[256,128]{1,0:T(8,128)S(1)} %collective-permute-done.22.refs_1_, f32[256,128]{1,0:T(8,128)S(1)} %collective-permute-done.24.refs_2_, f32[256,128]{1,0:T(8,128)S(1)} %collective-permute-done.26.refs_3_, ...), custom_call_target="tpu_custom_call" | custom-call | tf_op jit(solution)/shard_map/pallas_call | solution.py:119
  (28 shorter events, 0.4 us)
Async XLA Ops:
  2.1 1.7 %collective-permute-start = (f32[512,128]{1,0:T(8,128)S(1)}, f32[512,128]{1,0:T(8,128)S(1)}, u32[]{:S(2)}, u32[]{:S(2)}) collective-permute-start(f32[512,128]{1,0:T(8,128)S(1)} %get-tuple-element.119), channel_id=1, source_target_pairs={{0,2},{2,0},{4,6},{6,4},{8,10},{10,8},{12,14},{14,12},{16,18},{18,... | collective-permute-start | bytes 786440 | tf_op jit(solution)/shard_map/ppermute | solution.py:400
  2.9 6.0 %collective-permute-start.1 = (f32[512,128]{1,0:T(8,128)S(1)}, f32[512,128]{1,0:T(8,128)S(1)}, u32[]{:S(2)}, u32[]{:S(2)}) collective-permute-start(f32[512,128]{1,0:T(8,128)S(1)} %shard_map.87), channel_id=1, source_target_pairs={{0,2},{2,0},{4,6},{6,4},{8,10},{10,8},{12,14},{14,12},{16,18},{18,... | collective-permute-start | bytes 786440 | tf_op jit(solution)/shard_map/ppermute | solution.py:400
  3.8 14.0 %copy-start.2 = (bf16[192,2048]{1,0:T(8,128)(2,1)S(1)}, bf16[192,2048]{1,0:T(8,128)(2,1)}, u32[]{:S(2)}) copy-start(bf16[192,2048]{1,0:T(8,128)(2,1)} %cot_ref.1) | copy-start | bytes 2359300
  4.4 13.4 %copy-start.1 = (bf16[192,2048]{1,0:T(8,128)(2,1)S(1)}, bf16[192,2048]{1,0:T(8,128)(2,1)}, u32[]{:S(2)}) copy-start(bf16[192,2048]{1,0:T(8,128)(2,1)} %refs_8_.1) | copy-start | bytes 2359300
  4.5 13.4 %copy-start = (bf16[192,2048]{1,0:T(8,128)(2,1)S(1)}, bf16[192,2048]{1,0:T(8,128)(2,1)}, u32[]{:S(2)}) copy-start(bf16[192,2048]{1,0:T(8,128)(2,1)} %refs_10_.1) | copy-start | bytes 2359300
  4.5 6.1 %collective-permute-start.2 = (f32[256,128]{1,0:T(8,128)S(1)}, f32[256,128]{1,0:T(8,128)S(1)}, u32[]{:S(2)}, u32[]{:S(2)}) collective-permute-start(f32[256,128]{1,0:T(8,128)S(1)} %get-tuple-element.128), channel_id=1, source_target_pairs={{0,4},{2,6},{4,0},{6,2},{8,12},{10,14},{12,8},{14,10},{16,20},{18,... | collective-permute-start | bytes 393224 | tf_op jit(solution)/shard_map/ppermute | solution.py:405
  7.4 6.0 %collective-permute-start.3 = (f32[256,128]{1,0:T(8,128)S(1)}, f32[256,128]{1,0:T(8,128)S(1)}, u32[]{:S(2)}, u32[]{:S(2)}) collective-permute-start(f32[256,128]{1,0:T(8,128)S(1)} %get-tuple-element.129), channel_id=1, source_target_pairs={{0,8},{2,10},{4,12},{6,14},{8,0},{10,2},{12,4},{14,6},{16,24},{18,... | collective-permute-start | bytes 393224 | tf_op jit(solution)/shard_map/ppermute | solution.py:405
  9.0 5.9 %collective-permute-start.4 = (f32[256,128]{1,0:T(8,128)S(1)}, f32[256,128]{1,0:T(8,128)S(1)}, u32[]{:S(2)}, u32[]{:S(2)}) collective-permute-start(f32[256,128]{1,0:T(8,128)S(1)} %get-tuple-element.133), channel_id=1, source_target_pairs={{0,12},{2,14},{4,8},{6,10},{8,4},{10,6},{12,0},{14,2},{16,28},{18,... | collective-permute-start | bytes 393224 | tf_op jit(solution)/shard_map/ppermute | solution.py:405
  15.0 8.1 %collective-permute-start.5 = (f32[256,128]{1,0:T(8,128)S(1)}, f32[256,128]{1,0:T(8,128)S(1)}, u32[]{:S(2)}, u32[]{:S(2)}) collective-permute-start(f32[256,128]{1,0:T(8,128)S(1)} %add_add_fusion.1), channel_id=1, source_target_pairs={{0,16},{2,18},{4,20},{6,22},{8,24},{10,26},{12,28},{14,30},{16,0},... | collective-permute-start | bytes 393224 | tf_op jit(solution)/shard_map/ppermute | solution.py:400
  23.2 6.3 %collective-permute-start.6 = (f32[256,128]{1,0:T(8,128)S(1)}, f32[256,128]{1,0:T(8,128)S(1)}, u32[]{:S(2)}, u32[]{:S(2)}) collective-permute-start(f32[256,128]{1,0:T(8,128)S(1)} %get-tuple-element.153), channel_id=1, source_target_pairs={{0,4},{2,14},{4,0},{6,10},{8,12},{10,6},{12,8},{14,2},{16,20},{18,... | collective-permute-start | bytes 393224 | tf_op jit(solution)/shard_map/ppermute | solution.py:405
  23.9 5.8 %collective-permute-start.7 = (f32[256,128]{1,0:T(8,128)S(1)}, f32[256,128]{1,0:T(8,128)S(1)}, u32[]{:S(2)}, u32[]{:S(2)}) collective-permute-start(f32[256,128]{1,0:T(8,128)S(1)} %get-tuple-element.154), channel_id=1, source_target_pairs={{0,8},{2,6},{4,12},{6,2},{8,0},{10,14},{12,4},{14,10},{16,24},{18,... | collective-permute-start | bytes 393224 | tf_op jit(solution)/shard_map/ppermute | solution.py:405
  24.6 7.3 %collective-permute-start.8 = (f32[256,128]{1,0:T(8,128)S(1)}, f32[256,128]{1,0:T(8,128)S(1)}, u32[]{:S(2)}, u32[]{:S(2)}) collective-permute-start(f32[256,128]{1,0:T(8,128)S(1)} %get-tuple-element.155), channel_id=1, source_target_pairs={{0,12},{2,10},{4,8},{6,14},{8,4},{10,2},{12,0},{14,6},{16,28},{18,... | collective-permute-start | bytes 393224 | tf_op jit(solution)/shard_map/ppermute | solution.py:405
  26.8 5.5 %collective-permute-start.9 = (f32[256,128]{1,0:T(8,128)S(1)}, f32[256,128]{1,0:T(8,128)S(1)}, u32[]{:S(2)}, u32[]{:S(2)}) collective-permute-start(f32[256,128]{1,0:T(8,128)S(1)} %shard_map.94), channel_id=1, source_target_pairs={{0,2},{2,0},{4,6},{6,4},{8,10},{10,8},{12,14},{14,12},{16,18},{18,... | collective-permute-start | bytes 393224 | tf_op jit(solution)/shard_map/ppermute | solution.py:400
  29.6 2.8 %collective-permute-start.10 = (f32[256,128]{1,0:T(8,128)S(1)}, f32[256,128]{1,0:T(8,128)S(1)}, u32[]{:S(2)}, u32[]{:S(2)}) collective-permute-start(f32[256,128]{1,0:T(8,128)S(1)} %shard_map.95), channel_id=1, source_target_pairs={{0,2},{2,0},{4,6},{6,4},{8,10},{10,8},{12,14},{14,12},{16,18},{18,... | collective-permute-start | bytes 393224 | tf_op jit(solution)/shard_map/ppermute | solution.py:400
  29.7 2.6 %collective-permute-start.11 = (f32[256,128]{1,0:T(8,128)S(1)}, f32[256,128]{1,0:T(8,128)S(1)}, u32[]{:S(2)}, u32[]{:S(2)}) collective-permute-start(f32[256,128]{1,0:T(8,128)S(1)} %shard_map.96), channel_id=1, source_target_pairs={{0,2},{2,0},{4,6},{6,4},{8,10},{10,8},{12,14},{14,12},{16,18},{18,... | collective-permute-start | bytes 393224 | tf_op jit(solution)/shard_map/ppermute | solution.py:400
  31.9 1.4 %collective-permute-start.12 = (f32[256,128]{1,0:T(8,128)S(1)}, f32[256,128]{1,0:T(8,128)S(1)}, u32[]{:S(2)}, u32[]{:S(2)}) collective-permute-start(f32[256,128]{1,0:T(8,128)S(1)} %shard_map.97), channel_id=1, source_target_pairs={{0,2},{2,0},{4,6},{6,4},{8,10},{10,8},{12,14},{14,12},{16,18},{18,... | collective-permute-start | bytes 393224 | tf_op jit(solution)/shard_map/ppermute | solution.py:400
  33.8 3.7 %collective-permute-start.13 = (f32[8,192]{1,0:T(8,128)S(1)}, f32[8,192]{1,0:T(8,128)S(1)}, u32[]{:S(2)}, u32[]{:S(2)}) collective-permute-start(f32[8,192]{1,0:T(8,128)S(1)} %get-tuple-element.159.a_ref), channel_id=1, source_target_pairs={{0,1},{1,0},{2,3},{3,2},{4,5},{5,4},{6,7},{7,6},{8,9},{9,8},{10,11... | collective-permute-start | bytes 18440 | tf_op jit(solution)/shard_map/ppermute | solution.py:478
  38.2 1.6 %collective-permute-start.14 = (f32[512,128]{1,0:T(8,128)S(1)}, f32[512,128]{1,0:T(8,128)S(1)}, u32[]{:S(2)}, u32[]{:S(2)}) collective-permute-start(f32[512,128]{1,0:T(8,128)S(1)} %get-tuple-element.165), channel_id=1, source_target_pairs={{0,2},{2,0},{4,6},{6,4},{8,10},{10,8},{12,14},{14,12},{16,18},{18,... | collective-permute-start | bytes 786440 | tf_op jit(solution)/shard_map/ppermute | solution.py:400
  38.6 3.9 %collective-permute-start.15 = (f32[512,128]{1,0:T(8,128)S(1)}, f32[512,128]{1,0:T(8,128)S(1)}, u32[]{:S(2)}, u32[]{:S(2)}) collective-permute-start(f32[512,128]{1,0:T(8,128)S(1)} %shard_map.102), channel_id=1, source_target_pairs={{0,2},{2,0},{4,6},{6,4},{8,10},{10,8},{12,14},{14,12},{16,18},{18,... | collective-permute-start | bytes 786440 | tf_op jit(solution)/shard_map/ppermute | solution.py:400
  40.4 6.9 %collective-permute-start.16 = (f32[256,128]{1,0:T(8,128)S(1)}, f32[256,128]{1,0:T(8,128)S(1)}, u32[]{:S(2)}, u32[]{:S(2)}) collective-permute-start(f32[256,128]{1,0:T(8,128)S(1)} %get-tuple-element.179), channel_id=1, source_target_pairs={{0,4},{2,6},{4,0},{6,2},{8,12},{10,14},{12,8},{14,10},{16,20},{18,... | collective-permute-start | bytes 393224 | tf_op jit(solution)/shard_map/ppermute | solution.py:405
  40.8 6.5 %collective-permute-start.17 = (f32[256,128]{1,0:T(8,128)S(1)}, f32[256,128]{1,0:T(8,128)S(1)}, u32[]{:S(2)}, u32[]{:S(2)}) collective-permute-start(f32[256,128]{1,0:T(8,128)S(1)} %get-tuple-element.180), channel_id=1, source_target_pairs={{0,8},{2,10},{4,12},{6,14},{8,0},{10,2},{12,4},{14,6},{16,24},{18,... | collective-permute-start | bytes 393224 | tf_op jit(solution)/shard_map/ppermute | solution.py:405
  42.5 6.9 %collective-permute-start.18 = (f32[256,128]{1,0:T(8,128)S(1)}, f32[256,128]{1,0:T(8,128)S(1)}, u32[]{:S(2)}, u32[]{:S(2)}) collective-permute-start(f32[256,128]{1,0:T(8,128)S(1)} %get-tuple-element.184), channel_id=1, source_target_pairs={{0,12},{2,14},{4,8},{6,10},{8,4},{10,6},{12,0},{14,2},{16,28},{18,... | collective-permute-start | bytes 393224 | tf_op jit(solution)/shard_map/ppermute | solution.py:405
  49.5 7.1 %collective-permute-start.19 = (f32[256,128]{1,0:T(8,128)S(1)}, f32[256,128]{1,0:T(8,128)S(1)}, u32[]{:S(2)}, u32[]{:S(2)}) collective-permute-start(f32[256,128]{1,0:T(8,128)S(1)} %add_add_fusion), channel_id=1, source_target_pairs={{0,16},{2,18},{4,20},{6,22},{8,24},{10,26},{12,28},{14,30},{16,0},... | collective-permute-start | bytes 393224 | tf_op jit(solution)/shard_map/ppermute | solution.py:400
  56.7 5.0 %collective-permute-start.21 = (f32[256,128]{1,0:T(8,128)S(1)}, f32[256,128]{1,0:T(8,128)S(1)}, u32[]{:S(2)}, u32[]{:S(2)}) collective-permute-start(f32[256,128]{1,0:T(8,128)S(1)} %get-tuple-element.222), channel_id=1, source_target_pairs={{0,4},{2,14},{4,0},{6,10},{8,12},{10,6},{12,8},{14,2},{16,20},{18,... | collective-permute-start | bytes 393224 | tf_op jit(solution)/shard_map/ppermute | solution.py:405
  57.4 5.0 %collective-permute-start.23 = (f32[256,128]{1,0:T(8,128)S(1)}, f32[256,128]{1,0:T(8,128)S(1)}, u32[]{:S(2)}, u32[]{:S(2)}) collective-permute-start(f32[256,128]{1,0:T(8,128)S(1)} %get-tuple-element.223), channel_id=1, source_target_pairs={{0,8},{2,6},{4,12},{6,2},{8,0},{10,14},{12,4},{14,10},{16,24},{18,... | collective-permute-start | bytes 393224 | tf_op jit(solution)/shard_map/ppermute | solution.py:405
  57.7 6.9 %collective-permute-start.25 = (f32[256,128]{1,0:T(8,128)S(1)}, f32[256,128]{1,0:T(8,128)S(1)}, u32[]{:S(2)}, u32[]{:S(2)}) collective-permute-start(f32[256,128]{1,0:T(8,128)S(1)} %get-tuple-element.224), channel_id=1, source_target_pairs={{0,12},{2,10},{4,8},{6,14},{8,4},{10,2},{12,0},{14,6},{16,28},{18,... | collective-permute-start | bytes 393224 | tf_op jit(solution)/shard_map/ppermute | solution.py:405
  60.3 5.0 %collective-permute-start.20 = (f32[256,128]{1,0:T(8,128)S(1)}, f32[256,128]{1,0:T(8,128)S(1)}, u32[]{:S(2)}, u32[]{:S(2)}) collective-permute-start(f32[256,128]{1,0:T(8,128)S(1)} %shard_map.108), channel_id=1, source_target_pairs={{0,2},{2,0},{4,6},{6,4},{8,10},{10,8},{12,14},{14,12},{16,18},{18,... | collective-permute-start | bytes 393224 | tf_op jit(solution)/shard_map/ppermute | solution.py:400
  61.8 3.5 %collective-permute-start.22 = (f32[256,128]{1,0:T(8,128)S(1)}, f32[256,128]{1,0:T(8,128)S(1)}, u32[]{:S(2)}, u32[]{:S(2)}) collective-permute-start(f32[256,128]{1,0:T(8,128)S(1)} %shard_map.109), channel_id=1, source_target_pairs={{0,2},{2,0},{4,6},{6,4},{8,10},{10,8},{12,14},{14,12},{16,18},{18,... | collective-permute-start | bytes 393224 | tf_op jit(solution)/shard_map/ppermute | solution.py:400
  62.4 2.9 %collective-permute-start.24 = (f32[256,128]{1,0:T(8,128)S(1)}, f32[256,128]{1,0:T(8,128)S(1)}, u32[]{:S(2)}, u32[]{:S(2)}) collective-permute-start(f32[256,128]{1,0:T(8,128)S(1)} %shard_map.110), channel_id=1, source_target_pairs={{0,2},{2,0},{4,6},{6,4},{8,10},{10,8},{12,14},{14,12},{16,18},{18,... | collective-permute-start | bytes 393224 | tf_op jit(solution)/shard_map/ppermute | solution.py:400
  64.7 1.4 %collective-permute-start.26 = (f32[256,128]{1,0:T(8,128)S(1)}, f32[256,128]{1,0:T(8,128)S(1)}, u32[]{:S(2)}, u32[]{:S(2)}) collective-permute-start(f32[256,128]{1,0:T(8,128)S(1)} %shard_map.111), channel_id=1, source_target_pairs={{0,2},{2,0},{4,6},{6,4},{8,10},{10,8},{12,14},{14,12},{16,18},{18,... | collective-permute-start | bytes 393224 | tf_op jit(solution)/shard_map/ppermute | solution.py:400

commit v6 on v5

--- a/solution.py
+++ b/solution.py
@@ -271,9 +271,15 @@
         inv = 1.0 / jnp.sqrt(sumsq * (1.0 / (H * DH)) + EPSILON)
         coef = raw * inv * (1.0 / (H * DH)) * inv * inv
         line = lax.broadcasted_iota(jnp.int32, total.shape, 0)
-        rows = jnp.where(line == 0, inv, jnp.where(line == 1, coef, 0.0))
-        pick = chooser(8, 2 * DH)
-        both = sum(dot(term, pick, 0, 0) for term in thirds(rows))
+        packed = jnp.zeros_like(total)
+        for n, pair in enumerate(zip(thirds(inv), thirds(coef))):
+            for m, term in enumerate(pair):
+                packed = jnp.where(line == 2 * n + m, term.astype(F32), packed)
+        shape = (8, 2 * DH)
+        parity = lax.rem(lax.broadcasted_iota(jnp.int32, shape, 0), 2)
+        side = lax.broadcasted_iota(jnp.int32, shape, 1) // DH
+        pick = jnp.where(parity == side, 1.0, 0.0).astype(BF16)
+        both = dot(packed.astype(BF16), pick, 0, 0)
         inv, coef = both[:, :DH], both[:, DH:]
         more[0][...] = inv
         more[1][...] = coef

time: 67.7 us -> 67.5 us (level)
  no operation moved by 1% of the time
where the time goes in v6:
time: 67.5 us; the launch traced here: 67.4 us
  waiting for transfers between devices  25.4 us (38%)
  starting transfers between devices  24 us (36%)
  Pallas kernels  16.8 us (25%)
  between operations  1.14 us (2%)
    pallas_call x30, Pallas kernels, run(): pl.pallas_call(kernel, out_shape=out_shape, scratch_shapes=list(scratch),...  16.8 us
    ppermute x12, waiting for transfers between devices, quad_swap(): lax.ppermute(x, 'ctx', [(i, i ^ 2 * orders[i % 2][slot]) for i in range(c...  16.2 us
    ppermute x12, starting transfers between devices, quad_swap(): lax.ppermute(x, 'ctx', [(i, i ^ 2 * orders[i % 2][slot]) for i in range(c...  15.3 us
    ppermute x14, starting transfers between devices, swap(): return lax.ppermute(x, 'ctx', [(i, i ^ distance) for i in range(count)])  7.23 us
    ppermute x14, waiting for transfers between devices, swap(): return lax.ppermute(x, 'ctx', [(i, i ^ distance) for i in range(count)])  6.92 us
    ppermute x1, waiting for transfers between devices, head_total(): return (sums, lax.ppermute(sums, 'head', [(0, 1), (1, 0)]))  2.31 us
    ppermute x1, starting transfers between devices, head_total(): return (sums, lax.ppermute(sums, 'head', [(0, 1), (1, 0)]))  1.42 us
  transfers between devices with their start and end apart: 27, of which 16 were waited for; matrix products, arithmetic and copies ran while one was open for 0% of the time, Pallas kernels for 19%

profile of v6, /device:TPU:0, one launch (start us, length us, event | category | flops | bytes accessed | tf_op | source)
XLA Modules:
  0.0 67.4 jit_solution(12231788305834983818)
XLA Ops:
  0.6 1.5 %shard_map.84 = (bf16[192,2048]{1,0:T(8,128)(2,1)S(1)}, bf16[192,2048]{1,0:T(8,128)(2,1)S(1)}, f32[512,128]{1,0:T(8,128)S(1)}) custom-call(bf16[192,2048]{1,0:T(8,128)(2,1)} %k_hbm.1, bf16[192,2048]{1,0:T(8,128)(2,1)} %v_hbm.1), custom_call_target="tpu_custom_call" | custom-call | tf_op jit(solution)/shard_map/pallas_call | solution.py:119
  2.1 0.5 collective-permute-start
  2.6 0.3 shard_map.87
  2.9 0.1 collective-permute-start.1
  3.1 0.4 shard_map.85.keep_ref
  3.5 0.3 collective-permute-done.got_ref.refs_4_
  3.8 0.6 shard_map.86
  4.4 0.0 copy-start.1
  4.5 0.0 copy-start
  4.5 2.9 %collective-permute-start.2 = (f32[256,128]{1,0:T(8,128)S(1)}, f32[256,128]{1,0:T(8,128)S(1)}, u32[]{:S(2)}, u32[]{:S(2)}) collective-permute-start(f32[256,128]{1,0:T(8,128)S(1)} %get-tuple-element.128), channel_id=1, source_target_pairs={{0,4},{2,6},{4,0},{6,2},{8,12},{10,14},{12,8},{14,10},{16,20},{18,... | collective-permute-start | bytes 393224 | tf_op jit(solution)/shard_map/ppermute | solution.py:411
  7.4 1.6 %collective-permute-start.3 = (f32[256,128]{1,0:T(8,128)S(1)}, f32[256,128]{1,0:T(8,128)S(1)}, u32[]{:S(2)}, u32[]{:S(2)}) collective-permute-start(f32[256,128]{1,0:T(8,128)S(1)} %get-tuple-element.129), channel_id=1, source_target_pairs={{0,8},{2,10},{4,12},{6,14},{8,0},{10,2},{12,4},{14,6},{16,24},{18,... | collective-permute-start | bytes 393224 | tf_op jit(solution)/shard_map/ppermute | solution.py:411
  9.0 0.0 collective-permute-done.1.got_ref.refs_5_
  9.0 0.1 collective-permute-start.4
  9.1 1.5 %collective-permute-done.2.refs_1_ = f32[256,128]{1,0:T(8,128)S(1)} collective-permute-done((f32[256,128]{1,0:T(8,128)S(1)}, f32[256,128]{1,0:T(8,128)S(1)}, u32[]{:S(2)}, u32[]{:S(2)}) %collective-permute-start.2) | collective-permute-done | bytes 131104 | tf_op jit(solution)/shard_map/ppermute | solution.py:411
  10.6 2.9 %collective-permute-done.3.refs_2_ = f32[256,128]{1,0:T(8,128)S(1)} collective-permute-done((f32[256,128]{1,0:T(8,128)S(1)}, f32[256,128]{1,0:T(8,128)S(1)}, u32[]{:S(2)}, u32[]{:S(2)}) %collective-permute-start.3) | collective-permute-done | bytes 131104 | tf_op jit(solution)/shard_map/ppermute | solution.py:411
  13.4 1.5 %collective-permute-done.4.refs_3_ = f32[256,128]{1,0:T(8,128)S(1)} collective-permute-done((f32[256,128]{1,0:T(8,128)S(1)}, f32[256,128]{1,0:T(8,128)S(1)}, u32[]{:S(2)}, u32[]{:S(2)}) %collective-permute-start.4) | collective-permute-done | bytes 131104 | tf_op jit(solution)/shard_map/ppermute | solution.py:411
  15.0 2.8 %collective-permute-start.5 = (f32[256,128]{1,0:T(8,128)S(1)}, f32[256,128]{1,0:T(8,128)S(1)}, u32[]{:S(2)}, u32[]{:S(2)}) collective-permute-start(f32[256,128]{1,0:T(8,128)S(1)} %add_add_fusion.1), channel_id=1, source_target_pairs={{0,16},{2,18},{4,20},{6,22},{8,24},{10,26},{12,28},{14,30},{16,0},... | collective-permute-start | bytes 393224 | tf_op jit(solution)/shard_map/ppermute | solution.py:406
  17.8 1.1 %shard_map.91 = (bf16[192,1024]{1,0:T(8,128)(2,1)S(1)}, f32[192,1024]{1,0:T(8,128)S(1)}, bf16[192,1024]{1,0:T(8,128)(2,1)S(1)}, bf16[8,192,192]{2,1,0:T(8,128)(2...) custom-call(bf16[192,2048]{1,0:T(8,128)(2,1)S(1)} %copy-done.1, ...), custom_call_target="tpu_custom_call" | custom-call | tf_op jit(solution)/shard_map/pallas_call | solution.py:119
  18.9 1.1 %shard_map.90 = (bf16[192,1024]{1,0:T(8,128)(2,1)S(1)}, f32[192,1024]{1,0:T(8,128)S(1)}, bf16[192,1024]{1,0:T(8,128)(2,1)S(1)}, bf16[8,192,192]{2,1,0:T(8,128)(2...) custom-call(bf16[192,2048]{1,0:T(8,128)(2,1)S(1)} %copy-done.1, ...), custom_call_target="tpu_custom_call" | custom-call | tf_op jit(solution)/shard_map/pallas_call | solution.py:119
  20.1 3.0 %collective-permute-done.5.refs_4_ = f32[256,128]{1,0:T(8,128)S(1)} collective-permute-done((f32[256,128]{1,0:T(8,128)S(1)}, f32[256,128]{1,0:T(8,128)S(1)}, u32[]{:S(2)}, u32[]{:S(2)}) %collective-permute-start.5) | collective-permute-done | bytes 131104 | tf_op jit(solution)/shard_map/ppermute | solution.py:406
  23.1 0.1 shard_map.92
  23.2 0.7 collective-permute-start.6
  23.9 0.7 collective-permute-start.7
  24.6 2.2 %collective-permute-start.8 = (f32[256,128]{1,0:T(8,128)S(1)}, f32[256,128]{1,0:T(8,128)S(1)}, u32[]{:S(2)}, u32[]{:S(2)}) collective-permute-start(f32[256,128]{1,0:T(8,128)S(1)} %get-tuple-element.155), channel_id=1, source_target_pairs={{0,12},{2,10},{4,8},{6,14},{8,4},{10,2},{12,0},{14,6},{16,28},{18,... | collective-permute-start | bytes 393224 | tf_op jit(solution)/shard_map/ppermute | solution.py:411
  26.8 0.1 collective-permute-start.9
  26.9 2.7 %collective-permute-done.6.refs_1_.piece_ref = f32[256,128]{1,0:T(8,128)S(1)} collective-permute-done((f32[256,128]{1,0:T(8,128)S(1)}, f32[256,128]{1,0:T(8,128)S(1)}, u32[]{:S(2)}, u32[]{:S(2)}) %collective-permute-start.6) | collective-permute-done | bytes 131104 | tf_op jit(solution)/shard_map/ppermute | solution.py:411
  29.6 0.1 collective-permute-start.10
  29.7 0.5 collective-permute-start.11
  30.3 1.6 %collective-permute-done.8.refs_3_.piece_ref = f32[256,128]{1,0:T(8,128)S(1)} collective-permute-done((f32[256,128]{1,0:T(8,128)S(1)}, f32[256,128]{1,0:T(8,128)S(1)}, u32[]{:S(2)}, u32[]{:S(2)}) %collective-permute-start.8) | collective-permute-done | bytes 131104 | tf_op jit(solution)/shard_map/ppermute | solution.py:411
  31.9 0.1 collective-permute-start.12
  31.9 0.4 shard_map.93
  32.4 0.9 %collective-permute-done.12.refs_3_ = f32[256,128]{1,0:T(8,128)S(1)} collective-permute-done((f32[256,128]{1,0:T(8,128)S(1)}, f32[256,128]{1,0:T(8,128)S(1)}, u32[]{:S(2)}, u32[]{:S(2)}) %collective-permute-start.12) | collective-permute-done | bytes 131104 | tf_op jit(solution)/shard_map/ppermute | solution.py:406
  33.3 0.5 shard_map.98
  33.8 1.4 %collective-permute-start.13 = (f32[8,192]{1,0:T(8,128)S(1)}, f32[8,192]{1,0:T(8,128)S(1)}, u32[]{:S(2)}, u32[]{:S(2)}) collective-permute-start(f32[8,192]{1,0:T(8,128)S(1)} %get-tuple-element.159.a_ref), channel_id=1, source_target_pairs={{0,1},{1,0},{2,3},{3,2},{4,5},{5,4},{6,7},{7,6},{8,9},{9,8},{10,11... | collective-permute-start | bytes 18440 | tf_op jit(solution)/shard_map/ppermute | solution.py:484
  35.2 2.3 %collective-permute-done.13.b_ref = f32[8,192]{1,0:T(8,128)S(1)} collective-permute-done((f32[8,192]{1,0:T(8,128)S(1)}, f32[8,192]{1,0:T(8,128)S(1)}, u32[]{:S(2)}, u32[]{:S(2)}) %collective-permute-start.13) | collective-permute-done | bytes 6176 | tf_op jit(solution)/shard_map/ppermute | solution.py:484
  37.5 0.6 shard_map.99
  38.1 0.1 collective-permute-start.14
  38.1 0.3 shard_map.102
  38.5 0.5 collective-permute-start.15
  39.0 0.4 shard_map.100
  39.4 0.3 collective-permute-done.14.got_ref.refs_4_
  39.7 0.6 shard_map.101
  40.3 0.4 collective-permute-start.16
  40.7 1.7 %collective-permute-start.17 = (f32[256,128]{1,0:T(8,128)S(1)}, f32[256,128]{1,0:T(8,128)S(1)}, u32[]{:S(2)}, u32[]{:S(2)}) collective-permute-start(f32[256,128]{1,0:T(8,128)S(1)} %get-tuple-element.180), channel_id=1, source_target_pairs={{0,8},{2,10},{4,12},{6,14},{8,0},{10,2},{12,4},{14,6},{16,24},{18,... | collective-permute-start | bytes 393224 | tf_op jit(solution)/shard_map/ppermute | solution.py:411
  42.4 1.6 %collective-permute-start.18 = (f32[256,128]{1,0:T(8,128)S(1)}, f32[256,128]{1,0:T(8,128)S(1)}, u32[]{:S(2)}, u32[]{:S(2)}) collective-permute-start(f32[256,128]{1,0:T(8,128)S(1)} %get-tuple-element.184), channel_id=1, source_target_pairs={{0,12},{2,14},{4,8},{6,10},{8,4},{10,6},{12,0},{14,2},{16,28},{18,... | collective-permute-start | bytes 393224 | tf_op jit(solution)/shard_map/ppermute | solution.py:411
  44.0 3.2 %shard_map.105 = (bf16[192,2048]{1,0:T(8,128)(2,1)}, bf16[192,2048]{1,0:T(8,128)(2,1)}, f32[192,1024]{1,0:T(8,128)S(1)}, f32[192,1024]{1,0:T(8,128)S(1)}) custom-call(bf16[1024,128]{1,0:T(8,128)(2,1)S(1)} %get-tuple-element.186.refs_0_, f32[192,128]{1,0:T(8,128)S(1)} %get-tuple-element.204.a_ref.inv_ref.refs_1_, ...), custom_call_target="tpu_custom_call" | custom-call | tf_op jit(solution)/shard_map/pallas_call | solution.py:119
  47.2 2.1 %collective-permute-done.18.refs_3_ = f32[256,128]{1,0:T(8,128)S(1)} collective-permute-done((f32[256,128]{1,0:T(8,128)S(1)}, f32[256,128]{1,0:T(8,128)S(1)}, u32[]{:S(2)}, u32[]{:S(2)}) %collective-permute-start.18) | collective-permute-done | bytes 131104 | tf_op jit(solution)/shard_map/ppermute | solution.py:411
  49.3 2.1 %collective-permute-start.19 = (f32[256,128]{1,0:T(8,128)S(1)}, f32[256,128]{1,0:T(8,128)S(1)}, u32[]{:S(2)}, u32[]{:S(2)}) collective-permute-start(f32[256,128]{1,0:T(8,128)S(1)} %add_add_fusion), channel_id=1, source_target_pairs={{0,16},{2,18},{4,20},{6,22},{8,24},{10,26},{12,28},{14,30},{16,0},... | collective-permute-start | bytes 393224 | tf_op jit(solution)/shard_map/ppermute | solution.py:406
  51.4 3.4 %shard_map.106 = (bf16[192,2048]{1,0:T(8,128)(2,1)}, bf16[192,2048]{1,0:T(8,128)(2,1)}, f32[192,1024]{1,0:T(8,128)S(1)}, f32[192,1024]{1,0:T(8,128)S(1)}) custom-call(bf16[1024,128]{1,0:T(8,128)(2,1)S(1)} %get-tuple-element.203.refs_0_, f32[192,128]{1,0:T(8,128)S(1)} %get-tuple-element.204.a_ref.inv_ref.refs_1_, ...), custom_call_target="tpu_custom_call", output_to_operand_aliasing={{0}: (12, {}), {1}: (13, {})} | custom-call | tf_op jit(solution)/shard_map/pallas_call | solution.py:119
  54.8 1.6 %collective-permute-done.19.refs_4_ = f32[256,128]{1,0:T(8,128)S(1)} collective-permute-done((f32[256,128]{1,0:T(8,128)S(1)}, f32[256,128]{1,0:T(8,128)S(1)}, u32[]{:S(2)}, u32[]{:S(2)}) %collective-permute-start.19) | collective-permute-done | bytes 131104 | tf_op jit(solution)/shard_map/ppermute | solution.py:406
  56.4 0.1 shard_map.107
  56.6 0.6 collective-permute-start.21
  57.2 0.3 collective-permute-start.23
  57.6 2.6 %collective-permute-start.25 = (f32[256,128]{1,0:T(8,128)S(1)}, f32[256,128]{1,0:T(8,128)S(1)}, u32[]{:S(2)}, u32[]{:S(2)}) collective-permute-start(f32[256,128]{1,0:T(8,128)S(1)} %get-tuple-element.224), channel_id=1, source_target_pairs={{0,12},{2,10},{4,8},{6,14},{8,4},{10,2},{12,0},{14,6},{16,28},{18,... | collective-permute-start | bytes 393224 | tf_op jit(solution)/shard_map/ppermute | solution.py:411
  60.2 0.1 collective-permute-start.20
  60.3 1.4 %collective-permute-done.21.piece_ref.refs_1_ = f32[256,128]{1,0:T(8,128)S(1)} collective-permute-done((f32[256,128]{1,0:T(8,128)S(1)}, f32[256,128]{1,0:T(8,128)S(1)}, u32[]{:S(2)}, u32[]{:S(2)}) %collective-permute-start.21) | collective-permute-done | bytes 131104 | tf_op jit(solution)/shard_map/ppermute | solution.py:411
  61.7 0.1 collective-permute-start.22
  61.7 0.5 collective-permute-done.23.piece_ref.refs_2_
  62.2 0.1 collective-permute-start.24
  62.3 2.2 %collective-permute-done.25.piece_ref.refs_3_ = f32[256,128]{1,0:T(8,128)S(1)} collective-permute-done((f32[256,128]{1,0:T(8,128)S(1)}, f32[256,128]{1,0:T(8,128)S(1)}, u32[]{:S(2)}, u32[]{:S(2)}) %collective-permute-start.25) | collective-permute-done | bytes 131104 | tf_op jit(solution)/shard_map/ppermute | solution.py:411
  64.5 0.1 collective-permute-start.26
  64.6 0.5 shard_map.112
  65.2 0.8 %collective-permute-done.26.refs_3_ = f32[256,128]{1,0:T(8,128)S(1)} collective-permute-done((f32[256,128]{1,0:T(8,128)S(1)}, f32[256,128]{1,0:T(8,128)S(1)}, u32[]{:S(2)}, u32[]{:S(2)}) %collective-permute-start.26) | collective-permute-done | bytes 131104 | tf_op jit(solution)/shard_map/ppermute | solution.py:406
  65.9 1.3 %shard_map.113 = (bf16[192,2048]{1,0:T(8,128)(2,1)}, bf16[192,2048]{1,0:T(8,128)(2,1)}) custom-call(f32[256,128]{1,0:T(8,128)S(1)} %collective-permute-done.20.refs_0_, f32[256,128]{1,0:T(8,128)S(1)} %collective-permute-done.22.refs_1_, f32[256,128]{1,0:T(8,128)S(1)} %collective-permute-done.24.refs_2_, f32[256,128]{1,0:T(8,128)S(1)} %collective-permute-done.26.refs_3_, ...), custom_call_target="tpu_custom_call" | custom-call | tf_op jit(solution)/shard_map/pallas_call | solution.py:119
  (28 shorter events, 0.4 us)
Async XLA Ops:
  2.1 1.7 %collective-permute-start = (f32[512,128]{1,0:T(8,128)S(1)}, f32[512,128]{1,0:T(8,128)S(1)}, u32[]{:S(2)}, u32[]{:S(2)}) collective-permute-start(f32[512,128]{1,0:T(8,128)S(1)} %get-tuple-element.119), channel_id=1, source_target_pairs={{0,2},{2,0},{4,6},{6,4},{8,10},{10,8},{12,14},{14,12},{16,18},{18,... | collective-permute-start | bytes 786440 | tf_op jit(solution)/shard_map/ppermute | solution.py:406
  2.9 6.0 %collective-permute-start.1 = (f32[512,128]{1,0:T(8,128)S(1)}, f32[512,128]{1,0:T(8,128)S(1)}, u32[]{:S(2)}, u32[]{:S(2)}) collective-permute-start(f32[512,128]{1,0:T(8,128)S(1)} %shard_map.87), channel_id=1, source_target_pairs={{0,2},{2,0},{4,6},{6,4},{8,10},{10,8},{12,14},{14,12},{16,18},{18,... | collective-permute-start | bytes 786440 | tf_op jit(solution)/shard_map/ppermute | solution.py:406
  3.8 14.0 %copy-start.2 = (bf16[192,2048]{1,0:T(8,128)(2,1)S(1)}, bf16[192,2048]{1,0:T(8,128)(2,1)}, u32[]{:S(2)}) copy-start(bf16[192,2048]{1,0:T(8,128)(2,1)} %cot_ref.1) | copy-start | bytes 2359300
  4.4 13.4 %copy-start.1 = (bf16[192,2048]{1,0:T(8,128)(2,1)S(1)}, bf16[192,2048]{1,0:T(8,128)(2,1)}, u32[]{:S(2)}) copy-start(bf16[192,2048]{1,0:T(8,128)(2,1)} %refs_8_.1) | copy-start | bytes 2359300
  4.5 13.4 %copy-start = (bf16[192,2048]{1,0:T(8,128)(2,1)S(1)}, bf16[192,2048]{1,0:T(8,128)(2,1)}, u32[]{:S(2)}) copy-start(bf16[192,2048]{1,0:T(8,128)(2,1)} %refs_10_.1) | copy-start | bytes 2359300
  4.5 6.1 %collective-permute-start.2 = (f32[256,128]{1,0:T(8,128)S(1)}, f32[256,128]{1,0:T(8,128)S(1)}, u32[]{:S(2)}, u32[]{:S(2)}) collective-permute-start(f32[256,128]{1,0:T(8,128)S(1)} %get-tuple-element.128), channel_id=1, source_target_pairs={{0,4},{2,6},{4,0},{6,2},{8,12},{10,14},{12,8},{14,10},{16,20},{18,... | collective-permute-start | bytes 393224 | tf_op jit(solution)/shard_map/ppermute | solution.py:411
  7.4 6.0 %collective-permute-start.3 = (f32[256,128]{1,0:T(8,128)S(1)}, f32[256,128]{1,0:T(8,128)S(1)}, u32[]{:S(2)}, u32[]{:S(2)}) collective-permute-start(f32[256,128]{1,0:T(8,128)S(1)} %get-tuple-element.129), channel_id=1, source_target_pairs={{0,8},{2,10},{4,12},{6,14},{8,0},{10,2},{12,4},{14,6},{16,24},{18,... | collective-permute-start | bytes 393224 | tf_op jit(solution)/shard_map/ppermute | solution.py:411
  9.0 5.9 %collective-permute-start.4 = (f32[256,128]{1,0:T(8,128)S(1)}, f32[256,128]{1,0:T(8,128)S(1)}, u32[]{:S(2)}, u32[]{:S(2)}) collective-permute-start(f32[256,128]{1,0:T(8,128)S(1)} %get-tuple-element.133), channel_id=1, source_target_pairs={{0,12},{2,14},{4,8},{6,10},{8,4},{10,6},{12,0},{14,2},{16,28},{18,... | collective-permute-start | bytes 393224 | tf_op jit(solution)/shard_map/ppermute | solution.py:411
  15.0 8.1 %collective-permute-start.5 = (f32[256,128]{1,0:T(8,128)S(1)}, f32[256,128]{1,0:T(8,128)S(1)}, u32[]{:S(2)}, u32[]{:S(2)}) collective-permute-start(f32[256,128]{1,0:T(8,128)S(1)} %add_add_fusion.1), channel_id=1, source_target_pairs={{0,16},{2,18},{4,20},{6,22},{8,24},{10,26},{12,28},{14,30},{16,0},... | collective-permute-start | bytes 393224 | tf_op jit(solution)/shard_map/ppermute | solution.py:406
  23.2 6.3 %collective-permute-start.6 = (f32[256,128]{1,0:T(8,128)S(1)}, f32[256,128]{1,0:T(8,128)S(1)}, u32[]{:S(2)}, u32[]{:S(2)}) collective-permute-start(f32[256,128]{1,0:T(8,128)S(1)} %get-tuple-element.153), channel_id=1, source_target_pairs={{0,4},{2,14},{4,0},{6,10},{8,12},{10,6},{12,8},{14,2},{16,20},{18,... | collective-permute-start | bytes 393224 | tf_op jit(solution)/shard_map/ppermute | solution.py:411
  23.9 5.8 %collective-permute-start.7 = (f32[256,128]{1,0:T(8,128)S(1)}, f32[256,128]{1,0:T(8,128)S(1)}, u32[]{:S(2)}, u32[]{:S(2)}) collective-permute-start(f32[256,128]{1,0:T(8,128)S(1)} %get-tuple-element.154), channel_id=1, source_target_pairs={{0,8},{2,6},{4,12},{6,2},{8,0},{10,14},{12,4},{14,10},{16,24},{18,... | collective-permute-start | bytes 393224 | tf_op jit(solution)/shard_map/ppermute | solution.py:411
  24.6 7.3 %collective-permute-start.8 = (f32[256,128]{1,0:T(8,128)S(1)}, f32[256,128]{1,0:T(8,128)S(1)}, u32[]{:S(2)}, u32[]{:S(2)}) collective-permute-start(f32[256,128]{1,0:T(8,128)S(1)} %get-tuple-element.155), channel_id=1, source_target_pairs={{0,12},{2,10},{4,8},{6,14},{8,4},{10,2},{12,0},{14,6},{16,28},{18,... | collective-permute-start | bytes 393224 | tf_op jit(solution)/shard_map/ppermute | solution.py:411
  26.8 5.5 %collective-permute-start.9 = (f32[256,128]{1,0:T(8,128)S(1)}, f32[256,128]{1,0:T(8,128)S(1)}, u32[]{:S(2)}, u32[]{:S(2)}) collective-permute-start(f32[256,128]{1,0:T(8,128)S(1)} %shard_map.94), channel_id=1, source_target_pairs={{0,2},{2,0},{4,6},{6,4},{8,10},{10,8},{12,14},{14,12},{16,18},{18,... | collective-permute-start | bytes 393224 | tf_op jit(solution)/shard_map/ppermute | solution.py:406
  29.6 2.8 %collective-permute-start.10 = (f32[256,128]{1,0:T(8,128)S(1)}, f32[256,128]{1,0:T(8,128)S(1)}, u32[]{:S(2)}, u32[]{:S(2)}) collective-permute-start(f32[256,128]{1,0:T(8,128)S(1)} %shard_map.95), channel_id=1, source_target_pairs={{0,2},{2,0},{4,6},{6,4},{8,10},{10,8},{12,14},{14,12},{16,18},{18,... | collective-permute-start | bytes 393224 | tf_op jit(solution)/shard_map/ppermute | solution.py:406
  29.7 2.6 %collective-permute-start.11 = (f32[256,128]{1,0:T(8,128)S(1)}, f32[256,128]{1,0:T(8,128)S(1)}, u32[]{:S(2)}, u32[]{:S(2)}) collective-permute-start(f32[256,128]{1,0:T(8,128)S(1)} %shard_map.96), channel_id=1, source_target_pairs={{0,2},{2,0},{4,6},{6,4},{8,10},{10,8},{12,14},{14,12},{16,18},{18,... | collective-permute-start | bytes 393224 | tf_op jit(solution)/shard_map/ppermute | solution.py:406
  31.9 1.4 %collective-permute-start.12 = (f32[256,128]{1,0:T(8,128)S(1)}, f32[256,128]{1,0:T(8,128)S(1)}, u32[]{:S(2)}, u32[]{:S(2)}) collective-permute-start(f32[256,128]{1,0:T(8,128)S(1)} %shard_map.97), channel_id=1, source_target_pairs={{0,2},{2,0},{4,6},{6,4},{8,10},{10,8},{12,14},{14,12},{16,18},{18,... | collective-permute-start | bytes 393224 | tf_op jit(solution)/shard_map/ppermute | solution.py:406
  33.8 3.7 %collective-permute-start.13 = (f32[8,192]{1,0:T(8,128)S(1)}, f32[8,192]{1,0:T(8,128)S(1)}, u32[]{:S(2)}, u32[]{:S(2)}) collective-permute-start(f32[8,192]{1,0:T(8,128)S(1)} %get-tuple-element.159.a_ref), channel_id=1, source_target_pairs={{0,1},{1,0},{2,3},{3,2},{4,5},{5,4},{6,7},{7,6},{8,9},{9,8},{10,11... | collective-permute-start | bytes 18440 | tf_op jit(solution)/shard_map/ppermute | solution.py:484
  38.1 1.6 %collective-permute-start.14 = (f32[512,128]{1,0:T(8,128)S(1)}, f32[512,128]{1,0:T(8,128)S(1)}, u32[]{:S(2)}, u32[]{:S(2)}) collective-permute-start(f32[512,128]{1,0:T(8,128)S(1)} %get-tuple-element.165), channel_id=1, source_target_pairs={{0,2},{2,0},{4,6},{6,4},{8,10},{10,8},{12,14},{14,12},{16,18},{18,... | collective-permute-start | bytes 786440 | tf_op jit(solution)/shard_map/ppermute | solution.py:406
  38.5 3.9 %collective-permute-start.15 = (f32[512,128]{1,0:T(8,128)S(1)}, f32[512,128]{1,0:T(8,128)S(1)}, u32[]{:S(2)}, u32[]{:S(2)}) collective-permute-start(f32[512,128]{1,0:T(8,128)S(1)} %shard_map.102), channel_id=1, source_target_pairs={{0,2},{2,0},{4,6},{6,4},{8,10},{10,8},{12,14},{14,12},{16,18},{18,... | collective-permute-start | bytes 786440 | tf_op jit(solution)/shard_map/ppermute | solution.py:406
  40.3 6.9 %collective-permute-start.16 = (f32[256,128]{1,0:T(8,128)S(1)}, f32[256,128]{1,0:T(8,128)S(1)}, u32[]{:S(2)}, u32[]{:S(2)}) collective-permute-start(f32[256,128]{1,0:T(8,128)S(1)} %get-tuple-element.179), channel_id=1, source_target_pairs={{0,4},{2,6},{4,0},{6,2},{8,12},{10,14},{12,8},{14,10},{16,20},{18,... | collective-permute-start | bytes 393224 | tf_op jit(solution)/shard_map/ppermute | solution.py:411
  40.7 6.5 %collective-permute-start.17 = (f32[256,128]{1,0:T(8,128)S(1)}, f32[256,128]{1,0:T(8,128)S(1)}, u32[]{:S(2)}, u32[]{:S(2)}) collective-permute-start(f32[256,128]{1,0:T(8,128)S(1)} %get-tuple-element.180), channel_id=1, source_target_pairs={{0,8},{2,10},{4,12},{6,14},{8,0},{10,2},{12,4},{14,6},{16,24},{18,... | collective-permute-start | bytes 393224 | tf_op jit(solution)/shard_map/ppermute | solution.py:411
  42.4 6.9 %collective-permute-start.18 = (f32[256,128]{1,0:T(8,128)S(1)}, f32[256,128]{1,0:T(8,128)S(1)}, u32[]{:S(2)}, u32[]{:S(2)}) collective-permute-start(f32[256,128]{1,0:T(8,128)S(1)} %get-tuple-element.184), channel_id=1, source_target_pairs={{0,12},{2,14},{4,8},{6,10},{8,4},{10,6},{12,0},{14,2},{16,28},{18,... | collective-permute-start | bytes 393224 | tf_op jit(solution)/shard_map/ppermute | solution.py:411
  49.3 7.1 %collective-permute-start.19 = (f32[256,128]{1,0:T(8,128)S(1)}, f32[256,128]{1,0:T(8,128)S(1)}, u32[]{:S(2)}, u32[]{:S(2)}) collective-permute-start(f32[256,128]{1,0:T(8,128)S(1)} %add_add_fusion), channel_id=1, source_target_pairs={{0,16},{2,18},{4,20},{6,22},{8,24},{10,26},{12,28},{14,30},{16,0},... | collective-permute-start | bytes 393224 | tf_op jit(solution)/shard_map/ppermute | solution.py:406
  56.6 5.0 %collective-permute-start.21 = (f32[256,128]{1,0:T(8,128)S(1)}, f32[256,128]{1,0:T(8,128)S(1)}, u32[]{:S(2)}, u32[]{:S(2)}) collective-permute-start(f32[256,128]{1,0:T(8,128)S(1)} %get-tuple-element.222), channel_id=1, source_target_pairs={{0,4},{2,14},{4,0},{6,10},{8,12},{10,6},{12,8},{14,2},{16,20},{18,... | collective-permute-start | bytes 393224 | tf_op jit(solution)/shard_map/ppermute | solution.py:411
  57.2 5.0 %collective-permute-start.23 = (f32[256,128]{1,0:T(8,128)S(1)}, f32[256,128]{1,0:T(8,128)S(1)}, u32[]{:S(2)}, u32[]{:S(2)}) collective-permute-start(f32[256,128]{1,0:T(8,128)S(1)} %get-tuple-element.223), channel_id=1, source_target_pairs={{0,8},{2,6},{4,12},{6,2},{8,0},{10,14},{12,4},{14,10},{16,24},{18,... | collective-permute-start | bytes 393224 | tf_op jit(solution)/shard_map/ppermute | solution.py:411
  57.6 6.9 %collective-permute-start.25 = (f32[256,128]{1,0:T(8,128)S(1)}, f32[256,128]{1,0:T(8,128)S(1)}, u32[]{:S(2)}, u32[]{:S(2)}) collective-permute-start(f32[256,128]{1,0:T(8,128)S(1)} %get-tuple-element.224), channel_id=1, source_target_pairs={{0,12},{2,10},{4,8},{6,14},{8,4},{10,2},{12,0},{14,6},{16,28},{18,... | collective-permute-start | bytes 393224 | tf_op jit(solution)/shard_map/ppermute | solution.py:411
  60.2 5.0 %collective-permute-start.20 = (f32[256,128]{1,0:T(8,128)S(1)}, f32[256,128]{1,0:T(8,128)S(1)}, u32[]{:S(2)}, u32[]{:S(2)}) collective-permute-start(f32[256,128]{1,0:T(8,128)S(1)} %shard_map.108), channel_id=1, source_target_pairs={{0,2},{2,0},{4,6},{6,4},{8,10},{10,8},{12,14},{14,12},{16,18},{18,... | collective-permute-start | bytes 393224 | tf_op jit(solution)/shard_map/ppermute | solution.py:406
  61.7 3.5 %collective-permute-start.22 = (f32[256,128]{1,0:T(8,128)S(1)}, f32[256,128]{1,0:T(8,128)S(1)}, u32[]{:S(2)}, u32[]{:S(2)}) collective-permute-start(f32[256,128]{1,0:T(8,128)S(1)} %shard_map.109), channel_id=1, source_target_pairs={{0,2},{2,0},{4,6},{6,4},{8,10},{10,8},{12,14},{14,12},{16,18},{18,... | collective-permute-start | bytes 393224 | tf_op jit(solution)/shard_map/ppermute | solution.py:406
  62.2 2.9 %collective-permute-start.24 = (f32[256,128]{1,0:T(8,128)S(1)}, f32[256,128]{1,0:T(8,128)S(1)}, u32[]{:S(2)}, u32[]{:S(2)}) collective-permute-start(f32[256,128]{1,0:T(8,128)S(1)} %shard_map.110), channel_id=1, source_target_pairs={{0,2},{2,0},{4,6},{6,4},{8,10},{10,8},{12,14},{14,12},{16,18},{18,... | collective-permute-start | bytes 393224 | tf_op jit(solution)/shard_map/ppermute | solution.py:406
  64.5 1.4 %collective-permute-start.26 = (f32[256,128]{1,0:T(8,128)S(1)}, f32[256,128]{1,0:T(8,128)S(1)}, u32[]{:S(2)}, u32[]{:S(2)}) collective-permute-start(f32[256,128]{1,0:T(8,128)S(1)} %shard_map.111), channel_id=1, source_target_pairs={{0,2},{2,0},{4,6},{6,4},{8,10},{10,8},{12,14},{14,12},{16,18},{18,... | collective-permute-start | bytes 393224 | tf_op jit(solution)/shard_map/ppermute | solution.py:406

commit v7 on v6

--- a/solution.py
+++ b/solution.py
@@ -250,9 +250,9 @@
         else:
             square, inner = square + att * att, inner + gated_ref[:, head(g)] * att
     if last:
-        pick = chooser(8, 2 * DH)
+        pick = jnp.concatenate([chooser(8, 2 * DH)] * 3, axis=1)
         terms = thirds(jnp.concatenate([square, inner], axis=1))
-        refs[2][...] = sum(dot(pick, term, 1, 1) for term in terms)
+        refs[2][...] = dot(pick, jnp.concatenate(terms, axis=1), 1, 1)
     else:
         refs[2][...] = square
         refs[3][...] = inner

time: 67.5 us -> 67.5 us (level)
  no operation moved by 1% of the time
where the time goes in v7:
time: 67.5 us; the launch traced here: 67.4 us
  waiting for transfers between devices  25.4 us (38%)
  starting transfers between devices  24 us (36%)
  Pallas kernels  16.8 us (25%)
  between operations  1.14 us (2%)
    pallas_call x30, Pallas kernels, run(): pl.pallas_call(kernel, out_shape=out_shape, scratch_shapes=list(scratch),...  16.8 us
    ppermute x12, waiting for transfers between devices, quad_swap(): lax.ppermute(x, 'ctx', [(i, i ^ 2 * orders[i % 2][slot]) for i in range(c...  16.2 us
    ppermute x12, starting transfers between devices, quad_swap(): lax.ppermute(x, 'ctx', [(i, i ^ 2 * orders[i % 2][slot]) for i in range(c...  15.3 us
    ppermute x14, starting transfers between devices, swap(): return lax.ppermute(x, 'ctx', [(i, i ^ distance) for i in range(count)])  7.23 us
    ppermute x14, waiting for transfers between devices, swap(): return lax.ppermute(x, 'ctx', [(i, i ^ distance) for i in range(count)])  6.91 us
    ppermute x1, waiting for transfers between devices, head_total(): return (sums, lax.ppermute(sums, 'head', [(0, 1), (1, 0)]))  2.31 us
    ppermute x1, starting transfers between devices, head_total(): return (sums, lax.ppermute(sums, 'head', [(0, 1), (1, 0)]))  1.43 us
  transfers between devices with their start and end apart: 27, of which 16 were waited for; matrix products, arithmetic and copies ran while one was open for 0% of the time, Pallas kernels for 19%

profile of v7, /device:TPU:0, one launch (start us, length us, event | category | flops | bytes accessed | tf_op | source)
XLA Modules:
  0.0 67.4 jit_solution(1882596727907639622)
XLA Ops:
  0.6 1.5 %shard_map.84 = (bf16[192,2048]{1,0:T(8,128)(2,1)S(1)}, bf16[192,2048]{1,0:T(8,128)(2,1)S(1)}, f32[512,128]{1,0:T(8,128)S(1)}) custom-call(bf16[192,2048]{1,0:T(8,128)(2,1)} %k_hbm.1, bf16[192,2048]{1,0:T(8,128)(2,1)} %v_hbm.1), custom_call_target="tpu_custom_call" | custom-call | tf_op jit(solution)/shard_map/pallas_call | solution.py:119
  2.1 0.5 collective-permute-start
  2.6 0.3 shard_map.87
  2.9 0.1 collective-permute-start.1
  3.1 0.4 shard_map.85.keep_ref
  3.5 0.3 collective-permute-done.got_ref.refs_4_
  3.8 0.6 shard_map.86
  4.4 0.0 copy-start.1
  4.5 0.0 copy-start
  4.5 2.9 %collective-permute-start.2 = (f32[256,128]{1,0:T(8,128)S(1)}, f32[256,128]{1,0:T(8,128)S(1)}, u32[]{:S(2)}, u32[]{:S(2)}) collective-permute-start(f32[256,128]{1,0:T(8,128)S(1)} %get-tuple-element.128), channel_id=1, source_target_pairs={{0,4},{2,6},{4,0},{6,2},{8,12},{10,14},{12,8},{14,10},{16,20},{18,... | collective-permute-start | bytes 393224 | tf_op jit(solution)/shard_map/ppermute | solution.py:411
  7.4 1.6 %collective-permute-start.3 = (f32[256,128]{1,0:T(8,128)S(1)}, f32[256,128]{1,0:T(8,128)S(1)}, u32[]{:S(2)}, u32[]{:S(2)}) collective-permute-start(f32[256,128]{1,0:T(8,128)S(1)} %get-tuple-element.129), channel_id=1, source_target_pairs={{0,8},{2,10},{4,12},{6,14},{8,0},{10,2},{12,4},{14,6},{16,24},{18,... | collective-permute-start | bytes 393224 | tf_op jit(solution)/shard_map/ppermute | solution.py:411
  9.0 0.1 collective-permute-start.4
  9.1 1.5 %collective-permute-done.2.refs_1_ = f32[256,128]{1,0:T(8,128)S(1)} collective-permute-done((f32[256,128]{1,0:T(8,128)S(1)}, f32[256,128]{1,0:T(8,128)S(1)}, u32[]{:S(2)}, u32[]{:S(2)}) %collective-permute-start.2) | collective-permute-done | bytes 131104 | tf_op jit(solution)/shard_map/ppermute | solution.py:411
  10.6 2.9 %collective-permute-done.3.refs_2_ = f32[256,128]{1,0:T(8,128)S(1)} collective-permute-done((f32[256,128]{1,0:T(8,128)S(1)}, f32[256,128]{1,0:T(8,128)S(1)}, u32[]{:S(2)}, u32[]{:S(2)}) %collective-permute-start.3) | collective-permute-done | bytes 131104 | tf_op jit(solution)/shard_map/ppermute | solution.py:411
  13.4 1.5 %collective-permute-done.4.refs_3_ = f32[256,128]{1,0:T(8,128)S(1)} collective-permute-done((f32[256,128]{1,0:T(8,128)S(1)}, f32[256,128]{1,0:T(8,128)S(1)}, u32[]{:S(2)}, u32[]{:S(2)}) %collective-permute-start.4) | collective-permute-done | bytes 131104 | tf_op jit(solution)/shard_map/ppermute | solution.py:411
  15.0 2.8 %collective-permute-start.5 = (f32[256,128]{1,0:T(8,128)S(1)}, f32[256,128]{1,0:T(8,128)S(1)}, u32[]{:S(2)}, u32[]{:S(2)}) collective-permute-start(f32[256,128]{1,0:T(8,128)S(1)} %add_add_fusion.1), channel_id=1, source_target_pairs={{0,16},{2,18},{4,20},{6,22},{8,24},{10,26},{12,28},{14,30},{16,0},... | collective-permute-start | bytes 393224 | tf_op jit(solution)/shard_map/ppermute | solution.py:406
  17.8 1.1 %shard_map.91 = (bf16[192,1024]{1,0:T(8,128)(2,1)S(1)}, f32[192,1024]{1,0:T(8,128)S(1)}, bf16[192,1024]{1,0:T(8,128)(2,1)S(1)}, bf16[8,192,192]{2,1,0:T(8,128)(2...) custom-call(bf16[192,2048]{1,0:T(8,128)(2,1)S(1)} %copy-done.1, ...), custom_call_target="tpu_custom_call" | custom-call | tf_op jit(solution)/shard_map/pallas_call | solution.py:119
  18.9 1.1 %shard_map.90 = (bf16[192,1024]{1,0:T(8,128)(2,1)S(1)}, f32[192,1024]{1,0:T(8,128)S(1)}, bf16[192,1024]{1,0:T(8,128)(2,1)S(1)}, bf16[8,192,192]{2,1,0:T(8,128)(2...) custom-call(bf16[192,2048]{1,0:T(8,128)(2,1)S(1)} %copy-done.1, ...), custom_call_target="tpu_custom_call" | custom-call | tf_op jit(solution)/shard_map/pallas_call | solution.py:119
  20.1 3.0 %collective-permute-done.5.refs_4_ = f32[256,128]{1,0:T(8,128)S(1)} collective-permute-done((f32[256,128]{1,0:T(8,128)S(1)}, f32[256,128]{1,0:T(8,128)S(1)}, u32[]{:S(2)}, u32[]{:S(2)}) %collective-permute-start.5) | collective-permute-done | bytes 131104 | tf_op jit(solution)/shard_map/ppermute | solution.py:406
  23.1 0.1 shard_map.92
  23.2 0.7 collective-permute-start.6
  23.9 0.7 collective-permute-start.7
  24.6 2.2 %collective-permute-start.8 = (f32[256,128]{1,0:T(8,128)S(1)}, f32[256,128]{1,0:T(8,128)S(1)}, u32[]{:S(2)}, u32[]{:S(2)}) collective-permute-start(f32[256,128]{1,0:T(8,128)S(1)} %get-tuple-element.155), channel_id=1, source_target_pairs={{0,12},{2,10},{4,8},{6,14},{8,4},{10,2},{12,0},{14,6},{16,28},{18,... | collective-permute-start | bytes 393224 | tf_op jit(solution)/shard_map/ppermute | solution.py:411
  26.8 0.1 collective-permute-start.9
  26.9 2.7 %collective-permute-done.6.refs_1_.piece_ref = f32[256,128]{1,0:T(8,128)S(1)} collective-permute-done((f32[256,128]{1,0:T(8,128)S(1)}, f32[256,128]{1,0:T(8,128)S(1)}, u32[]{:S(2)}, u32[]{:S(2)}) %collective-permute-start.6) | collective-permute-done | bytes 131104 | tf_op jit(solution)/shard_map/ppermute | solution.py:411
  29.6 0.1 collective-permute-start.10
  29.7 0.0 collective-permute-done.7.refs_2_.piece_ref
  29.7 0.5 collective-permute-start.11
  30.3 1.6 %collective-permute-done.8.refs_3_.piece_ref = f32[256,128]{1,0:T(8,128)S(1)} collective-permute-done((f32[256,128]{1,0:T(8,128)S(1)}, f32[256,128]{1,0:T(8,128)S(1)}, u32[]{:S(2)}, u32[]{:S(2)}) %collective-permute-start.8) | collective-permute-done | bytes 131104 | tf_op jit(solution)/shard_map/ppermute | solution.py:411
  31.9 0.1 collective-permute-start.12
  31.9 0.4 shard_map.93
  32.4 0.9 %collective-permute-done.12.refs_3_ = f32[256,128]{1,0:T(8,128)S(1)} collective-permute-done((f32[256,128]{1,0:T(8,128)S(1)}, f32[256,128]{1,0:T(8,128)S(1)}, u32[]{:S(2)}, u32[]{:S(2)}) %collective-permute-start.12) | collective-permute-done | bytes 131104 | tf_op jit(solution)/shard_map/ppermute | solution.py:406
  33.3 0.5 shard_map.98
  33.8 1.4 %collective-permute-start.13 = (f32[8,192]{1,0:T(8,128)S(1)}, f32[8,192]{1,0:T(8,128)S(1)}, u32[]{:S(2)}, u32[]{:S(2)}) collective-permute-start(f32[8,192]{1,0:T(8,128)S(1)} %get-tuple-element.159.a_ref), channel_id=1, source_target_pairs={{0,1},{1,0},{2,3},{3,2},{4,5},{5,4},{6,7},{7,6},{8,9},{9,8},{10,11... | collective-permute-start | bytes 18440 | tf_op jit(solution)/shard_map/ppermute | solution.py:484
  35.2 2.3 %collective-permute-done.13.b_ref = f32[8,192]{1,0:T(8,128)S(1)} collective-permute-done((f32[8,192]{1,0:T(8,128)S(1)}, f32[8,192]{1,0:T(8,128)S(1)}, u32[]{:S(2)}, u32[]{:S(2)}) %collective-permute-start.13) | collective-permute-done | bytes 6176 | tf_op jit(solution)/shard_map/ppermute | solution.py:484
  37.5 0.6 shard_map.99
  38.1 0.1 collective-permute-start.14
  38.2 0.3 shard_map.102
  38.5 0.5 collective-permute-start.15
  39.0 0.4 shard_map.100
  39.4 0.3 collective-permute-done.14.got_ref.refs_4_
  39.7 0.6 shard_map.101
  40.3 0.4 collective-permute-start.16
  40.7 1.7 %collective-permute-start.17 = (f32[256,128]{1,0:T(8,128)S(1)}, f32[256,128]{1,0:T(8,128)S(1)}, u32[]{:S(2)}, u32[]{:S(2)}) collective-permute-start(f32[256,128]{1,0:T(8,128)S(1)} %get-tuple-element.180), channel_id=1, source_target_pairs={{0,8},{2,10},{4,12},{6,14},{8,0},{10,2},{12,4},{14,6},{16,24},{18,... | collective-permute-start | bytes 393224 | tf_op jit(solution)/shard_map/ppermute | solution.py:411
  42.4 1.6 %collective-permute-start.18 = (f32[256,128]{1,0:T(8,128)S(1)}, f32[256,128]{1,0:T(8,128)S(1)}, u32[]{:S(2)}, u32[]{:S(2)}) collective-permute-start(f32[256,128]{1,0:T(8,128)S(1)} %get-tuple-element.184), channel_id=1, source_target_pairs={{0,12},{2,14},{4,8},{6,10},{8,4},{10,6},{12,0},{14,2},{16,28},{18,... | collective-permute-start | bytes 393224 | tf_op jit(solution)/shard_map/ppermute | solution.py:411
  44.0 3.2 %shard_map.105 = (bf16[192,2048]{1,0:T(8,128)(2,1)}, bf16[192,2048]{1,0:T(8,128)(2,1)}, f32[192,1024]{1,0:T(8,128)S(1)}, f32[192,1024]{1,0:T(8,128)S(1)}) custom-call(bf16[1024,128]{1,0:T(8,128)(2,1)S(1)} %get-tuple-element.186.refs_0_, f32[192,128]{1,0:T(8,128)S(1)} %get-tuple-element.204.a_ref.inv_ref.refs_1_, ...), custom_call_target="tpu_custom_call" | custom-call | tf_op jit(solution)/shard_map/pallas_call | solution.py:119
  47.2 2.1 %collective-permute-done.18.refs_3_ = f32[256,128]{1,0:T(8,128)S(1)} collective-permute-done((f32[256,128]{1,0:T(8,128)S(1)}, f32[256,128]{1,0:T(8,128)S(1)}, u32[]{:S(2)}, u32[]{:S(2)}) %collective-permute-start.18) | collective-permute-done | bytes 131104 | tf_op jit(solution)/shard_map/ppermute | solution.py:411
  49.3 2.1 %collective-permute-start.19 = (f32[256,128]{1,0:T(8,128)S(1)}, f32[256,128]{1,0:T(8,128)S(1)}, u32[]{:S(2)}, u32[]{:S(2)}) collective-permute-start(f32[256,128]{1,0:T(8,128)S(1)} %add_add_fusion), channel_id=1, source_target_pairs={{0,16},{2,18},{4,20},{6,22},{8,24},{10,26},{12,28},{14,30},{16,0},... | collective-permute-start | bytes 393224 | tf_op jit(solution)/shard_map/ppermute | solution.py:406
  51.4 3.4 %shard_map.106 = (bf16[192,2048]{1,0:T(8,128)(2,1)}, bf16[192,2048]{1,0:T(8,128)(2,1)}, f32[192,1024]{1,0:T(8,128)S(1)}, f32[192,1024]{1,0:T(8,128)S(1)}) custom-call(bf16[1024,128]{1,0:T(8,128)(2,1)S(1)} %get-tuple-element.203.refs_0_, f32[192,128]{1,0:T(8,128)S(1)} %get-tuple-element.204.a_ref.inv_ref.refs_1_, ...), custom_call_target="tpu_custom_call", output_to_operand_aliasing={{0}: (12, {}), {1}: (13, {})} | custom-call | tf_op jit(solution)/shard_map/pallas_call | solution.py:119
  54.8 1.6 %collective-permute-done.19.refs_4_ = f32[256,128]{1,0:T(8,128)S(1)} collective-permute-done((f32[256,128]{1,0:T(8,128)S(1)}, f32[256,128]{1,0:T(8,128)S(1)}, u32[]{:S(2)}, u32[]{:S(2)}) %collective-permute-start.19) | collective-permute-done | bytes 131104 | tf_op jit(solution)/shard_map/ppermute | solution.py:406
  56.4 0.1 shard_map.107
  56.6 0.6 collective-permute-start.21
  57.2 0.3 collective-permute-start.23
  57.6 2.6 %collective-permute-start.25 = (f32[256,128]{1,0:T(8,128)S(1)}, f32[256,128]{1,0:T(8,128)S(1)}, u32[]{:S(2)}, u32[]{:S(2)}) collective-permute-start(f32[256,128]{1,0:T(8,128)S(1)} %get-tuple-element.224), channel_id=1, source_target_pairs={{0,12},{2,10},{4,8},{6,14},{8,4},{10,2},{12,0},{14,6},{16,28},{18,... | collective-permute-start | bytes 393224 | tf_op jit(solution)/shard_map/ppermute | solution.py:411
  60.2 0.1 collective-permute-start.20
  60.3 1.4 %collective-permute-done.21.piece_ref.refs_1_ = f32[256,128]{1,0:T(8,128)S(1)} collective-permute-done((f32[256,128]{1,0:T(8,128)S(1)}, f32[256,128]{1,0:T(8,128)S(1)}, u32[]{:S(2)}, u32[]{:S(2)}) %collective-permute-start.21) | collective-permute-done | bytes 131104 | tf_op jit(solution)/shard_map/ppermute | solution.py:411
  61.7 0.1 collective-permute-start.22
  61.7 0.5 collective-permute-done.23.piece_ref.refs_2_
  62.2 0.1 collective-permute-start.24
  62.3 2.2 %collective-permute-done.25.piece_ref.refs_3_ = f32[256,128]{1,0:T(8,128)S(1)} collective-permute-done((f32[256,128]{1,0:T(8,128)S(1)}, f32[256,128]{1,0:T(8,128)S(1)}, u32[]{:S(2)}, u32[]{:S(2)}) %collective-permute-start.25) | collective-permute-done | bytes 131104 | tf_op jit(solution)/shard_map/ppermute | solution.py:411
  64.5 0.1 collective-permute-start.26
  64.6 0.5 shard_map.112
  65.2 0.8 %collective-permute-done.26.refs_3_ = f32[256,128]{1,0:T(8,128)S(1)} collective-permute-done((f32[256,128]{1,0:T(8,128)S(1)}, f32[256,128]{1,0:T(8,128)S(1)}, u32[]{:S(2)}, u32[]{:S(2)}) %collective-permute-start.26) | collective-permute-done | bytes 131104 | tf_op jit(solution)/shard_map/ppermute | solution.py:406
  65.9 1.3 %shard_map.113 = (bf16[192,2048]{1,0:T(8,128)(2,1)}, bf16[192,2048]{1,0:T(8,128)(2,1)}) custom-call(f32[256,128]{1,0:T(8,128)S(1)} %collective-permute-done.20.refs_0_, f32[256,128]{1,0:T(8,128)S(1)} %collective-permute-done.22.refs_1_, f32[256,128]{1,0:T(8,128)S(1)} %collective-permute-done.24.refs_2_, f32[256,128]{1,0:T(8,128)S(1)} %collective-permute-done.26.refs_3_, ...), custom_call_target="tpu_custom_call" | custom-call | tf_op jit(solution)/shard_map/pallas_call | solution.py:119
  (28 shorter events, 0.4 us)
Async XLA Ops:
  2.1 1.7 %collective-permute-start = (f32[512,128]{1,0:T(8,128)S(1)}, f32[512,128]{1,0:T(8,128)S(1)}, u32[]{:S(2)}, u32[]{:S(2)}) collective-permute-start(f32[512,128]{1,0:T(8,128)S(1)} %get-tuple-element.119), channel_id=1, source_target_pairs={{0,2},{2,0},{4,6},{6,4},{8,10},{10,8},{12,14},{14,12},{16,18},{18,... | collective-permute-start | bytes 786440 | tf_op jit(solution)/shard_map/ppermute | solution.py:406
  2.9 6.0 %collective-permute-start.1 = (f32[512,128]{1,0:T(8,128)S(1)}, f32[512,128]{1,0:T(8,128)S(1)}, u32[]{:S(2)}, u32[]{:S(2)}) collective-permute-start(f32[512,128]{1,0:T(8,128)S(1)} %shard_map.87), channel_id=1, source_target_pairs={{0,2},{2,0},{4,6},{6,4},{8,10},{10,8},{12,14},{14,12},{16,18},{18,... | collective-permute-start | bytes 786440 | tf_op jit(solution)/shard_map/ppermute | solution.py:406
  3.8 14.0 %copy-start.2 = (bf16[192,2048]{1,0:T(8,128)(2,1)S(1)}, bf16[192,2048]{1,0:T(8,128)(2,1)}, u32[]{:S(2)}) copy-start(bf16[192,2048]{1,0:T(8,128)(2,1)} %cot_ref.1) | copy-start | bytes 2359300
  4.4 13.4 %copy-start.1 = (bf16[192,2048]{1,0:T(8,128)(2,1)S(1)}, bf16[192,2048]{1,0:T(8,128)(2,1)}, u32[]{:S(2)}) copy-start(bf16[192,2048]{1,0:T(8,128)(2,1)} %refs_8_.1) | copy-start | bytes 2359300
  4.5 13.4 %copy-start = (bf16[192,2048]{1,0:T(8,128)(2,1)S(1)}, bf16[192,2048]{1,0:T(8,128)(2,1)}, u32[]{:S(2)}) copy-start(bf16[192,2048]{1,0:T(8,128)(2,1)} %refs_10_.1) | copy-start | bytes 2359300
  4.5 6.1 %collective-permute-start.2 = (f32[256,128]{1,0:T(8,128)S(1)}, f32[256,128]{1,0:T(8,128)S(1)}, u32[]{:S(2)}, u32[]{:S(2)}) collective-permute-start(f32[256,128]{1,0:T(8,128)S(1)} %get-tuple-element.128), channel_id=1, source_target_pairs={{0,4},{2,6},{4,0},{6,2},{8,12},{10,14},{12,8},{14,10},{16,20},{18,... | collective-permute-start | bytes 393224 | tf_op jit(solution)/shard_map/ppermute | solution.py:411
  7.4 6.0 %collective-permute-start.3 = (f32[256,128]{1,0:T(8,128)S(1)}, f32[256,128]{1,0:T(8,128)S(1)}, u32[]{:S(2)}, u32[]{:S(2)}) collective-permute-start(f32[256,128]{1,0:T(8,128)S(1)} %get-tuple-element.129), channel_id=1, source_target_pairs={{0,8},{2,10},{4,12},{6,14},{8,0},{10,2},{12,4},{14,6},{16,24},{18,... | collective-permute-start | bytes 393224 | tf_op jit(solution)/shard_map/ppermute | solution.py:411
  9.0 5.9 %collective-permute-start.4 = (f32[256,128]{1,0:T(8,128)S(1)}, f32[256,128]{1,0:T(8,128)S(1)}, u32[]{:S(2)}, u32[]{:S(2)}) collective-permute-start(f32[256,128]{1,0:T(8,128)S(1)} %get-tuple-element.133), channel_id=1, source_target_pairs={{0,12},{2,14},{4,8},{6,10},{8,4},{10,6},{12,0},{14,2},{16,28},{18,... | collective-permute-start | bytes 393224 | tf_op jit(solution)/shard_map/ppermute | solution.py:411
  15.0 8.1 %collective-permute-start.5 = (f32[256,128]{1,0:T(8,128)S(1)}, f32[256,128]{1,0:T(8,128)S(1)}, u32[]{:S(2)}, u32[]{:S(2)}) collective-permute-start(f32[256,128]{1,0:T(8,128)S(1)} %add_add_fusion.1), channel_id=1, source_target_pairs={{0,16},{2,18},{4,20},{6,22},{8,24},{10,26},{12,28},{14,30},{16,0},... | collective-permute-start | bytes 393224 | tf_op jit(solution)/shard_map/ppermute | solution.py:406
  23.2 6.3 %collective-permute-start.6 = (f32[256,128]{1,0:T(8,128)S(1)}, f32[256,128]{1,0:T(8,128)S(1)}, u32[]{:S(2)}, u32[]{:S(2)}) collective-permute-start(f32[256,128]{1,0:T(8,128)S(1)} %get-tuple-element.153), channel_id=1, source_target_pairs={{0,4},{2,14},{4,0},{6,10},{8,12},{10,6},{12,8},{14,2},{16,20},{18,... | collective-permute-start | bytes 393224 | tf_op jit(solution)/shard_map/ppermute | solution.py:411
  23.9 5.8 %collective-permute-start.7 = (f32[256,128]{1,0:T(8,128)S(1)}, f32[256,128]{1,0:T(8,128)S(1)}, u32[]{:S(2)}, u32[]{:S(2)}) collective-permute-start(f32[256,128]{1,0:T(8,128)S(1)} %get-tuple-element.154), channel_id=1, source_target_pairs={{0,8},{2,6},{4,12},{6,2},{8,0},{10,14},{12,4},{14,10},{16,24},{18,... | collective-permute-start | bytes 393224 | tf_op jit(solution)/shard_map/ppermute | solution.py:411
  24.6 7.3 %collective-permute-start.8 = (f32[256,128]{1,0:T(8,128)S(1)}, f32[256,128]{1,0:T(8,128)S(1)}, u32[]{:S(2)}, u32[]{:S(2)}) collective-permute-start(f32[256,128]{1,0:T(8,128)S(1)} %get-tuple-element.155), channel_id=1, source_target_pairs={{0,12},{2,10},{4,8},{6,14},{8,4},{10,2},{12,0},{14,6},{16,28},{18,... | collective-permute-start | bytes 393224 | tf_op jit(solution)/shard_map/ppermute | solution.py:411
  26.8 5.5 %collective-permute-start.9 = (f32[256,128]{1,0:T(8,128)S(1)}, f32[256,128]{1,0:T(8,128)S(1)}, u32[]{:S(2)}, u32[]{:S(2)}) collective-permute-start(f32[256,128]{1,0:T(8,128)S(1)} %shard_map.94), channel_id=1, source_target_pairs={{0,2},{2,0},{4,6},{6,4},{8,10},{10,8},{12,14},{14,12},{16,18},{18,... | collective-permute-start | bytes 393224 | tf_op jit(solution)/shard_map/ppermute | solution.py:406
  29.6 2.8 %collective-permute-start.10 = (f32[256,128]{1,0:T(8,128)S(1)}, f32[256,128]{1,0:T(8,128)S(1)}, u32[]{:S(2)}, u32[]{:S(2)}) collective-permute-start(f32[256,128]{1,0:T(8,128)S(1)} %shard_map.95), channel_id=1, source_target_pairs={{0,2},{2,0},{4,6},{6,4},{8,10},{10,8},{12,14},{14,12},{16,18},{18,... | collective-permute-start | bytes 393224 | tf_op jit(solution)/shard_map/ppermute | solution.py:406
  29.7 2.6 %collective-permute-start.11 = (f32[256,128]{1,0:T(8,128)S(1)}, f32[256,128]{1,0:T(8,128)S(1)}, u32[]{:S(2)}, u32[]{:S(2)}) collective-permute-start(f32[256,128]{1,0:T(8,128)S(1)} %shard_map.96), channel_id=1, source_target_pairs={{0,2},{2,0},{4,6},{6,4},{8,10},{10,8},{12,14},{14,12},{16,18},{18,... | collective-permute-start | bytes 393224 | tf_op jit(solution)/shard_map/ppermute | solution.py:406
  31.9 1.4 %collective-permute-start.12 = (f32[256,128]{1,0:T(8,128)S(1)}, f32[256,128]{1,0:T(8,128)S(1)}, u32[]{:S(2)}, u32[]{:S(2)}) collective-permute-start(f32[256,128]{1,0:T(8,128)S(1)} %shard_map.97), channel_id=1, source_target_pairs={{0,2},{2,0},{4,6},{6,4},{8,10},{10,8},{12,14},{14,12},{16,18},{18,... | collective-permute-start | bytes 393224 | tf_op jit(solution)/shard_map/ppermute | solution.py:406
  33.8 3.7 %collective-permute-start.13 = (f32[8,192]{1,0:T(8,128)S(1)}, f32[8,192]{1,0:T(8,128)S(1)}, u32[]{:S(2)}, u32[]{:S(2)}) collective-permute-start(f32[8,192]{1,0:T(8,128)S(1)} %get-tuple-element.159.a_ref), channel_id=1, source_target_pairs={{0,1},{1,0},{2,3},{3,2},{4,5},{5,4},{6,7},{7,6},{8,9},{9,8},{10,11... | collective-permute-start | bytes 18440 | tf_op jit(solution)/shard_map/ppermute | solution.py:484
  38.1 1.6 %collective-permute-start.14 = (f32[512,128]{1,0:T(8,128)S(1)}, f32[512,128]{1,0:T(8,128)S(1)}, u32[]{:S(2)}, u32[]{:S(2)}) collective-permute-start(f32[512,128]{1,0:T(8,128)S(1)} %get-tuple-element.165), channel_id=1, source_target_pairs={{0,2},{2,0},{4,6},{6,4},{8,10},{10,8},{12,14},{14,12},{16,18},{18,... | collective-permute-start | bytes 786440 | tf_op jit(solution)/shard_map/ppermute | solution.py:406
  38.5 3.9 %collective-permute-start.15 = (f32[512,128]{1,0:T(8,128)S(1)}, f32[512,128]{1,0:T(8,128)S(1)}, u32[]{:S(2)}, u32[]{:S(2)}) collective-permute-start(f32[512,128]{1,0:T(8,128)S(1)} %shard_map.102), channel_id=1, source_target_pairs={{0,2},{2,0},{4,6},{6,4},{8,10},{10,8},{12,14},{14,12},{16,18},{18,... | collective-permute-start | bytes 786440 | tf_op jit(solution)/shard_map/ppermute | solution.py:406
  40.3 6.9 %collective-permute-start.16 = (f32[256,128]{1,0:T(8,128)S(1)}, f32[256,128]{1,0:T(8,128)S(1)}, u32[]{:S(2)}, u32[]{:S(2)}) collective-permute-start(f32[256,128]{1,0:T(8,128)S(1)} %get-tuple-element.179), channel_id=1, source_target_pairs={{0,4},{2,6},{4,0},{6,2},{8,12},{10,14},{12,8},{14,10},{16,20},{18,... | collective-permute-start | bytes 393224 | tf_op jit(solution)/shard_map/ppermute | solution.py:411
  40.7 6.5 %collective-permute-start.17 = (f32[256,128]{1,0:T(8,128)S(1)}, f32[256,128]{1,0:T(8,128)S(1)}, u32[]{:S(2)}, u32[]{:S(2)}) collective-permute-start(f32[256,128]{1,0:T(8,128)S(1)} %get-tuple-element.180), channel_id=1, source_target_pairs={{0,8},{2,10},{4,12},{6,14},{8,0},{10,2},{12,4},{14,6},{16,24},{18,... | collective-permute-start | bytes 393224 | tf_op jit(solution)/shard_map/ppermute | solution.py:411
  42.4 6.9 %collective-permute-start.18 = (f32[256,128]{1,0:T(8,128)S(1)}, f32[256,128]{1,0:T(8,128)S(1)}, u32[]{:S(2)}, u32[]{:S(2)}) collective-permute-start(f32[256,128]{1,0:T(8,128)S(1)} %get-tuple-element.184), channel_id=1, source_target_pairs={{0,12},{2,14},{4,8},{6,10},{8,4},{10,6},{12,0},{14,2},{16,28},{18,... | collective-permute-start | bytes 393224 | tf_op jit(solution)/shard_map/ppermute | solution.py:411
  49.3 7.1 %collective-permute-start.19 = (f32[256,128]{1,0:T(8,128)S(1)}, f32[256,128]{1,0:T(8,128)S(1)}, u32[]{:S(2)}, u32[]{:S(2)}) collective-permute-start(f32[256,128]{1,0:T(8,128)S(1)} %add_add_fusion), channel_id=1, source_target_pairs={{0,16},{2,18},{4,20},{6,22},{8,24},{10,26},{12,28},{14,30},{16,0},... | collective-permute-start | bytes 393224 | tf_op jit(solution)/shard_map/ppermute | solution.py:406
  56.6 5.0 %collective-permute-start.21 = (f32[256,128]{1,0:T(8,128)S(1)}, f32[256,128]{1,0:T(8,128)S(1)}, u32[]{:S(2)}, u32[]{:S(2)}) collective-permute-start(f32[256,128]{1,0:T(8,128)S(1)} %get-tuple-element.222), channel_id=1, source_target_pairs={{0,4},{2,14},{4,0},{6,10},{8,12},{10,6},{12,8},{14,2},{16,20},{18,... | collective-permute-start | bytes 393224 | tf_op jit(solution)/shard_map/ppermute | solution.py:411
  57.2 5.0 %collective-permute-start.23 = (f32[256,128]{1,0:T(8,128)S(1)}, f32[256,128]{1,0:T(8,128)S(1)}, u32[]{:S(2)}, u32[]{:S(2)}) collective-permute-start(f32[256,128]{1,0:T(8,128)S(1)} %get-tuple-element.223), channel_id=1, source_target_pairs={{0,8},{2,6},{4,12},{6,2},{8,0},{10,14},{12,4},{14,10},{16,24},{18,... | collective-permute-start | bytes 393224 | tf_op jit(solution)/shard_map/ppermute | solution.py:411
  57.6 6.9 %collective-permute-start.25 = (f32[256,128]{1,0:T(8,128)S(1)}, f32[256,128]{1,0:T(8,128)S(1)}, u32[]{:S(2)}, u32[]{:S(2)}) collective-permute-start(f32[256,128]{1,0:T(8,128)S(1)} %get-tuple-element.224), channel_id=1, source_target_pairs={{0,12},{2,10},{4,8},{6,14},{8,4},{10,2},{12,0},{14,6},{16,28},{18,... | collective-permute-start | bytes 393224 | tf_op jit(solution)/shard_map/ppermute | solution.py:411
  60.2 5.0 %collective-permute-start.20 = (f32[256,128]{1,0:T(8,128)S(1)}, f32[256,128]{1,0:T(8,128)S(1)}, u32[]{:S(2)}, u32[]{:S(2)}) collective-permute-start(f32[256,128]{1,0:T(8,128)S(1)} %shard_map.108), channel_id=1, source_target_pairs={{0,2},{2,0},{4,6},{6,4},{8,10},{10,8},{12,14},{14,12},{16,18},{18,... | collective-permute-start | bytes 393224 | tf_op jit(solution)/shard_map/ppermute | solution.py:406
  61.7 3.5 %collective-permute-start.22 = (f32[256,128]{1,0:T(8,128)S(1)}, f32[256,128]{1,0:T(8,128)S(1)}, u32[]{:S(2)}, u32[]{:S(2)}) collective-permute-start(f32[256,128]{1,0:T(8,128)S(1)} %shard_map.109), channel_id=1, source_target_pairs={{0,2},{2,0},{4,6},{6,4},{8,10},{10,8},{12,14},{14,12},{16,18},{18,... | collective-permute-start | bytes 393224 | tf_op jit(solution)/shard_map/ppermute | solution.py:406
  62.2 2.9 %collective-permute-start.24 = (f32[256,128]{1,0:T(8,128)S(1)}, f32[256,128]{1,0:T(8,128)S(1)}, u32[]{:S(2)}, u32[]{:S(2)}) collective-permute-start(f32[256,128]{1,0:T(8,128)S(1)} %shard_map.110), channel_id=1, source_target_pairs={{0,2},{2,0},{4,6},{6,4},{8,10},{10,8},{12,14},{14,12},{16,18},{18,... | collective-permute-start | bytes 393224 | tf_op jit(solution)/shard_map/ppermute | solution.py:406
  64.5 1.4 %collective-permute-start.26 = (f32[256,128]{1,0:T(8,128)S(1)}, f32[256,128]{1,0:T(8,128)S(1)}, u32[]{:S(2)}, u32[]{:S(2)}) collective-permute-start(f32[256,128]{1,0:T(8,128)S(1)} %shard_map.111), channel_id=1, source_target_pairs={{0,2},{2,0},{4,6},{6,4},{8,10},{10,8},{12,14},{14,12},{16,18},{18,... | collective-permute-start | bytes 393224 | tf_op jit(solution)/shard_map/ppermute | solution.py:406
